TPU v7x, 768 devices: a whole 4x8x12 slice. The times are simulated.
768 devices in a mesh: graph: 24 (over z, core), dp: 32 (over x, y).
Axes of the slice: x: 4, y: 8, z: 12, core: 2. Of those that a mesh axis runs over, the one named last changes fastest.
Arguments:
- node_features: bfloat16 [32, 49, 64, 3072], P('dp', None, None, 'graph'), may hold values from -6 to 6
- cotangent: bfloat16 [32, 49, 64, 3072], P('dp', None, None, 'graph'), may hold values from -6 to 6
- wigner: bfloat16 [128, 29, 49], replicated, as said below
- w_zero: bfloat16 [448, 448], replicated, may hold values from -0.25 to 0.25
- w_one: bfloat16 [2, 384, 384], replicated, may hold values from -0.21875 to 0.21875
- w_two: bfloat16 [2, 320, 320], replicated, may hold values from -0.25 to 0.25
- edge_source: int32 [32, 3072], P('dp', 'graph'), may hold values from 0 to 127
- edge_target: int32 [32, 3072], P('dp', 'graph'), may hold values from 0 to 127
- edge_bin: int32 [32, 3072], P('dp', 'graph'), may hold values from 0 to 127
- edge_scale: float32 [32, 3072], P('dp', 'graph'), may hold values from 0.25 to 1
- send_atoms: int32 [32, 48, 32], P('dp', 'graph'), may hold values from 0 to 127
- send_bins: int32 [32, 48, 32], P('dp', 'graph'), may hold values from 0 to 127, as said below
- recv_targets: int32 [32, 48, 32], P('dp', 'graph'), may hold values from 0 to 127
- recv_bins: int32 [32, 48, 32], P('dp', 'graph'), may hold values from 0 to 127
- recv_scale: float32 [32, 48, 32], P('dp', 'graph'), may hold values from 0.25 to 1
Outputs:
- updated: bfloat16 [32, 49, 64, 3072], P('dp', None, None, 'graph')
- feature_grad: float32 [32, 49, 64, 3072], P('dp', None, None, 'graph')
- grad_zero: float32 [448, 448], replicated
- grad_one: float32 [2, 384, 384], replicated
- grad_two: float32 [2, 320, 320], replicated
Inputs may be any that keep to these rules, and one draw needn't show every extreme that they name: `wigner`: nonzero only between rows of the same degree l; entries independent. `send_bins`: block 0 of graph index s equals recv_bins slot 1 of index s - 1, block 1 equals slot 0 of index s + 1, cyclically.
All inputs are finite; a program needn't handle non-finite values.
Results may differ from a plain program's by a relative error of at most 0.0056.
Values may be sent and summed in bfloat16 or wider, within the bound.
No kernel may reach another device: no remote copies, remote signals or barrier semaphores. Data moves between devices by JAX's collectives and lax.ppermute only.
A program may use at most 128 MiB of HBM per device.

v0:
```python
import jax
import jax.numpy as jnp
from jax import lax
from jax.sharding import PartitionSpec as P


def from_behind(value, axis, steps):
    count = lax.axis_size(axis)
    pairs = [(source, (source + steps) % count) for source in range(count)]
    return lax.ppermute(value, axis, pairs)


def product(left, right):
    return jnp.dot(left, right, preferred_element_type=jnp.float32)


def product_t(left, right):
    return lax.dot_general(
        left, right, (((0,), (0,)), ((), ())), preferred_element_type=jnp.float32
    )


def outer_sum(left, right):
    return lax.dot_general(
        left, right, (((1,), (1,)), ((), ())), preferred_element_type=jnp.float32
    )


def degree_rows(degree):
    rows = [degree]
    if degree >= 1:
        rows = rows + [6 + degree, 12 + degree]
    if degree >= 2:
        rows = rows + [17 + degree, 22 + degree]
    return rows


def rotate_into(frames, values):
    found = {}
    for degree in range(7):
        rows = degree_rows(degree)
        first = degree * degree
        last = (degree + 1) * (degree + 1)
        coeffs = values[first:last].astype(jnp.float32)
        for row in rows:
            weights = frames[row, first:last].astype(jnp.float32)
            found[row] = jnp.sum(weights[:, None, :] * coeffs, axis=0)
    return jnp.stack([found[row] for row in range(29)])


def rotate_back(frames, values):
    blocks = []
    for degree in range(7):
        rows = degree_rows(degree)
        first = degree * degree
        last = (degree + 1) * (degree + 1)
        total = None
        for row in rows:
            weights = frames[row, first:last].astype(jnp.float32)
            term = weights[:, None, :] * values[row].astype(jnp.float32)[None]
            total = term if total is None else total + term
        blocks.append(total)
    return jnp.concatenate(blocks, axis=0)


def split_orders(values):
    channels = values.shape[1]
    count = values.shape[2]
    return [
        values[0:7].reshape(7 * channels, count),
        values[7:13].reshape(6 * channels, count),
        values[13:19].reshape(6 * channels, count),
        values[19:24].reshape(5 * channels, count),
        values[24:29].reshape(5 * channels, count),
    ]


def join_orders(pieces, channels, count):
    return jnp.concatenate([piece.reshape(-1, channels, count) for piece in pieces], axis=0)


def convolve(rotated, w_zero, w_one, w_two):
    parts = split_orders(rotated)
    outputs = [
        product(w_zero, parts[0]),
        product(w_one[0], parts[1]) - product(w_one[1], parts[2]),
        product(w_one[1], parts[1]) + product(w_one[0], parts[2]),
        product(w_two[0], parts[3]) - product(w_two[1], parts[4]),
        product(w_two[1], parts[3]) + product(w_two[0], parts[4]),
    ]
    return join_orders(outputs, rotated.shape[1], rotated.shape[2])


def convolve_back(conv_grad, rotated, w_zero, w_one, w_two):
    grads = split_orders(conv_grad)
    parts = split_orders(rotated)
    inputs = [
        product_t(w_zero, grads[0]),
        product_t(w_one[0], grads[1]) + product_t(w_one[1], grads[2]),
        product_t(w_one[0], grads[2]) - product_t(w_one[1], grads[1]),
        product_t(w_two[0], grads[3]) + product_t(w_two[1], grads[4]),
        product_t(w_two[0], grads[4]) - product_t(w_two[1], grads[3]),
    ]
    grad_zero = outer_sum(grads[0], parts[0])
    grad_one = jnp.stack(
        [
            outer_sum(grads[1], parts[1]) + outer_sum(grads[2], parts[2]),
            outer_sum(grads[2], parts[1]) - outer_sum(grads[1], parts[2]),
        ]
    )
    grad_two = jnp.stack(
        [
            outer_sum(grads[3], parts[3]) + outer_sum(grads[4], parts[4]),
            outer_sum(grads[4], parts[3]) - outer_sum(grads[3], parts[4]),
        ]
    )
    return (
        join_orders(inputs, rotated.shape[1], rotated.shape[2]),
        (grad_zero, grad_one, grad_two),
    )


def message_forward(rotated, frames_out, weighting, w_zero, w_one, w_two):
    conv_out = convolve(rotated, w_zero, w_one, w_two)
    gating = jax.nn.sigmoid(conv_out[0])
    factor = gating * weighting[None, :]
    message = conv_out * factor[None]
    node_part = rotate_back(frames_out, message)
    return (node_part.astype(jnp.bfloat16), conv_out, gating, factor)


def message_backward(
    node_grad, rotated, frames_out, weighting, conv_out, gating, factor, w_zero, w_one, w_two
):
    message_grad = rotate_into(frames_out, node_grad)
    factor_grad = jnp.sum(message_grad * conv_out, axis=0)
    conv_grad = message_grad * factor[None]
    conv_grad = conv_grad.at[0].add(factor_grad * weighting[None, :] * gating * (1.0 - gating))
    conv_grad = conv_grad.astype(jnp.bfloat16)
    input_grad, weight_grads = convolve_back(conv_grad, rotated, w_zero, w_one, w_two)
    return (input_grad.astype(jnp.bfloat16), weight_grads)


def node_sum(node_part, targets, atom_count):
    table = (targets[:, None] == jnp.arange(atom_count, dtype=jnp.int32)[None, :]).astype(
        jnp.bfloat16
    )
    return product(node_part.reshape(-1, node_part.shape[2]), table)


def body(
    node_features,
    cotangent,
    wigner,
    w_zero,
    w_one,
    w_two,
    edge_source,
    edge_target,
    edge_bin,
    edge_scale,
    send_atoms,
    send_bins,
    recv_targets,
    recv_bins,
    recv_scale,
):
    node_local = node_features[0]
    cot_local = cotangent[0]
    atom_count = node_local.shape[2]
    channels = node_local.shape[1]
    out_atoms = send_atoms[0]
    capacity = out_atoms.shape[1]
    table_rkb = jnp.transpose(wigner, (1, 2, 0))
    out_frames = jnp.take(table_rkb, out_atoms.shape[0] * 0 + send_bins[0].reshape(-1), axis=2)
    out_gathered = jnp.take(node_local, out_atoms.reshape(-1), axis=2)
    rim_flat = rotate_into(out_frames, out_gathered).astype(jnp.bfloat16)
    rim_blocks = jnp.transpose(
        rim_flat.reshape(rim_flat.shape[0], channels, 2, capacity), (2, 0, 1, 3)
    )
    from_lower = from_behind(rim_blocks[1], "graph", 1)
    from_upper = from_behind(rim_blocks[0], "graph", -1)
    sources = edge_source[0]
    targets = edge_target[0]
    inner_frames = jnp.take(table_rkb, edge_bin[0], axis=2)
    inner_scale = edge_scale[0]
    inner_gathered = jnp.take(node_local, sources, axis=2)
    inner_rotated = rotate_into(inner_frames, inner_gathered).astype(jnp.bfloat16)
    inner_node, inner_conv, inner_gating, inner_factor = message_forward(
        inner_rotated, inner_frames, inner_scale, w_zero, w_one, w_two
    )
    halo_rotated = jnp.concatenate([from_lower, from_upper], axis=2)
    halo_targets = recv_targets[0].reshape(-1)
    halo_frames = jnp.take(table_rkb, recv_bins[0].reshape(-1), axis=2)
    halo_scale = recv_scale[0].reshape(-1)
    halo_node, halo_conv, halo_gating, halo_factor = message_forward(
        halo_rotated, halo_frames, halo_scale, w_zero, w_one, w_two
    )
    summed = node_sum(inner_node, targets, atom_count) + node_sum(
        halo_node, halo_targets, atom_count
    )
    updated = (node_local.astype(jnp.float32) + 0.5 * summed.reshape(node_local.shape)).astype(
        jnp.bfloat16
    )
    halo_node_grad = 0.5 * jnp.take(cot_local, halo_targets, axis=2).astype(jnp.float32)
    halo_input, halo_weights = message_backward(
        halo_node_grad,
        halo_rotated,
        halo_frames,
        halo_scale,
        halo_conv,
        halo_gating,
        halo_factor,
        w_zero,
        w_one,
        w_two,
    )
    lower_grad = halo_input[:, :, :capacity]
    upper_grad = halo_input[:, :, capacity:]
    back_zero = from_behind(upper_grad, "graph", 1)
    back_one = from_behind(lower_grad, "graph", -1)
    inner_node_grad = 0.5 * jnp.take(cot_local, targets, axis=2).astype(jnp.float32)
    inner_input, inner_weights = message_backward(
        inner_node_grad,
        inner_rotated,
        inner_frames,
        inner_scale,
        inner_conv,
        inner_gating,
        inner_factor,
        w_zero,
        w_one,
        w_two,
    )
    inner_source = rotate_back(inner_frames, inner_input).astype(jnp.bfloat16)
    feature_grad = cot_local.astype(jnp.float32) + node_sum(
        inner_source, sources, atom_count
    ).reshape(node_local.shape)
    back_flat = jnp.concatenate([back_zero, back_one], axis=2)
    rim_source = rotate_back(out_frames, back_flat).astype(jnp.bfloat16)
    feature_grad = feature_grad + node_sum(rim_source, out_atoms.reshape(-1), atom_count).reshape(
        node_local.shape
    )
    grad_zero = inner_weights[0] + halo_weights[0]
    grad_one = inner_weights[1] + halo_weights[1]
    grad_two = inner_weights[2] + halo_weights[2]
    grad_zero, grad_one, grad_two = lax.psum((grad_zero, grad_one, grad_two), ("graph", "dp"))
    replicas = lax.axis_size("dp")
    return (
        updated[None],
        feature_grad[None],
        grad_zero / replicas,
        grad_one / replicas,
        grad_two / replicas,
    )


def solution(mesh):
    in_specs = (
        P("dp", None, None, "graph"),
        P("dp", None, None, "graph"),
        P(),
        P(),
        P(),
        P(),
        P("dp", "graph"),
        P("dp", "graph"),
        P("dp", "graph"),
        P("dp", "graph"),
        P("dp", "graph", None),
        P("dp", "graph", None),
        P("dp", "graph", None),
        P("dp", "graph", None),
        P("dp", "graph", None),
    )
    out_specs = (P("dp", None, None, "graph"), P("dp", None, None, "graph"), P(), P(), P())
    return jax.shard_map(body, mesh=mesh, in_specs=in_specs, out_specs=out_specs, check_vma=False)
```

profile of v0, /device:TPU:1, one launch (start us, length us, event | category | flops | bytes accessed | tf_op | source)
XLA Modules:
  0.0 829.8 jit_solution(9582445608818863455)
XLA Ops:
  11.4 2.7 copy.453
  19.4 4.6 copy.454
  25.5 2.8 copy.486
  34.9 10.5 %collective-permute-start.1 = (bf16[29,64,32]{1,2,0:T(8,128)(2,1)}, bf16[29,64,32]{1,2,0:T(8,128)(2,1)}, u32[]{:S(2)}, u32[]{:S(2)}) collective-permute-start(bf16[29,64,32]{1,2,0:T(8,128)(2,1)} %get-tuple-element.362), channel_id=1, source_target_pairs={{0,736},{32,0},{64,32},{96,64},{128,96},{160,128},{192,160},{224,1... | collective-permute-start | bytes 356360 | tf_op jit(solution)/shard_map/ppermute | solution.py:10
  71.6 3.4 copy.585
  75.0 2.0 gather_fusion.5
  77.0 3.5 copy.586
  80.5 3.5 gather_fusion.1
  84.0 3.9 copy.455
  98.8 1.8 fusion.133
  108.8 1.7 copy.475
  110.5 1.9 fusion.10
  112.4 1.7 copy.474
  206.2 1.7 gather_fusion.6
  242.3 1.8 fusion.18
  244.0 1.7 copy.550
  245.7 1.7 copy.555
  247.4 1.7 fusion.19
  250.8 1.7 copy.554
  252.5 1.8 fusion.20
  254.3 1.8 fusion.21
  256.1 1.7 reshape.1099
  257.8 1.7 reshape.1100
  274.6 1.9 fusion.234
  278.1 1.7 reshape.1115
  279.8 1.7 fusion.73
  281.5 1.9 fusion.233
  298.6 3.1 collective-permute-start.3
  314.7 2.0 convert_element_type.1391
  316.8 2.5 convolution_add_fusion.1
  329.2 489.0 %all-reduce.3.cloned.1.call-done = (f32[448,448]{1,0:T(8,128)}, f32[2,384,384]{2,1,0:T(8,128)}, f32[2,320,320]{2,1,0:T(8,128)}) async-done(((f32[448,448]{1,0:T(8,128)}, f32[2,384,384]{2,1,0:T(8,128)}, f32[2,320,320]{2,1,0:T(8,128)}), (f32[448,448]{1,0:T(8,128)}, f32[2,384,384]{2,1,0:T(8,128)}, f32[2,320,320]{2,1,0:T(8,128)})) %all-reduce.3.cloned.1.call-update) | async-done | bytes 2801680 | tf_op jit(solution)/shard_map/psum | solution.py:247
  818.2 2.3 broadcast_multiply_fusion.6
  (1059 shorter events, 243.3 us)
Async XLA Ops:
  7.2 114.3 %copy-start = (bf16[448,448]{1,0:T(8,128)(2,1)S(1)}, bf16[448,448]{1,0:T(8,128)(2,1)}, u32[]{:S(2)}) copy-start(bf16[448,448]{1,0:T(8,128)(2,1)} %param.28) | copy-start | bytes 1204228
  7.2 811.0 %all-reduce.3.cloned.1.call-start = ((), (), s32[]{:S(2)}) async-start(), calls=%async_computation | async-start | bytes 6160384 | tf_op jit(solution)/shard_map/psum | solution.py:247
  15.4 14.2 %copy-start.283 = (f32[64]{0:T(128)}, f32[64]{0:T(128)S(1)}, u32[]{:S(2)}) copy-start(f32[64]{0:T(128)S(1)} %fusion.180) | copy-start | bytes 772
  34.9 193.7 %collective-permute-start.1 = (bf16[29,64,32]{1,2,0:T(8,128)(2,1)}, bf16[29,64,32]{1,2,0:T(8,128)(2,1)}, u32[]{:S(2)}, u32[]{:S(2)}) collective-permute-start(bf16[29,64,32]{1,2,0:T(8,128)(2,1)} %get-tuple-element.362), channel_id=1, source_target_pairs={{0,736},{32,0},{64,32},{96,64},{128,96},{160,128},{192,160},{224,1... | collective-permute-start | bytes 356360 | tf_op jit(solution)/shard_map/ppermute | solution.py:10
  45.4 182.2 %collective-permute-start = (bf16[29,64,32]{1,2,0:T(8,128)(2,1)}, bf16[29,64,32]{1,2,0:T(8,128)(2,1)}, u32[]{:S(2)}, u32[]{:S(2)}) collective-permute-start(bf16[29,64,32]{1,2,0:T(8,128)(2,1)} %get-tuple-element.363), channel_id=1, source_target_pairs={{0,32},{32,64},{64,96},{96,128},{128,160},{160,192},{192,224},{224... | collective-permute-start | bytes 356360 | tf_op jit(solution)/shard_map/ppermute | solution.py:10
  55.0 34.2 %copy-start.281 = (f32[128]{0:T(128)}, f32[128]{0:T(128)S(1)}, u32[]{:S(2)}) copy-start(f32[128]{0:T(128)S(1)} %fusion.137) | copy-start | bytes 1540
  58.5 35.1 %copy-start.143 = (f32[13,128]{1,0:T(8,128)}, f32[13,128]{1,0:T(8,128)S(1)}, u32[]{:S(2)}) copy-start(f32[13,128]{1,0:T(8,128)S(1)} %copy.461) | copy-start | bytes 19972
  58.6 35.1 %copy-start.145 = (f32[13,128]{1,0:T(8,128)}, f32[13,128]{1,0:T(8,128)S(1)}, u32[]{:S(2)}) copy-start(f32[13,128]{1,0:T(8,128)S(1)} %copy.485) | copy-start | bytes 19972
  71.3 19.4 %copy-start.235 = (f32[7,128]{1,0:T(8,128)}, f32[7,128]{1,0:T(8,128)S(1)}, u32[]{:S(2)}) copy-start(f32[7,128]{1,0:T(8,128)S(1)} %copy.464) | copy-start | bytes 10756
  71.4 18.5 %copy-start.238 = (f32[5,128]{1,0:T(8,128)}, f32[5,128]{1,0:T(8,128)S(1)}, u32[]{:S(2)}) copy-start(f32[5,128]{1,0:T(8,128)S(1)} %copy.476) | copy-start | bytes 7684
  71.5 18.4 %copy-start.239 = (f32[5,128]{1,0:T(8,128)}, f32[5,128]{1,0:T(8,128)S(1)}, u32[]{:S(2)}) copy-start(f32[5,128]{1,0:T(8,128)S(1)} %copy.469) | copy-start | bytes 7684
  71.6 18.3 %copy-start.240 = (f32[5,128]{1,0:T(8,128)}, f32[5,128]{1,0:T(8,128)S(1)}, u32[]{:S(2)}) copy-start(f32[5,128]{1,0:T(8,128)S(1)} %copy.463) | copy-start | bytes 7684
  107.8 14.9 %copy-start.36 = (bf16[6,64,128]{2,1,0:T(8,128)(2,1)}, bf16[6,64,128]{2,1,0:T(8,128)(2,1)S(1)}, u32[]{:S(2)}) copy-start(bf16[6,64,128]{2,1,0:T(8,128)(2,1)S(1)} %constant_dynamic-update-slice_fusion.13) | copy-start | bytes 294916
  114.1 29.4 %copy-start.123 = (f32[64,128]{1,0:T(8,128)S(1)}, f32[64,128]{1,0:T(8,128)}, u32[]{:S(2)}) copy-start(f32[64,128]{1,0:T(8,128)} %get-tuple-element.146) | copy-start | bytes 98308
  114.1 30.0 %copy-start.125 = (f32[64,128]{1,0:T(8,128)S(1)}, f32[64,128]{1,0:T(8,128)}, u32[]{:S(2)}) copy-start(f32[64,128]{1,0:T(8,128)} %get-tuple-element.151) | copy-start | bytes 98308
  114.1 30.6 %copy-start.126 = (f32[64,128]{1,0:T(8,128)S(1)}, f32[64,128]{1,0:T(8,128)}, u32[]{:S(2)}) copy-start(f32[64,128]{1,0:T(8,128)} %get-tuple-element.156) | copy-start | bytes 98308
  114.1 31.2 %copy-start.116 = (f32[64,128]{1,0:T(8,128)S(1)}, f32[64,128]{1,0:T(8,128)}, u32[]{:S(2)}) copy-start(f32[64,128]{1,0:T(8,128)} %get-tuple-element.160) | copy-start | bytes 98308
  114.1 31.8 %copy-start.118 = (f32[64,128]{1,0:T(8,128)S(1)}, f32[64,128]{1,0:T(8,128)}, u32[]{:S(2)}) copy-start(f32[64,128]{1,0:T(8,128)} %get-tuple-element.165) | copy-start | bytes 98308
  114.1 32.4 %copy-start.120 = (f32[64,128]{1,0:T(8,128)S(1)}, f32[64,128]{1,0:T(8,128)}, u32[]{:S(2)}) copy-start(f32[64,128]{1,0:T(8,128)} %get-tuple-element.145) | copy-start | bytes 98308
  114.1 33.1 %copy-start.122 = (f32[64,128]{1,0:T(8,128)S(1)}, f32[64,128]{1,0:T(8,128)}, u32[]{:S(2)}) copy-start(f32[64,128]{1,0:T(8,128)} %get-tuple-element.150) | copy-start | bytes 98308
  114.1 33.7 %copy-start.124 = (f32[64,128]{1,0:T(8,128)S(1)}, f32[64,128]{1,0:T(8,128)}, u32[]{:S(2)}) copy-start(f32[64,128]{1,0:T(8,128)} %get-tuple-element.155) | copy-start | bytes 98308
  114.2 34.9 %copy-start.115 = (f32[64,128]{1,0:T(8,128)S(1)}, f32[64,128]{1,0:T(8,128)}, u32[]{:S(2)}) copy-start(f32[64,128]{1,0:T(8,128)} %get-tuple-element.168) | copy-start | bytes 98308
  114.2 35.5 %copy-start.117 = (f32[64,128]{1,0:T(8,128)S(1)}, f32[64,128]{1,0:T(8,128)}, u32[]{:S(2)}) copy-start(f32[64,128]{1,0:T(8,128)} %get-tuple-element.148) | copy-start | bytes 98308
  115.6 34.7 %copy-start.119 = (f32[64,128]{1,0:T(8,128)S(1)}, f32[64,128]{1,0:T(8,128)}, u32[]{:S(2)}) copy-start(f32[64,128]{1,0:T(8,128)} %get-tuple-element.153) | copy-start | bytes 98308
  116.9 34.0 %copy-start.121 = (f32[64,128]{1,0:T(8,128)S(1)}, f32[64,128]{1,0:T(8,128)}, u32[]{:S(2)}) copy-start(f32[64,128]{1,0:T(8,128)} %get-tuple-element.158) | copy-start | bytes 98308
  119.5 32.0 %copy-start.295 = (f32[1,128]{1,0:T(1,128)S(1)}, f32[1,128]{1,0:T(1,128)}, u32[]{:S(2)}) copy-start(f32[1,128]{1,0:T(1,128)} %param.34) | copy-start | bytes 1540
  121.5 30.1 %copy-start.55 = (f32[384,128]{1,0:T(8,128)S(1)}, f32[384,128]{1,0:T(8,128)}, u32[]{:S(2)}) copy-start(f32[384,128]{1,0:T(8,128)} %copy.474) | copy-start | bytes 589828
  122.7 28.9 %copy-start.54 = (f32[384,128]{1,0:T(8,128)S(1)}, f32[384,128]{1,0:T(8,128)}, u32[]{:S(2)}) copy-start(f32[384,128]{1,0:T(8,128)} %copy.475) | copy-start | bytes 589828
  122.7 28.9 %copy-start.59 = (f32[128,320]{0,1:T(8,128)S(1)}, f32[128,320]{0,1:T(8,128)}, u32[]{:S(2)}) copy-start(f32[128,320]{0,1:T(8,128)} %convolution_subtract_fusion.6) | copy-start | bytes 491524
  122.8 28.9 %copy-start.58 = (f32[128,320]{0,1:T(8,128)S(1)}, f32[128,320]{0,1:T(8,128)}, u32[]{:S(2)}) copy-start(f32[128,320]{0,1:T(8,128)} %convolution_add_fusion.8) | copy-start | bytes 491524
  298.6 26.7 %collective-permute-start.2 = (bf16[29,64,32]{2,1,0:T(8,128)(2,1)}, bf16[29,64,32]{2,1,0:T(8,128)(2,1)S(1)}, u32[]{:S(2)}, u32[]{:S(2)}) collective-permute-start(bf16[29,64,32]{2,1,0:T(8,128)(2,1)} %get-tuple-element.348), channel_id=1, source_target_pairs={{0,32},{32,64},{64,96},{96,128},{128,160},{160,192},{192,224},{224... | collective-permute-start | bytes 356360 | tf_op jit(solution)/shard_map/ppermute | solution.py:10
  298.6 26.7 %collective-permute-start.3 = (bf16[29,64,32]{2,1,0:T(8,128)(2,1)}, bf16[29,64,32]{2,1,0:T(8,128)(2,1)S(1)}, u32[]{:S(2)}, u32[]{:S(2)}) collective-permute-start(bf16[29,64,32]{2,1,0:T(8,128)(2,1)} %get-tuple-element.349), channel_id=1, source_target_pairs={{0,736},{32,0},{64,32},{96,64},{128,96},{160,128},{192,160},{224,1... | collective-permute-start | bytes 356360 | tf_op jit(solution)/shard_map/ppermute | solution.py:10
  (276 other events, 1274.1 us)
Sparse Core Ops, SparseCore 0:
  325.4 492.7 all-reduce.2
where the time goes:
time: 840 us; the launch traced here: 830 us
  waiting for transfers between devices  489 us (58%)
  local copies, waits for them, and re-layouts  194 us (23%)
  matrix products  62.5 us (7%)
  other arithmetic  51.9 us (6%)
  between operations  18.9 us (2%)
  starting transfers between devices  13.7 us (2%)
    psum x1, waiting for transfers between devices, body(): lax.psum((grad_zero, grad_one, grad_two), ('graph', 'dp'))  489 us
    unnamed x724, local copies, waits for them, and re-layouts  57.8 us
    convert_element_type x28, local copies, waits for them, and re-layouts, rotate_back(): weights = frames[row, first:last].astype(jnp.float32)  39.8 us
    dot_general x22, matrix products, product(): return jnp.dot(left, right, preferred_element_type=jnp.float32)  23.6 us
    dot_general x18, matrix products, outer_sum(): lax.dot_general(left, right, (((1,), (1,)), ((), ())), preferred_element_...  22.1 us
    convert_element_type x56, local copies, waits for them, and re-layouts, rotate_into(): weights = frames[row, first:last].astype(jnp.float32)  17.6 us
    dot_general x18, matrix products, product_t(): lax.dot_general(left, right, (((0,), (0,)), ((), ())), preferred_element_...  16.9 us
  transfers between devices with their start and end apart: 5, of which 1 were waited for; matrix products, arithmetic and copies ran while one was open for 24% of the time, Pallas kernels for 0%

commit v1 on v0

v1 whole, which is shorter than its diff:
```python
import functools

import jax
import jax.numpy as jnp
from jax import lax
from jax.experimental import pallas as pl
from jax.experimental.pallas import tpu as pltpu
from jax.sharding import PartitionSpec as P

COEF, TRUNC, CH, LANES = 49, 29, 64, 128
CAP, GROUPS, SUB = 32, 4, 16
ROWS = TRUNC * CH
PAD_ROWS = 32
ZERO, PLUS1, MINUS1, PLUS2, MINUS2 = (0, 448), (448, 832), (832, 1216), (1216, 1536), (1536, 1856)
VMEM = 56 * 1024 * 1024
f32, bf16 = jnp.float32, jnp.bfloat16


def degree_rows(degree):
    rows = [degree]
    if degree >= 1:
        rows = rows + [6 + degree, 12 + degree]
    if degree >= 2:
        rows = rows + [17 + degree, 22 + degree]
    return rows


def dot(left, right):
    return jnp.dot(left, right, preferred_element_type=f32)


def dot_nt(left, right):
    return lax.dot_general(left, right, (((1,), (1,)), ((), ())), preferred_element_type=f32)


def dot_tn(left, right):
    return lax.dot_general(left, right, (((0,), (0,)), ((), ())), preferred_element_type=f32)


def iota(shape, axis):
    return lax.broadcasted_iota(jnp.int32, shape, axis)


def one_hot(index, value=1.0):
    lanes = index.shape[1]
    return jnp.where(iota((LANES, lanes), 0) == index, value, 0.0).astype(f32).astype(bf16)


def one_hot_rows(index_row, value=1.0):
    return one_hot(index_row, value)


def load_frames(frames, padded, wigner, bins):
    padded[:, 0:TRUNC, :] = wigner[...]
    lanes = bins.shape[1]
    found = dot(padded[...].reshape(COEF * PAD_ROWS, LANES), one_hot(bins))
    frames[...] = found.reshape(COEF, PAD_ROWS, lanes)


def rotate_into(frames, values, found, chunk):
    channels = values.shape[1]

    def step(index, carry):
        part = pl.ds(pl.multiple_of(index * chunk, chunk), chunk)
        for degree in range(7):
            rows = degree_rows(degree)
            total = {}
            for k in range(degree * degree, (degree + 1) * (degree + 1)):
                value = values[k, part, :].astype(f32)
                for row in rows:
                    term = frames[k, row : row + 1, :] * value
                    total[row] = term if row not in total else total[row] + term
            for row in rows:
                found[row, part, :] = total[row].astype(found.dtype)
        return carry

    lax.fori_loop(0, channels // chunk, step, 0)


def rotate_back(frames, values, found, chunk):
    channels = values.shape[1]

    def step(index, carry):
        part = pl.ds(pl.multiple_of(index * chunk, chunk), chunk)
        for degree in range(7):
            rows = degree_rows(degree)
            held = {row: values[row, part, :].astype(f32) for row in rows}
            for k in range(degree * degree, (degree + 1) * (degree + 1)):
                total = None
                for row in rows:
                    term = frames[k, row : row + 1, :] * held[row]
                    total = term if total is None else total + term
                found[k, part, :] = total.astype(found.dtype)
        return carry

    lax.fori_loop(0, channels // chunk, step, 0)


def flat(value):
    return value.reshape(value.shape[0] * value.shape[1], value.shape[2])


def halo_row(pair, fill):
    rest = jnp.full((1, LANES - 2 * CAP), fill, pair.dtype)
    return jnp.concatenate([pair[0:1, :], pair[1:2, :], rest], axis=1)


def packed_row(pair):
    pieces = [pair[slot : slot + 1, :] for slot in range(2) for _ in range(GROUPS)]
    return jnp.concatenate(pieces, axis=1)


def rim_kernel(node, wigner, atoms, bins, to_lower, to_upper, frames, padded, gathered, rotated):
    load_frames(frames, padded, wigner, packed_row(bins[...]))
    row = packed_row(atoms[...])
    wide = 2 * LANES
    group = (iota((GROUPS * LANES, wide), 1) & (LANES - 1)) >> 5
    entry = iota((GROUPS * LANES, wide), 0)
    table = jnp.where(entry == row + group * LANES, 1.0, 0.0).astype(f32).astype(bf16)
    left = jnp.concatenate(
        [flat(node[:, g * SUB : (g + 1) * SUB, :]) for g in range(GROUPS)], axis=1
    )
    gathered[...] = dot(left, table).reshape(COEF, SUB, wide)
    rotate_into(frames, gathered, rotated, SUB)
    to_lower[...] = rotated[:, :, 0:LANES]
    to_upper[...] = rotated[:, :, LANES:wide]


def conv_forward(rotated, conv, w_zero, w_one, w_two):
    def rows(span):
        return flat(rotated[span[0] // CH : span[1] // CH])

    def put(span, value):
        conv[span[0] // CH : span[1] // CH] = value.reshape(-1, CH, LANES)

    put(ZERO, dot(w_zero[...], rows(ZERO)))
    put(PLUS1, dot(w_one[0], rows(PLUS1)) - dot(w_one[1], rows(MINUS1)))
    put(MINUS1, dot(w_one[1], rows(PLUS1)) + dot(w_one[0], rows(MINUS1)))
    put(PLUS2, dot(w_two[0], rows(PLUS2)) - dot(w_two[1], rows(MINUS2)))
    put(MINUS2, dot(w_two[1], rows(PLUS2)) + dot(w_two[0], rows(MINUS2)))


def edge_work(rotated, frames, cot, targets, scale, weights, conv, message_grad, values, conv_grad, message):
    conv_forward(rotated, conv, *weights)
    values[...] = dot(flat(cot[...]), one_hot(targets, 0.5)).reshape(COEF, CH, LANES)
    rotate_into(frames, values, message_grad, 32)
    gating = jax.nn.sigmoid(conv[0])
    factor = gating * scale
    factor_grad = message_grad[0] * conv[0]
    for row in range(1, TRUNC):
        factor_grad = factor_grad + message_grad[row] * conv[row]
    extra = factor_grad * scale * gating * (1.0 - gating)
    for row in range(TRUNC):
        grad = message_grad[row] * factor
        if row == 0:
            grad = grad + extra
        conv_grad[row] = grad.astype(bf16)
        message[row] = conv[row] * factor


def inner_kernel(
    node, cot, wigner, w_zero, w_one, w_two, sources, targets, bins, scale,
    rotated, conv_grad, message,
    frames, padded, values, conv, message_grad,
):
    load_frames(frames, padded, wigner, bins[...])
    values[...] = dot(flat(node[...]), one_hot(sources[...])).reshape(COEF, CH, LANES)
    rotate_into(frames, values, rotated, 32)
    edge_work(rotated, frames, cot, targets[...], scale[...], (w_zero, w_one, w_two),
              conv, message_grad, values, conv_grad, message)


def spread_table():
    shape = (2 * LANES, GROUPS * LANES)
    lane, column = iota(shape, 0), iota(shape, 1)
    slot, where = lane >> 7, lane & (LANES - 1)
    group, inside = column >> 7, column & (LANES - 1)
    same = (where >> 5 == group) & (inside == slot * CAP + (where & (CAP - 1)))
    return jnp.where(same, 1.0, 0.0).astype(f32).astype(bf16)


def pack_grads(packed, zero, one, two):
    at = 0
    for value in [zero] + one + two:
        height, width = value.shape
        for first in range(0, width - LANES + 1, LANES):
            packed[at : at + height, :] = value[:, first : first + LANES].astype(bf16)
            at += height
        if width % LANES:
            first, half = width - width % LANES, height // 2
            piece = value[:, first:width]
            packed[at : at + half, :] = jnp.concatenate([piece[0:half], piece[half:]], axis=1).astype(bf16)
            at += half
    if at < packed.shape[0]:
        packed[at:, :] = jnp.zeros((packed.shape[0] - at, LANES), bf16)


def halo_kernel(
    core, from_lower, from_upper, cot, wigner, w_zero, w_one, w_two, targets, bins, scale, inner_rotated, inner_grad,
    conv_grad, message, keep, send,
    frames, padded, rotated, values, conv, message_grad, packed,
):
    load_frames(frames, padded, wigner, halo_row(bins[...], -1))
    left = jnp.concatenate([flat(from_lower[...]), flat(from_upper[...])], axis=1)
    spread = dot(left, spread_table()).astype(bf16)
    for g in range(GROUPS):
        rotated[:, g * SUB : (g + 1) * SUB, :] = spread[:, g * LANES : (g + 1) * LANES].reshape(TRUNC, SUB, LANES)
    edge_work(rotated, frames, cot, halo_row(targets[...], -1), halo_row(scale[...], 0.0), (w_zero, w_one, w_two),
              conv, message_grad, values, conv_grad, message)

    def grads(span):
        part = slice(span[0] // CH, span[1] // CH)
        return jnp.concatenate([flat(inner_grad[part]), flat(conv_grad[part])], axis=1)

    def inputs(span):
        part = slice(span[0] // CH, span[1] // CH)
        return jnp.concatenate([flat(inner_rotated[part]), flat(rotated[part])], axis=1)

    zero = dot_nt(grads(ZERO), inputs(ZERO))
    pairs = []
    for plus, minus in ((PLUS1, MINUS1), (PLUS2, MINUS2)):
        pairs.append([
            dot_nt(grads(plus), inputs(plus)) + dot_nt(grads(minus), inputs(minus)),
            dot_nt(grads(minus), inputs(plus)) - dot_nt(grads(plus), inputs(minus)),
        ])
    pack_grads(packed, zero, pairs[0], pairs[1])
    half = packed.shape[0] // 2
    keep[...] = packed[pl.ds(pl.multiple_of(core[0] * half, SUB), half), :]
    send[...] = packed[pl.ds(pl.multiple_of((1 - core[0]) * half, SUB), half), :]


def input_kernel(
    inner_grad, halo_grad, wigner, w_zero, w_one, w_two, bins, sources, cot,
    to_lower, to_upper, feature_grad,
    frames, padded, joint, source_grad,
):
    def grads(span):
        part = slice(span[0] // CH, span[1] // CH)
        return jnp.concatenate([flat(inner_grad[part]), flat(halo_grad[part])], axis=1)

    def put(span, value):
        joint[span[0] // CH : span[1] // CH] = value.astype(bf16).reshape(-1, CH, 2 * LANES)

    put(ZERO, dot_tn(w_zero[...], grads(ZERO)))
    for weights, plus, minus in ((w_one, PLUS1, MINUS1), (w_two, PLUS2, MINUS2)):
        put(plus, dot_tn(weights[0], grads(plus)) + dot_tn(weights[1], grads(minus)))
        put(minus, dot_tn(weights[0], grads(minus)) - dot_tn(weights[1], grads(plus)))
    left = jnp.concatenate(
        [flat(joint[:, g * SUB : (g + 1) * SUB, LANES : 2 * LANES]) for g in range(GROUPS)], axis=1
    )
    shape = (GROUPS * LANES, 2 * LANES)
    column, lane = iota(shape, 0), iota(shape, 1)
    slot, where = lane >> 7, lane & (LANES - 1)
    group, inside = column >> 7, column & (LANES - 1)
    same = (where >> 5 == group) & (inside == slot * CAP + (where & (CAP - 1)))
    gathered = dot(left, jnp.where(same, 1.0, 0.0).astype(f32).astype(bf16)).astype(bf16)
    to_lower[...] = gathered[:, 0:LANES].reshape(TRUNC, SUB, LANES)
    to_upper[...] = gathered[:, LANES : 2 * LANES].reshape(TRUNC, SUB, LANES)
    load_frames(frames, padded, wigner, bins[...])
    rotate_back(frames, joint.at[:, :, 0:LANES], source_grad, 32)
    scattered = dot_nt(flat(source_grad[...]), one_hot(sources[...])).reshape(COEF, CH, LANES)
    feature_grad[...] = cot[...].astype(f32) + scattered


def update_kernel(
    node, wigner, inner_message, halo_message, inner_bins, inner_targets, halo_bins, halo_targets,
    updated, frames, padded, inner_part, halo_part,
):
    load_frames(frames, padded, wigner, inner_bins[...])
    rotate_back(frames, inner_message, inner_part, 32)
    load_frames(frames, padded, wigner, halo_row(halo_bins[...], -1))
    rotate_back(frames, halo_message, halo_part, 32)
    left = jnp.concatenate([flat(inner_part[...]), flat(halo_part[...])], axis=1)
    table = jnp.concatenate(
        [one_hot(inner_targets[...], 0.5), one_hot(halo_row(halo_targets[...], -1), 0.5)], axis=1
    )
    summed = dot_nt(left, table).reshape(COEF, CH, LANES)
    updated[...] = (node[...].astype(f32) + summed).astype(bf16)


def back_kernel(
    back_zero, back_one, wigner, bins, atoms, partial, feature_grad,
    frames, padded, joint, source_grad,
):
    load_frames(frames, padded, wigner, packed_row(bins[...]))
    joint[:, :, 0:LANES] = back_zero[...]
    joint[:, :, LANES : 2 * LANES] = back_one[...]
    rotate_back(frames, joint, source_grad, SUB)
    row = packed_row(atoms[...])
    wide = 2 * LANES
    group = (iota((LANES, wide), 1) & (LANES - 1)) >> 5
    entry = iota((LANES, wide), 0)
    values = flat(source_grad[...])
    for g in range(GROUPS):
        table = jnp.where((entry == row) & (group == g), 1.0, 0.0).astype(f32).astype(bf16)
        scattered = dot_nt(values, table).reshape(COEF, SUB, LANES)
        part = slice(g * SUB, (g + 1) * SUB)
        feature_grad[:, part, :] = partial[:, part, :] + scattered


def unpack_kernel(replicas, core, mine, other, zero, one, two, packed):
    half = packed.shape[0] // 2
    packed[pl.ds(pl.multiple_of(core[0] * half, SUB), half), :] = flat(mine[...])
    packed[pl.ds(pl.multiple_of((1 - core[0]) * half, SUB), half), :] = flat(other[...])
    at = 0
    refs = [zero] + [one.at[0], one.at[1]] + [two.at[0], two.at[1]]
    for ref in refs:
        height, width = ref.shape
        for first in range(0, width - LANES + 1, LANES):
            ref[:, first : first + LANES] = packed[at : at + height, :].astype(f32) * (1.0 / replicas)
            at += height
        if width % LANES:
            first, half = width - width % LANES, height // 2
            value = packed[at : at + half, :].astype(f32) * (1.0 / replicas)
            ref[0:half, first:width] = value[:, 0 : width - first]
            ref[half:height, first:width] = value[:, width - first :]
            at += half


def call(kernel, outs, scratch, operands, flops, name, scalars=0):
    whole = pl.BlockSpec(memory_space=pltpu.VMEM)
    scalar = pl.BlockSpec(memory_space=pltpu.SMEM)
    moved = sum(v.size * v.dtype.itemsize for v in list(operands) + list(outs))
    return pl.pallas_call(
        kernel,
        out_shape=tuple(outs),
        in_specs=[scalar] * scalars + [whole] * (len(operands) - scalars),
        out_specs=tuple([whole] * len(outs)),
        scratch_shapes=scratch,
        compiler_params=pltpu.CompilerParams(vmem_limit_bytes=VMEM),
        cost_estimate=pl.CostEstimate(flops=flops, bytes_accessed=moved, transcendentals=0),
        name=name,
    )(*operands)


def arr(shape, dtype):
    return jax.ShapeDtypeStruct(shape, dtype)


def scr(shape, dtype):
    return pltpu.VMEM(shape, dtype)


def swap_cores(value):
    return lax.ppermute(value, "core", [(0, 1), (1, 0)])


def add_up(values):
    return jnp.sum(values.astype(f32), axis=0).astype(bf16)


def to_all(value, axes):
    copies = jnp.broadcast_to(value[None], (lax.axis_size(axes),) + value.shape)
    return lax.all_to_all(copies, axes, 0, 0)


def reduce_all(keep, send):
    plane = ("x", "y")
    pieces = lax.axis_size(plane)
    joint = (keep.astype(f32) + swap_cores(send).astype(f32)).astype(bf16)
    piece = add_up(lax.all_to_all(joint.reshape(pieces, -1, LANES), plane, 0, 0))
    piece = add_up(to_all(piece, "z"))
    mine = to_all(piece, plane)
    return mine, swap_cores(mine)


def from_behind(value, axis, steps):
    count = lax.axis_size(axis)
    return lax.ppermute(value, axis, [(source, (source + steps) % count) for source in range(count)])


PACKED = 5632


def body(
    node_features, cotangent, wigner, w_zero, w_one, w_two, edge_source, edge_target, edge_bin, edge_scale,
    send_atoms, send_bins, recv_targets, recv_bins, recv_scale,
):
    node, cot = node_features[0], cotangent[0]
    table = jnp.transpose(wigner, (2, 1, 0))
    graph = ("z", "core")
    out_atoms, out_bins = send_atoms[0], send_bins[0]
    in_targets, in_bins, in_scale = recv_targets[0], recv_bins[0], recv_scale[0]
    weights = [w_zero, w_one, w_two]
    packed_shape = arr((TRUNC, SUB, LANES), bf16)
    edges16, edges32 = arr((TRUNC, CH, LANES), bf16), arr((TRUNC, CH, LANES), f32)
    frames1, frames2 = scr((COEF, PAD_ROWS, LANES), f32), scr((COEF, PAD_ROWS, 2 * LANES), f32)
    padded = scr((COEF, PAD_ROWS, LANES), bf16)
    atoms32, rows32 = scr((COEF, CH, LANES), f32), scr((TRUNC, CH, LANES), f32)

    to_lower, to_upper = call(
        rim_kernel, [packed_shape] * 2,
        [frames2, padded, scr((COEF, SUB, 2 * LANES), f32), scr((TRUNC, SUB, 2 * LANES), bf16)],
        [node, table, out_atoms, out_bins], 10**9, "rim",
    )
    from_lower = from_behind(to_upper, graph, 1)
    from_upper = from_behind(to_lower, graph, -1)
    inner_rotated, inner_grad, inner_message = call(
        inner_kernel, [edges16, edges16, edges32],
        [frames1, padded, atoms32, rows32, rows32],
        [node, cot, table] + weights + [edge_source, edge_target, edge_bin, edge_scale], 10**10, "inner",
    )
    core = lax.axis_index("core").reshape(1)
    half = arr((PACKED // 2, LANES), bf16)
    halo_grad, halo_message, keep, send = call(
        halo_kernel, [edges16, edges32, half, half],
        [frames1, padded, scr((TRUNC, CH, LANES), bf16), atoms32, rows32, rows32, scr((PACKED, LANES), bf16)],
        [core, from_lower, from_upper, cot, table] + weights + [in_targets, in_bins, in_scale, inner_rotated, inner_grad],
        10**10, "halo", scalars=1,
    )
    mine, other = reduce_all(keep, send)
    back_lower, back_upper, partial = call(
        input_kernel, [packed_shape, packed_shape, arr((COEF, CH, LANES), f32)],
        [frames1, padded, scr((TRUNC, CH, 2 * LANES), bf16), scr((COEF, CH, LANES), bf16)],
        [inner_grad, halo_grad, table] + weights + [edge_bin, edge_source, cot], 10**10, "inputs",
    )
    back_zero = from_behind(back_upper, graph, 1)
    back_one = from_behind(back_lower, graph, -1)
    (updated,) = call(
        update_kernel, [arr((COEF, CH, LANES), bf16)],
        [frames1, padded, scr((COEF, CH, LANES), bf16), scr((COEF, CH, LANES), bf16)],
        [node, table, inner_message, halo_message, edge_bin, edge_target, in_bins, in_targets], 10**10, "update",
    )
    (feature_grad,) = call(
        back_kernel, [arr((COEF, CH, LANES), f32)],
        [frames2, padded, scr((TRUNC, SUB, 2 * LANES), bf16), scr((COEF, SUB, 2 * LANES), bf16)],
        [back_zero, back_one, table, out_bins, out_atoms, partial], 10**10, "back",
    )
    grad_zero, grad_one, grad_two = call(
        functools.partial(unpack_kernel, lax.axis_size(("x", "y"))), [arr(w_zero.shape, f32), arr(w_one.shape, f32), arr(w_two.shape, f32)],
        [scr((PACKED, LANES), bf16)], [core, mine, other], 0, "unpack", scalars=1,
    )
    return updated[None], feature_grad[None], grad_zero, grad_one, grad_two


def solution(mesh):
    cores, rows, columns = 2, 4, 8
    graph, replicas = mesh.shape["graph"], mesh.shape["dp"]
    if (graph, replicas) != (24, 32):
        cores, rows, columns = SMALL
    fine = jax.sharding.Mesh(mesh.devices.reshape(graph // cores, cores, rows, columns), ("z", "core", "x", "y"))
    dp, along = ("x", "y"), ("z", "core")
    nodes, edges = P(dp, None, None, along), P(dp, along)
    in_specs = (nodes, nodes) + (P(),) * 4 + (edges,) * 4 + (P(dp, along, None),) * 5
    return jax.shard_map(
        body, mesh=fine, in_specs=in_specs, out_specs=(nodes, nodes, P(), P(), P()), check_vma=False
    )
```

time: 840 us -> 127 us (0.15); the launches traced: 830 us -> 126 us
  waiting for transfers between devices: 489 us -> 4.08 us
  local copies, waits for them, and re-layouts: 194 us -> 3.19 us
  matrix products: 62.5 us -> 0 us
  other arithmetic: 51.9 us -> 1.45 us
  blocking collectives: 0 us -> 43.6 us
  Pallas kernels: 0 us -> 34.1 us
  starting transfers between devices: 13.7 us -> 38.5 us
  between operations: 18.9 us -> 0.73 us
    psum x1 -> x0, waiting for transfers between devices: 489 us -> none  [body(): lax.psum((grad_zero, grad_one, grad_two), ('graph', 'dp'))]
    dot_general x58 -> x0, matrix products: 62.5 us -> none  [the longest x22 23.6 us: product(): return jnp.dot(left, right, preferred_element_type=jnp.float32)]
    convert_element_type x85 -> x0, local copies, waits for them, and re-layouts: 59.4 us -> none  [the longest x28 39.8 us: rotate_back(): weights = frames[row, first:last].astype(jnp.float32)]
    unnamed x724 -> x12, local copies, waits for them, and re-layouts: 57.8 us -> 2.2 us
    all_to_all x0 -> x2, blocking collectives: none -> 43.6 us  [the longest x1 27.3 us: reduce_all(): lax.all_to_all(joint.reshape(pieces, -1, LANES), plane, 0, 0)]
    pallas_call x0 -> x7, Pallas kernels: none -> 34.1 us  [call(): pl.pallas_call(kernel, out_shape=tuple(outs), in_specs=[scalar] * scalars...]
    gather x10 -> x0, local copies, waits for them, and re-layouts: 21.2 us -> none  [the longest x2 7.47 us: body(): inner_gathered = jnp.take(node_local, sources, axis=2)]
    reshape x14 -> x0, local copies, waits for them, and re-layouts: 14.6 us -> none  [the longest x8 9.43 us: join_orders(): piece.reshape(-1, channels, count)]
  transfers between devices with their start and end apart: 5 -> 7, of which waited for: 1 -> 2; matrix products, arithmetic and copies ran while one was open for 24% -> 0% of each run, Pallas kernels for 0% -> 17%
where the time goes in v1:
time: 127 us; the launch traced here: 126 us
  blocking collectives  43.6 us (34%)
  starting transfers between devices  38.5 us (30%)
  Pallas kernels  34.1 us (27%)
  waiting for transfers between devices  4.08 us (3%)
  local copies, waits for them, and re-layouts  3.19 us (3%)
  other arithmetic  1.45 us (1%)
    pallas_call x7, Pallas kernels, call(): pl.pallas_call(kernel, out_shape=tuple(outs), in_specs=[scalar] * scalars...  34.1 us
    all_to_all x1, blocking collectives, reduce_all(): lax.all_to_all(joint.reshape(pieces, -1, LANES), plane, 0, 0)  27.3 us
    all_to_all x1, blocking collectives, to_all(): return lax.all_to_all(copies, axes, 0, 0)  16.4 us
    ppermute x4, starting transfers between devices, from_behind(): lax.ppermute(value, axis, [(source, (source + steps) % count) for source...  14.3 us
    ppermute x2, starting transfers between devices, swap_cores(): return lax.ppermute(value, 'core', [(0, 1), (1, 0)])  12.7 us
    all_to_all x1, starting transfers between devices, to_all(): return lax.all_to_all(copies, axes, 0, 0)  11.4 us
  transfers between devices with their start and end apart: 7, of which 2 were waited for; matrix products, arithmetic and copies ran while one was open for 0% of the time, Pallas kernels for 17%

profile of v1, /device:TPU:1, one launch (start us, length us, event | category | flops | bytes accessed | tf_op | source)
XLA Modules:
  0.0 125.7 jit_solution(5501501723760676782)
XLA Ops:
  0.6 2.7 %rim.1 = (bf16[29,16,128]{2,1,0:T(8,128)(2,1)}, bf16[29,16,128]{2,1,0:T(8,128)(2,1)}) custom-call(bf16[49,64,128]{2,1,0:T(8,128)(2,1)} %bitcast.16, bf16[49,29,128]{2,1,0:T(8,128)(2,1)} %bitcast.19, s32[2,32]{1,0:T(2,128)} %bitcast.30, s32[2,32]{1,0:T(2,128)} %bitcast.32), custom_call_target="tpu_custom_call" | custom-call | flops 1000000000 | bytes 1404672 | tf_op jit(solution)/shard_map/rim/pallas_call | solution.py:324
  3.3 3.5 %collective-permute-start = (bf16[29,16,128]{2,1,0:T(8,128)(2,1)}, bf16[29,16,128]{2,1,0:T(8,128)(2,1)S(1)}, u32[]{:S(2)}, u32[]{:S(2)}) collective-permute-start(bf16[29,16,128]{2,1,0:T(8,128)(2,1)} %get-tuple-element.21), channel_id=1, source_target_pairs={{0,32},{32,64},{64,96},{96,128},{128,160},{160,192},{192,224},{224... | collective-permute-start | bytes 356360 | tf_op jit(solution)/shard_map/ppermute | solution.py:369
  6.8 7.0 %collective-permute-start.1 = (bf16[29,16,128]{2,1,0:T(8,128)(2,1)}, bf16[29,16,128]{2,1,0:T(8,128)(2,1)S(1)}, u32[]{:S(2)}, u32[]{:S(2)}) collective-permute-start(bf16[29,16,128]{2,1,0:T(8,128)(2,1)} %get-tuple-element.22), channel_id=1, source_target_pairs={{0,736},{32,0},{64,32},{96,64},{128,96},{160,128},{192,160},{224,1... | collective-permute-start | bytes 356360 | tf_op jit(solution)/shard_map/ppermute | solution.py:369
  13.9 6.1 %inner.1 = (bf16[29,64,128]{2,1,0:T(8,128)(2,1)}, bf16[29,64,128]{2,1,0:T(8,128)(2,1)}, f32[29,64,128]{2,1,0:T(8,128)}) custom-call(bf16[49,64,128]{2,1,0:T(8,128)(2,1)} %bitcast.17, bf16[49,64,128]{2,1,0:T(8,128)(2,1)} %bitcast.13, bf16[49,29,128]{2,1,0:T(8,128)(2,1)} %bitcast.20, bf16[448,448]{1,0:T(8,128)(2,1)} %w_zero.5, bf16[2,384,384]{2,1,0:T(8,128)(2,1)} %w_one.5, ...), custom_call_target="tpu_custom_call" | custom-call | flops 10000000000 | bytes 5272832 | tf_op jit(solution)/shard_map/inner/pallas_call | solution.py:324
  19.9 0.0 collective-permute-done.from_lower
  20.0 0.0 collective-permute-done.1.from_upper
  20.0 0.6 copy-done.2
  20.6 0.0 copy-done.4
  20.6 7.2 %halo.1 = (bf16[29,64,128]{2,1,0:T(8,128)(2,1)}, f32[29,64,128]{2,1,0:T(8,128)}, bf16[2816,128]{1,0:T(8,128)(2,1)}, bf16[2816,128]{1,0:T(8,128)(2,1)}) custom-call(s32[1]{0:T(128)} %bitcast.3.core, bf16[29,16,128]{2,1,0:T(8,128)(2,1)} %copy-done.2, bf16[29,16,128]{2,1,0:T(8,128)(2,1)} %copy-done.4, bf16[49,64,128]{2,1,0:T(8,128)(2,1)} %bitcast.14, ...), custom_call_target="tpu_custom_call" | custom-call | flops 10000000000 | bytes 6623236 | tf_op jit(solution)/shard_map/halo/pallas_call | solution.py:324
  27.9 5.0 %collective-permute-start.4 = (bf16[2816,128]{1,0:T(8,128)(2,1)}, bf16[2816,128]{1,0:T(8,128)(2,1)S(1)}, u32[]{:S(2)}, u32[]{:S(2)}) collective-permute-start(bf16[2816,128]{1,0:T(8,128)(2,1)} %get-tuple-element.31), channel_id=1, source_target_pairs={{0,32},{32,0},{1,33},{33,1},{2,34},{34,2},{3,35},{35,3},{4,36},{36... | collective-permute-start | bytes 2162696 | tf_op jit(solution)/shard_map/ppermute | solution.py:345
  32.9 2.0 %collective-permute-done.4 = bf16[2816,128]{1,0:T(8,128)(2,1)S(1)} collective-permute-done((bf16[2816,128]{1,0:T(8,128)(2,1)}, bf16[2816,128]{1,0:T(8,128)(2,1)S(1)}, u32[]{:S(2)}, u32[]{:S(2)}) %collective-permute-start.4) | collective-permute-done | bytes 720928 | tf_op jit(solution)/shard_map/ppermute | solution.py:345
  34.9 1.3 %add_convert_fusion = bf16[2816,128]{1,0:T(8,128)(2,1)S(1)} fusion(bf16[2816,128]{1,0:T(8,128)(2,1)S(1)} %collective-permute-done.4, bf16[2816,128]{1,0:T(8,128)(2,1)} %get-tuple-element.30), kind=kLoop, calls=%fused_computation | loop fusion | flops 1441792 | bytes 2162688 | tf_op jit(solution)/shard_map/convert_element_type | solution.py:360
  36.2 27.3 %all_to_all.15 = bf16[32,88,128]{2,1,0:T(8,128)(2,1)S(1)} all-to-all(bf16[32,88,128]{2,1,0:T(8,128)(2,1)S(1)} %bitcast.12), channel_id=1, replica_groups=mesh['z'=12,'core'=2,'x'=4,'y'=8] {'x','y'}, dimensions={0} | all-to-all | bytes 1441792 | tf_op jit(solution)/shard_map/all_to_all | solution.py:361
  63.5 0.1 reduce_sum.24
  63.6 16.4 %all_to_all.16 = bf16[12,88,128]{2,1,0:T(8,128)(2,1)S(1)} all-to-all(bf16[12,88,128]{2,1,0:T(8,128)(2,1)S(1)} %broadcast_in_dim.20), channel_id=1, replica_groups=mesh['z'=12,'core'=2,'x'=4,'y'=8] {'z'}, dimensions={0} | all-to-all | bytes 540672 | tf_op jit(solution)/shard_map/all_to_all | solution.py:354
  80.0 1.0 broadcast_in_dim.21
  81.0 11.4 %all-to-all-start.2 = ((bf16[32,88,128]{2,1,0:T(8,128)(2,1)}), bf16[32,88,128]{2,1,0:T(8,128)(2,1)S(1)}, u32[]{:S(2)}, u32[]{:S(2)}) async-start(bf16[32,88,128]{2,1,0:T(8,128)(2,1)} %broadcast_in_dim.21), calls=%async_computation.2 | async-start | bytes 1441792 | tf_op jit(solution)/shard_map/all_to_all | solution.py:354
  92.4 5.6 %inputs.1 = (bf16[29,16,128]{2,1,0:T(8,128)(2,1)}, bf16[29,16,128]{2,1,0:T(8,128)(2,1)}, f32[49,64,128]{2,1,0:T(8,128)}) custom-call(bf16[29,64,128]{2,1,0:T(8,128)(2,1)} %get-tuple-element.24.inner_grad, bf16[29,64,128]{2,1,0:T(8,128)(2,1)} %get-tuple-element.26.halo_grad, bf16[49,29,128]{2,1,0:T(8,128)(2,1)} %bitcast.22, bf16[448,448]{1,0:T(8,128)(2,1)} %w_zero.5, ...), custom_call_target="tpu_custom_call" | custom-call | flops 10000000000 | bytes 5361920 | tf_op jit(solution)/shard_map/inputs/pallas_call | solution.py:324
  98.0 3.8 %collective-permute-start.2 = (bf16[29,16,128]{2,1,0:T(8,128)(2,1)}, bf16[29,16,128]{2,1,0:T(8,128)(2,1)S(1)}, u32[]{:S(2)}, u32[]{:S(2)}) collective-permute-start(bf16[29,16,128]{2,1,0:T(8,128)(2,1)} %get-tuple-element.27), channel_id=1, source_target_pairs={{0,32},{32,64},{64,96},{96,128},{128,160},{160,192},{192,224},{224... | collective-permute-start | bytes 356360 | tf_op jit(solution)/shard_map/ppermute | solution.py:369
  101.8 0.0 collective-permute-start.3
  101.8 5.1 %update.1 = bf16[49,64,128]{2,1,0:T(8,128)(2,1)} custom-call(bf16[49,64,128]{2,1,0:T(8,128)(2,1)} %bitcast.18, bf16[49,29,128]{2,1,0:T(8,128)(2,1)} %bitcast.23, f32[29,64,128]{2,1,0:T(8,128)} %get-tuple-element.20.inner_message, f32[29,64,128]{2,1,0:T(8,128)} %get-tuple-element.25.halo_message, s32[1,128]{1,0:T(1,128)} %bins.3, s32[1,128]{1,0:T(1,128)} %inner_targets.1, ...), custom_call_target="tpu_custom_call" | custom-call | flops 10000000000 | bytes 3871488 | tf_op jit(solution)/shard_map/update/pallas_call | solution.py:324
  106.9 2.1 %all-to-all-done.2.mine = bf16[32,88,128]{2,1,0:T(8,128)(2,1)S(1)} async-done(((bf16[32,88,128]{2,1,0:T(8,128)(2,1)}), bf16[32,88,128]{2,1,0:T(8,128)(2,1)S(1)}, u32[]{:S(2)}, u32[]{:S(2)}) %all-to-all-start.2) | async-done | bytes 720928 | tf_op jit(solution)/shard_map/all_to_all | solution.py:354
  109.0 7.7 %collective-permute-start.5 = (bf16[32,88,128]{2,1,0:T(8,128)(2,1)S(1)}, bf16[32,88,128]{2,1,0:T(8,128)(2,1)S(1)}, u32[]{:S(2)}, u32[]{:S(2)}) collective-permute-start(bf16[32,88,128]{2,1,0:T(8,128)(2,1)S(1)} %all-to-all-done.2.mine), channel_id=1, source_target_pairs={{0,32},{32,0},{1,33},{33,1},{2,34},{34,2},{3,35},{35,3},{4,36},{36... | collective-permute-start | bytes 2162696 | tf_op jit(solution)/shard_map/ppermute | solution.py:345
  116.7 0.0 collective-permute-done.2.back_zero
  116.7 0.0 copy-start.3
  116.7 0.0 collective-permute-done.3.back_one
  116.7 0.0 copy-start.5
  116.8 0.6 copy-done.3
  117.4 0.0 copy-done.5
  117.4 4.2 %back.1 = f32[49,64,128]{2,1,0:T(8,128)} custom-call(bf16[29,16,128]{2,1,0:T(8,128)(2,1)} %copy-done.3, bf16[29,16,128]{2,1,0:T(8,128)(2,1)} %copy-done.5, bf16[49,29,128]{2,1,0:T(8,128)(2,1)} %bitcast.24, s32[2,32]{1,0:T(2,128)} %bitcast.33, s32[2,32]{1,0:T(2,128)} %bitcast.31, f32[49,64,128]{2,1,0:T(8,128)} %get-tuple-element.29.partial), custom_call_target="tpu_custom_call" | custom-call | flops 10000000000 | bytes 3813120 | tf_op jit(solution)/shard_map/back/pallas_call | solution.py:324
  121.6 0.9 copy-done.1
  122.4 3.2 %unpack.1 = (f32[448,448]{1,0:T(8,128)}, f32[2,384,384]{2,1,0:T(8,128)}, f32[2,320,320]{2,1,0:T(8,128)}) custom-call(s32[1]{0:T(128)} %bitcast.3.core, bf16[32,88,128]{2,1,0:T(8,128)(2,1)} %copy-done, bf16[32,88,128]{2,1,0:T(8,128)(2,1)} %copy-done.1), custom_call_target="tpu_custom_call" | custom-call | bytes 4243460 | tf_op jit(solution)/shard_map/unpack/pallas_call | solution.py:324
  (8 shorter events, 0.1 us)
Async XLA Ops:
  3.3 16.6 %collective-permute-start = (bf16[29,16,128]{2,1,0:T(8,128)(2,1)}, bf16[29,16,128]{2,1,0:T(8,128)(2,1)S(1)}, u32[]{:S(2)}, u32[]{:S(2)}) collective-permute-start(bf16[29,16,128]{2,1,0:T(8,128)(2,1)} %get-tuple-element.21), channel_id=1, source_target_pairs={{0,32},{32,64},{64,96},{96,128},{128,160},{160,192},{192,224},{224... | collective-permute-start | bytes 356360 | tf_op jit(solution)/shard_map/ppermute | solution.py:369
  6.8 13.1 %collective-permute-start.1 = (bf16[29,16,128]{2,1,0:T(8,128)(2,1)}, bf16[29,16,128]{2,1,0:T(8,128)(2,1)S(1)}, u32[]{:S(2)}, u32[]{:S(2)}) collective-permute-start(bf16[29,16,128]{2,1,0:T(8,128)(2,1)} %get-tuple-element.22), channel_id=1, source_target_pairs={{0,736},{32,0},{64,32},{96,64},{128,96},{160,128},{192,160},{224,1... | collective-permute-start | bytes 356360 | tf_op jit(solution)/shard_map/ppermute | solution.py:369
  19.9 0.7 copy-start.2
  20.0 0.7 copy-start.4
  27.9 7.0 %collective-permute-start.4 = (bf16[2816,128]{1,0:T(8,128)(2,1)}, bf16[2816,128]{1,0:T(8,128)(2,1)S(1)}, u32[]{:S(2)}, u32[]{:S(2)}) collective-permute-start(bf16[2816,128]{1,0:T(8,128)(2,1)} %get-tuple-element.31), channel_id=1, source_target_pairs={{0,32},{32,0},{1,33},{33,1},{2,34},{34,2},{3,35},{35,3},{4,36},{36... | collective-permute-start | bytes 2162696 | tf_op jit(solution)/shard_map/ppermute | solution.py:345
  81.0 28.0 %all-to-all-start.2 = ((bf16[32,88,128]{2,1,0:T(8,128)(2,1)}), bf16[32,88,128]{2,1,0:T(8,128)(2,1)S(1)}, u32[]{:S(2)}, u32[]{:S(2)}) async-start(bf16[32,88,128]{2,1,0:T(8,128)(2,1)} %broadcast_in_dim.21), calls=%async_computation.2 | async-start | bytes 1441792 | tf_op jit(solution)/shard_map/all_to_all | solution.py:354
  98.0 18.7 %collective-permute-start.2 = (bf16[29,16,128]{2,1,0:T(8,128)(2,1)}, bf16[29,16,128]{2,1,0:T(8,128)(2,1)S(1)}, u32[]{:S(2)}, u32[]{:S(2)}) collective-permute-start(bf16[29,16,128]{2,1,0:T(8,128)(2,1)} %get-tuple-element.27), channel_id=1, source_target_pairs={{0,32},{32,64},{64,96},{96,128},{128,160},{160,192},{192,224},{224... | collective-permute-start | bytes 356360 | tf_op jit(solution)/shard_map/ppermute | solution.py:369
  101.8 14.9 %collective-permute-start.3 = (bf16[29,16,128]{2,1,0:T(8,128)(2,1)}, bf16[29,16,128]{2,1,0:T(8,128)(2,1)S(1)}, u32[]{:S(2)}, u32[]{:S(2)}) collective-permute-start(bf16[29,16,128]{2,1,0:T(8,128)(2,1)} %get-tuple-element.28), channel_id=1, source_target_pairs={{0,736},{32,0},{64,32},{96,64},{128,96},{160,128},{192,160},{224,1... | collective-permute-start | bytes 356360 | tf_op jit(solution)/shard_map/ppermute | solution.py:369
  109.0 12.6 %copy-start = (bf16[32,88,128]{2,1,0:T(8,128)(2,1)}, bf16[32,88,128]{2,1,0:T(8,128)(2,1)S(1)}, u32[]{:S(2)}) copy-start(bf16[32,88,128]{2,1,0:T(8,128)(2,1)S(1)} %all-to-all-done.2.mine) | copy-start | bytes 2162692
  109.0 12.6 %collective-permute-start.5 = (bf16[32,88,128]{2,1,0:T(8,128)(2,1)S(1)}, bf16[32,88,128]{2,1,0:T(8,128)(2,1)S(1)}, u32[]{:S(2)}, u32[]{:S(2)}) collective-permute-start(bf16[32,88,128]{2,1,0:T(8,128)(2,1)S(1)} %all-to-all-done.2.mine), channel_id=1, source_target_pairs={{0,32},{32,0},{1,33},{33,1},{2,34},{34,2},{3,35},{35,3},{4,36},{36... | collective-permute-start | bytes 2162696 | tf_op jit(solution)/shard_map/ppermute | solution.py:345
  116.7 0.7 copy-start.3
  116.7 0.7 copy-start.5
  121.6 0.9 copy-start.1

commit v2 on v1

v2 whole, which is shorter than its diff:
```python
import functools

import jax
import jax.numpy as jnp
from jax import lax
from jax.experimental import pallas as pl
from jax.experimental.pallas import tpu as pltpu
from jax.sharding import PartitionSpec as P

COEF, TRUNC, CH, LANES = 49, 29, 64, 128
CAP, GROUPS, SUB = 32, 4, 16
WIDE = 2 * LANES
PAD_ROWS = 32
ZERO, PLUS1, MINUS1, PLUS2, MINUS2 = (0, 448), (448, 832), (832, 1216), (1216, 1536), (1536, 1856)
VMEM = 24 * 1024 * 1024
f32, bf16 = jnp.float32, jnp.bfloat16


def degree_rows(degree):
    rows = [degree]
    if degree >= 1:
        rows = rows + [6 + degree, 12 + degree]
    if degree >= 2:
        rows = rows + [17 + degree, 22 + degree]
    return rows


def dot(left, right):
    return jnp.dot(left, right, preferred_element_type=f32)


def dot_nt(left, right):
    return lax.dot_general(left, right, (((1,), (1,)), ((), ())), preferred_element_type=f32)


def dot_tn(left, right):
    return lax.dot_general(left, right, (((0,), (0,)), ((), ())), preferred_element_type=f32)


def iota(shape, axis):
    return lax.broadcasted_iota(jnp.int32, shape, axis)


def one_hot(index, value=1.0):
    lanes = index.shape[1]
    return jnp.where(iota((LANES, lanes), 0) == index, value, 0.0).astype(f32).astype(bf16)


def load_frames(frames, padded, wigner, bins):
    padded[:, 0:TRUNC, :] = wigner[...]
    lanes = bins.shape[1]
    found = dot(padded[...].reshape(COEF * PAD_ROWS, LANES), one_hot(bins))
    frames[...] = found.reshape(COEF, PAD_ROWS, lanes)


def rotate_into(frames, values, found, chunk):
    channels = values.shape[1]

    def step(index, carry):
        part = pl.ds(pl.multiple_of(index * chunk, chunk), chunk)
        for degree in range(7):
            rows = degree_rows(degree)
            total = {}
            for k in range(degree * degree, (degree + 1) * (degree + 1)):
                value = values[k, part, :].astype(f32)
                for row in rows:
                    term = frames[k, row : row + 1, :] * value
                    total[row] = term if row not in total else total[row] + term
            for row in rows:
                found[row, part, :] = total[row].astype(found.dtype)
        return carry

    lax.fori_loop(0, channels // chunk, step, 0)


def rotate_back(frames, values, found, chunk):
    channels = values.shape[1]

    def step(index, carry):
        part = pl.ds(pl.multiple_of(index * chunk, chunk), chunk)
        for degree in range(7):
            rows = degree_rows(degree)
            held = {row: values[row, part, :].astype(f32) for row in rows}
            for k in range(degree * degree, (degree + 1) * (degree + 1)):
                total = None
                for row in rows:
                    term = frames[k, row : row + 1, :] * held[row]
                    total = term if total is None else total + term
                found[k, part, :] = total.astype(found.dtype)
        return carry

    lax.fori_loop(0, channels // chunk, step, 0)


def flat(value):
    return value.reshape(value.shape[0] * value.shape[1], value.shape[2])


def halo_row(pair, fill):
    rest = jnp.full((1, LANES - 2 * CAP), fill, pair.dtype)
    return jnp.concatenate([pair[0:1, :], pair[1:2, :], rest], axis=1)


def packed_row(pair):
    pieces = [pair[slot : slot + 1, :] for slot in range(2) for _ in range(GROUPS)]
    return jnp.concatenate(pieces, axis=1)


def rim_kernel(
    node_far, wigner_far, atoms_far, bins_far, to_lower, to_upper,
    frames, padded, gathered, rotated, node, wigner, atoms, bins, sems,
):
    pairs = [(wigner_far, wigner), (bins_far, bins), (atoms_far, atoms), (node_far, node)]
    copies = [pltpu.make_async_copy(far, near, sems.at[index]) for index, (far, near) in enumerate(pairs)]
    for copy in copies:
        copy.start()
    for copy in copies[0:3]:
        copy.wait()
    load_frames(frames, padded, wigner, packed_row(bins[...]))
    copies[3].wait()
    row = packed_row(atoms[...])
    wide = 2 * LANES
    group = (iota((GROUPS * LANES, wide), 1) & (LANES - 1)) >> 5
    entry = iota((GROUPS * LANES, wide), 0)
    table = jnp.where(entry == row + group * LANES, 1.0, 0.0).astype(f32).astype(bf16)
    left = jnp.concatenate(
        [flat(node[:, g * SUB : (g + 1) * SUB, :]) for g in range(GROUPS)], axis=1
    )
    gathered[...] = dot(left, table).reshape(COEF, SUB, wide)
    rotate_into(frames, gathered, rotated, SUB)
    to_lower[...] = rotated[:, :, 0:LANES]
    to_upper[...] = rotated[:, :, LANES:wide]


def pre_kernel(node, wigner, sources, bins, rotated_far, frames, padded, values, rotated, sem):
    load_frames(frames, padded, wigner, bins[...])
    values[...] = dot(flat(node[...]), one_hot(sources[...])).reshape(COEF, CH, LANES)
    rotate_into(frames, values, rotated, 32)
    copy = pltpu.make_async_copy(rotated, rotated_far, sem)
    copy.start()
    copy.wait()


def rows_of(values, first, last):
    return flat(values[first[0] // CH : last[1] // CH])


def conv_forward(rotated, conv, w_zero, w_one, w_two):
    def put(span, value):
        conv[span[0] // CH : span[1] // CH] = value.reshape(-1, CH, WIDE)

    put(ZERO, dot(w_zero[...], rows_of(rotated, ZERO, ZERO)))
    both = rows_of(rotated, PLUS1, MINUS1)
    put(PLUS1, dot(jnp.concatenate([w_one[0], -w_one[1]], axis=1), both))
    put(MINUS1, dot(jnp.concatenate([w_one[1], w_one[0]], axis=1), both))
    plus, minus = rows_of(rotated, PLUS2, PLUS2), rows_of(rotated, MINUS2, MINUS2)
    put(PLUS2, dot(w_two[0], plus) - dot(w_two[1], minus))
    put(MINUS2, dot(w_two[1], plus) + dot(w_two[0], minus))


def spread_table():
    shape = (2 * LANES, GROUPS * LANES)
    lane, column = iota(shape, 0), iota(shape, 1)
    slot, where = lane >> 7, lane & (LANES - 1)
    group, inside = column >> 7, column & (LANES - 1)
    same = (where >> 5 == group) & (inside == slot * CAP + (where & (CAP - 1)))
    return jnp.where(same, 1.0, 0.0).astype(f32).astype(bf16)


def pack_grads(packed, values):
    at = 0
    for value in values:
        height, width = value.shape
        for first in range(0, width - LANES + 1, LANES):
            packed[at : at + height, :] = value[:, first : first + LANES].astype(bf16)
            at += height
        if width % LANES:
            first, half = width - width % LANES, height // 2
            piece = value[:, first:width]
            packed[at : at + half, :] = jnp.concatenate([piece[0:half], piece[half:]], axis=1).astype(bf16)
            at += half
    packed[at:, :] = jnp.zeros((packed.shape[0] - at, LANES), bf16)


def conv_kernel(
    core, from_lower, from_upper, cot, wigner, targets, bins, halo_targets, halo_bins, w_zero, w_one, w_two,
    scale, halo_scale, inner_rotated,
    conv_grad_far, message, keep, send,
    rotated, conv, packed, message_grad, conv_grad, frames, padded, values, sems,
):
    get_rotated = pltpu.make_async_copy(inner_rotated, rotated.at[:, :, 0:LANES], sems.at[0])
    get_rotated.start()
    joint_bins = jnp.concatenate([bins[...], halo_row(halo_bins[...], -1)], axis=1)
    joint_targets = jnp.concatenate([targets[...], halo_row(halo_targets[...], -1)], axis=1)
    load_frames(frames, padded, wigner, joint_bins)
    values[...] = dot(flat(cot[...]), one_hot(joint_targets, 0.5)).reshape(COEF, CH, WIDE)
    rotate_into(frames, values, message_grad, 16)
    left = jnp.concatenate([flat(from_lower[...]), flat(from_upper[...])], axis=1)
    spread = dot(left, spread_table()).astype(bf16)
    for g in range(GROUPS):
        rotated[:, g * SUB : (g + 1) * SUB, LANES:WIDE] = spread[:, g * LANES : (g + 1) * LANES].reshape(
            TRUNC, SUB, LANES
        )
    get_rotated.wait()
    conv_forward(rotated, conv, w_zero, w_one, w_two)
    weight = jnp.concatenate([scale[...], halo_row(halo_scale[...], 0.0)], axis=1)
    gating = jax.nn.sigmoid(conv[0])
    factor = gating * weight
    factor_grad = message_grad[0] * conv[0]
    for row in range(1, TRUNC):
        value = conv[row]
        grad = message_grad[row]
        factor_grad = factor_grad + grad * value
        conv_grad[row] = (grad * factor).astype(bf16)
        message[row] = value * factor
    conv_grad[0] = (message_grad[0] * factor + factor_grad * weight * gating * (1.0 - gating)).astype(bf16)
    message[0] = conv[0] * factor
    put = pltpu.make_async_copy(conv_grad, conv_grad_far, sems.at[1])
    put.start()

    zero = dot_nt(rows_of(conv_grad, ZERO, ZERO), rows_of(rotated, ZERO, ZERO))
    pairs = []
    for plus, minus in ((PLUS1, MINUS1), (PLUS2, MINUS2)):
        g_plus, g_minus = rows_of(conv_grad, plus, plus), rows_of(conv_grad, minus, minus)
        inputs = jnp.concatenate([rows_of(rotated, plus, plus), rows_of(rotated, minus, minus)], axis=1)
        pairs.append([
            dot_nt(jnp.concatenate([g_plus, g_minus], axis=1), inputs),
            dot_nt(jnp.concatenate([g_minus, -g_plus], axis=1), inputs),
        ])
    one, two = pairs
    pack_grads(packed.at[0], [zero, one[0]])
    pack_grads(packed.at[1], [one[1]] + two)
    keep[...] = packed[core[0]]
    send[...] = packed[1 - core[0]]
    put.wait()


def input_kernel(conv_grad, w_zero, w_one, w_two, after, to_lower, to_upper, inner, joint):
    def put(span, value):
        joint[span[0] // CH : span[1] // CH] = value.astype(bf16).reshape(-1, CH, WIDE)

    put(ZERO, dot_tn(w_zero[...], rows_of(conv_grad, ZERO, ZERO)))
    for weights, plus, minus in ((w_one, PLUS1, MINUS1), (w_two, PLUS2, MINUS2)):
        both = flat(weights[...])
        put(plus, dot_tn(both, rows_of(conv_grad, plus, minus)))
        crossed = jnp.concatenate([rows_of(conv_grad, minus, minus), -rows_of(conv_grad, plus, plus)], axis=0)
        put(minus, dot_tn(both, crossed))
    left = jnp.concatenate(
        [flat(joint[:, g * SUB : (g + 1) * SUB, LANES:WIDE]) for g in range(GROUPS)], axis=1
    )
    shape = (GROUPS * LANES, WIDE)
    column, lane = iota(shape, 0), iota(shape, 1)
    slot, where = lane >> 7, lane & (LANES - 1)
    group, inside = column >> 7, column & (LANES - 1)
    same = (where >> 5 == group) & (inside == slot * CAP + (where & (CAP - 1)))
    gathered = dot(left, jnp.where(same, 1.0, 0.0).astype(f32).astype(bf16)).astype(bf16)
    to_lower[...] = gathered[:, 0:LANES].reshape(TRUNC, SUB, LANES)
    to_upper[...] = gathered[:, LANES:WIDE].reshape(TRUNC, SUB, LANES)
    inner[...] = joint[:, :, 0:LANES]


def update_kernel(
    node, wigner, message, bins, targets, halo_bins, halo_targets, after,
    updated, token, frames, padded, part,
):
    joint_bins = jnp.concatenate([bins[...], halo_row(halo_bins[...], -1)], axis=1)
    joint_targets = jnp.concatenate([targets[...], halo_row(halo_targets[...], -1)], axis=1)
    load_frames(frames, padded, wigner, joint_bins)
    rotate_back(frames, message, part, 16)
    summed = dot_nt(flat(part[...]), one_hot(joint_targets, 0.5)).reshape(COEF, CH, LANES)
    updated[...] = (node[...].astype(f32) + summed).astype(bf16)
    token[...] = jnp.zeros(token.shape, token.dtype)


def back_kernel(
    back_zero, back_one, inner, wigner, rim_bins, atoms, bins, sources, cot, after, feature_grad, token,
    frames, inner_frames, padded, joint, rim_grad, inner_grad,
):
    load_frames(inner_frames, padded, wigner, bins[...])
    rotate_back(inner_frames, inner, inner_grad, 32)
    load_frames(frames, padded, wigner, packed_row(rim_bins[...]))
    joint[:, :, 0:LANES] = back_zero[...]
    joint[:, :, LANES:WIDE] = back_one[...]
    rotate_back(frames, joint, rim_grad, SUB)
    row = packed_row(atoms[...])
    group = (iota((LANES, WIDE), 1) & (LANES - 1)) >> 5
    entry = iota((LANES, WIDE), 0)
    values = flat(rim_grad[...])
    inner_table = one_hot(sources[...])
    for g in range(GROUPS):
        part = slice(g * SUB, (g + 1) * SUB)
        table = jnp.where((entry == row) & (group == g), 1.0, 0.0).astype(f32).astype(bf16)
        scattered = dot_nt(values, table) + dot_nt(flat(inner_grad[:, part, :]), inner_table)
        feature_grad[:, part, :] = cot[:, part, :].astype(f32) + scattered.reshape(COEF, SUB, LANES)
    token[...] = jnp.zeros(token.shape, token.dtype)


def add_kernel(pieces, after, total):
    found = pieces[0].astype(f32)
    for index in range(1, pieces.shape[0]):
        found = found + pieces[index].astype(f32)
    found = found.astype(bf16)
    if total.ndim == 2:
        total[...] = found
    else:
        for index in range(total.shape[0]):
            total[index] = found


def join_kernel(keep, other, joint):
    joint[...] = (keep[...].astype(f32) + other[...].astype(f32)).astype(bf16)


def unpack_kernel(replicas, swapped, which, packed, *refs):
    (zero, one, two), (zero_v, one_v, two_v), sems = refs[-7:-4], refs[-4:-1], refs[-1]

    def write(pairs):
        at = 0
        copies = []
        for index, (ref, out) in enumerate(pairs):
            height, width = ref.shape
            for first in range(0, width - LANES + 1, LANES):
                ref[:, first : first + LANES] = packed[at : at + height, :].astype(f32) * (1.0 / replicas)
                at += height
            if width % LANES:
                first, part = width - width % LANES, height // 2
                value = packed[at : at + part, :].astype(f32) * (1.0 / replicas)
                ref[0:part, first:width] = value[:, 0 : width - first]
                ref[part:height, first:width] = value[:, width - first :]
                at += part
            copy = pltpu.make_async_copy(ref, out, sems.at[index])
            copy.start()
            copies.append(copy)
        for copy in copies:
            copy.wait()

    half = 1 - which[0] if swapped else which[0]

    @pl.when(half == 0)
    def first():
        write([(zero_v, zero), (one_v.at[0], one.at[0])])

    @pl.when(half == 1)
    def second():
        write([(one_v.at[1], one.at[1]), (two_v.at[0], two.at[0]), (two_v.at[1], two.at[1])])


def call(kernel, outs, scratch, operands, flops, name, scalars=0, far=0, hbm=0, far_outs=0, aliases=None):
    whole = pl.BlockSpec(memory_space=pltpu.VMEM)
    scalar = pl.BlockSpec(memory_space=pltpu.SMEM)
    away = pl.BlockSpec(memory_space=pl.ANY)
    main = pl.BlockSpec(memory_space=pltpu.HBM)
    moved = sum(v.size * v.dtype.itemsize for v in list(operands) + list(outs))
    operands = list(operands)
    for index in range(len(operands) - hbm, len(operands)):
        operands[index] = pltpu.with_memory_space_constraint(operands[index], pltpu.HBM)
    outs = [pltpu.HBM(v.shape, v.dtype) if index < far_outs else v for index, v in enumerate(outs)]
    near = len(operands) - scalars - far - hbm
    return pl.pallas_call(
        kernel,
        out_shape=tuple(outs),
        in_specs=[scalar] * scalars + [whole] * near + [away] * far + [main] * hbm,
        out_specs=tuple([main] * far_outs + [whole] * (len(outs) - far_outs)),
        scratch_shapes=scratch,
        input_output_aliases=aliases or {},
        compiler_params=pltpu.CompilerParams(vmem_limit_bytes=VMEM),
        cost_estimate=pl.CostEstimate(flops=flops, bytes_accessed=moved, transcendentals=0),
        name=name,
    )(*operands)


def arr(shape, dtype):
    return jax.ShapeDtypeStruct(shape, dtype)


def scr(shape, dtype):
    return pltpu.VMEM(shape, dtype)


def from_behind(value, axis, steps):
    count = lax.axis_size(axis)
    return lax.ppermute(value, axis, [(source, (source + steps) % count) for source in range(count)])


def swap_cores(value):
    return lax.ppermute(value, "core", [(0, 1), (1, 0)])


def to_all(copies, axes):
    return lax.all_to_all(copies, axes, 0, 0)


PACKED = 5632
SPLIT = (2, 4, 8)
PLANE = ("x", "y")


def body(
    node_features, cotangent, wigner, w_zero, w_one, w_two, edge_source, edge_target, edge_bin, edge_scale,
    send_atoms, send_bins, recv_targets, recv_bins, recv_scale,
):
    node, cot = node_features[0], cotangent[0]
    table = jnp.transpose(wigner, (2, 1, 0))
    graph = ("z", "core")
    out_atoms, out_bins = send_atoms[0], send_bins[0]
    in_targets, in_bins, in_scale = recv_targets[0], recv_bins[0], recv_scale[0]
    weights = [w_zero, w_one, w_two]
    packed_shape = arr((TRUNC, SUB, LANES), bf16)
    edges16, edges32 = arr((TRUNC, CH, WIDE), bf16), arr((TRUNC, CH, WIDE), f32)
    frames1, frames2 = scr((COEF, PAD_ROWS, LANES), f32), scr((COEF, PAD_ROWS, WIDE), f32)
    padded = scr((COEF, PAD_ROWS, LANES), bf16)
    mark = arr((8, LANES), f32)

    to_lower, to_upper = call(
        rim_kernel, [packed_shape] * 2,
        [frames2, padded, scr((COEF, SUB, WIDE), f32), scr((TRUNC, SUB, WIDE), bf16),
         scr(node.shape, bf16), scr(table.shape, bf16), scr(out_atoms.shape, jnp.int32),
         scr(out_bins.shape, jnp.int32), pltpu.SemaphoreType.DMA((4,))],
        [node, table, out_atoms, out_bins], 10**9, "rim", hbm=4,
    )
    from_lower = from_behind(to_upper, graph, 1)
    from_upper = from_behind(to_lower, graph, -1)
    (inner_rotated,) = call(
        pre_kernel, [arr((TRUNC, CH, LANES), bf16)],
        [frames1, padded, scr((COEF, CH, LANES), f32), scr((TRUNC, CH, LANES), bf16), pltpu.SemaphoreType.DMA],
        [node, table, edge_source, edge_bin], 10**9, "pre", far_outs=1,
    )
    core = lax.axis_index("core").reshape(1)
    half = arr((PACKED // 2, LANES), bf16)
    conv_grad, message, keep, send = call(
        conv_kernel, [edges16, edges32, half, half],
        [scr((TRUNC, CH, WIDE), bf16), scr((TRUNC, CH, WIDE), f32), scr((2, PACKED // 2, LANES), bf16),
         scr((TRUNC, CH, WIDE), f32), scr((TRUNC, CH, WIDE), bf16), frames2, padded, scr((COEF, CH, WIDE), f32),
         pltpu.SemaphoreType.DMA((2,))],
        [core, from_lower, from_upper, cot, table, edge_target, edge_bin, in_targets, in_bins] + weights
        + [edge_scale, in_scale, inner_rotated], 10**10, "conv", scalars=1, hbm=1, far_outs=1,
    )

    pieces = lax.axis_size(PLANE)
    (joint,) = call(join_kernel, [half], [], [keep, swap_cores(send)], 10**6, "join")
    joint = joint.reshape(pieces, -1, LANES)
    piece = joint.shape[1:]
    parts = to_all(joint, PLANE)
    back_lower, back_upper, inner = call(
        input_kernel, [packed_shape, packed_shape, arr((TRUNC, CH, LANES), bf16)], [scr((TRUNC, CH, WIDE), bf16)],
        [conv_grad] + weights + [joint], 10**10, "inputs", far=1,
    )
    back_zero = from_behind(back_upper, graph, 1)
    back_one = from_behind(back_lower, graph, -1)
    updated, token = call(
        update_kernel, [arr((COEF, CH, LANES), bf16), mark],
        [frames2, padded, scr((COEF, CH, WIDE), bf16)],
        [node, table, message, edge_bin, edge_target, in_bins, in_targets, inner], 10**10, "update", far=1,
    )
    feature_grad, token = call(
        back_kernel, [arr((COEF, CH, LANES), f32), mark],
        [frames2, frames1, padded, scr((TRUNC, SUB, WIDE), bf16), scr((COEF, SUB, WIDE), bf16),
         scr((COEF, CH, LANES), bf16)],
        [back_zero, back_one, inner, table, out_bins, out_atoms, edge_bin, edge_source, cot, token], 10**10,
        "back", far=1,
    )
    layers = lax.axis_size("z")
    (copies,) = call(add_kernel, [arr((layers,) + piece, bf16)], [], [parts, token], 10**7, "add_plane", far=1)
    sums = to_all(copies, "z")
    (copies,) = call(add_kernel, [arr((pieces,) + piece, bf16)], [], [sums, token], 10**7, "add_z", far=1)
    mine = to_all(copies, PLANE)
    other = swap_cores(mine)
    grads = []
    for swapped, value in enumerate((mine, other)):
        grads = call(
            functools.partial(unpack_kernel, pieces, swapped), [arr(w.shape, f32) for w in weights],
            [scr(w.shape, f32) for w in weights] + [pltpu.SemaphoreType.DMA((3,))],
            [core, value.reshape(half.shape)] + list(grads), 10**7, "unpack", scalars=1, hbm=len(grads),
            far_outs=3, aliases={2 + index: index for index in range(len(grads))},
        )
    grad_zero, grad_one, grad_two = grads
    return updated[None], feature_grad[None], grad_zero, grad_one, grad_two


def solution(mesh):
    cores, rows, columns = SPLIT
    graph = mesh.shape["graph"]
    fine = jax.sharding.Mesh(mesh.devices.reshape(graph // cores, cores, rows, columns), ("z", "core", "x", "y"))
    dp, along = PLANE, ("z", "core")
    nodes, edges = P(dp, None, None, along), P(dp, along)
    in_specs = (nodes, nodes) + (P(),) * 4 + (edges,) * 4 + (P(dp, along, None),) * 5
    return jax.shard_map(
        body, mesh=fine, in_specs=in_specs, out_specs=(nodes, nodes, P(), P(), P()), check_vma=False
    )
```

time: 127 us -> 117 us (0.921)
  Pallas kernels: 34.1 us -> 22.3 us
  waiting for transfers between devices: 4.08 us -> 9.07 us
  starting transfers between devices: 38.5 us -> 34.4 us
  blocking collectives: 43.6 us -> 46.6 us
  other arithmetic: 1.45 us -> 0 us
    all_to_all x1 -> x2, blocking collectives: 16.4 us -> 46.6 us  [to_all(): return lax.all_to_all(copies, axes, 0, 0)]
    all_to_all x1 -> x0, blocking collectives: 27.3 us -> none  [reduce_all(): lax.all_to_all(joint.reshape(pieces, -1, LANES), plane, 0, 0)]
    pallas_call x7 -> x11, Pallas kernels: 34.1 us -> 22.3 us  [call(): pl.pallas_call(kernel, out_shape=tuple(outs), in_specs=[scalar] * scalars...]
    all_to_all x1, waiting for transfers between devices: 2.06 us -> 6.13 us  [to_all(): return lax.all_to_all(copies, axes, 0, 0)]
    ppermute x4, starting transfers between devices: 14.3 us -> 11.3 us  [from_behind(): lax.ppermute(value, axis, [(source, (source + steps) % count) for source...]
    all_to_all x1, starting transfers between devices: 11.4 us -> 9.67 us  [to_all(): return lax.all_to_all(copies, axes, 0, 0)]
    convert_element_type x1 -> x0, other arithmetic: 1.3 us -> none  [reduce_all(): joint = (keep.astype(f32) + swap_cores(send).astype(f32)).astype(bf16)]
  transfers between devices with their start and end apart: 7 -> 7, of which waited for: 2 -> 4; matrix products, arithmetic and copies ran while one was open for 0% -> 0% of each run, Pallas kernels for 17% -> 10%
where the time goes in v2:
time: 117 us; the launch traced here: 116 us
  blocking collectives  46.6 us (40%)
  starting transfers between devices  34.4 us (29%)
  Pallas kernels  22.3 us (19%)
  waiting for transfers between devices  9.07 us (8%)
  local copies, waits for them, and re-layouts  2.3 us (2%)
    all_to_all x2, blocking collectives, to_all(): return lax.all_to_all(copies, axes, 0, 0)  46.6 us
    pallas_call x11, Pallas kernels, call(): pl.pallas_call(kernel, out_shape=tuple(outs), in_specs=[scalar] * scalars...  22.3 us
    ppermute x2, starting transfers between devices, swap_cores(): return lax.ppermute(value, 'core', [(0, 1), (1, 0)])  13.5 us
    ppermute x4, starting transfers between devices, from_behind(): lax.ppermute(value, axis, [(source, (source + steps) % count) for source...  11.3 us
    all_to_all x1, starting transfers between devices, to_all(): return lax.all_to_all(copies, axes, 0, 0)  9.67 us
    all_to_all x1, waiting for transfers between devices, to_all(): return lax.all_to_all(copies, axes, 0, 0)  6.13 us
    ppermute x2, waiting for transfers between devices, swap_cores(): return lax.ppermute(value, 'core', [(0, 1), (1, 0)])  2.36 us
  transfers between devices with their start and end apart: 7, of which 4 were waited for; matrix products, arithmetic and copies ran while one was open for 0% of the time, Pallas kernels for 10%

profile of v2, /device:TPU:1, one launch (start us, length us, event | category | flops | bytes accessed | tf_op | source)
XLA Modules:
  0.0 115.6 jit_solution(11757836095801917455)
XLA Ops:
  0.7 3.1 %rim.1 = (bf16[29,16,128]{2,1,0:T(8,128)(2,1)S(1)}, bf16[29,16,128]{2,1,0:T(8,128)(2,1)}) custom-call(bf16[49,64,128]{2,1,0:T(8,128)(2,1)} %bitcast.16, bf16[49,29,128]{2,1,0:T(8,128)(2,1)} %bitcast.21, s32[2,32]{1,0:T(2,128)} %bitcast.31, s32[2,32]{1,0:T(2,128)} %bitcast.33), custom_call_target="tpu_custom_call" | custom-call | flops 1000000000 | bytes 1404672 | tf_op jit(solution)/shard_map/rim/pallas_call | solution.py:359
  3.8 3.5 %collective-permute-start = (bf16[29,16,128]{2,1,0:T(8,128)(2,1)}, bf16[29,16,128]{2,1,0:T(8,128)(2,1)S(1)}, u32[]{:S(2)}, u32[]{:S(2)}) collective-permute-start(bf16[29,16,128]{2,1,0:T(8,128)(2,1)} %get-tuple-element.24), channel_id=1, source_target_pairs={{0,32},{32,64},{64,96},{96,128},{128,160},{160,192},{192,224},{224... | collective-permute-start | bytes 356360 | tf_op jit(solution)/shard_map/ppermute | solution.py:382
  7.3 7.1 %collective-permute-start.1 = (bf16[29,16,128]{2,1,0:T(8,128)(2,1)S(1)}, bf16[29,16,128]{2,1,0:T(8,128)(2,1)S(1)}, u32[]{:S(2)}, u32[]{:S(2)}) collective-permute-start(bf16[29,16,128]{2,1,0:T(8,128)(2,1)S(1)} %get-tuple-element.25), channel_id=1, source_target_pairs={{0,736},{32,0},{64,32},{96,64},{128,96},{160,128},{192,160},{224,1... | collective-permute-start | bytes 356360 | tf_op jit(solution)/shard_map/ppermute | solution.py:382
  14.4 0.0 copy-start.1
  14.4 0.0 copy-start.2
  14.4 0.0 copy-start.8
  14.4 0.0 copy-start.9
  14.5 0.0 copy-start.14
  14.5 1.8 %pre.1.inner_rotated = bf16[29,64,128]{2,1,0:T(8,128)(2,1)} custom-call(bf16[49,64,128]{2,1,0:T(8,128)(2,1)S(1)} %bitcast.17, bf16[49,29,128]{2,1,0:T(8,128)(2,1)S(1)} %bitcast.22, s32[1,128]{1,0:T(1,128)S(1)} %copy-done.16, s32[1,128]{1,0:T(1,128)S(1)} %copy-done.15), custom_call_target="tpu_custom_call" | custom-call | flops 1000000000 | bytes 1642752 | tf_op jit(solution)/shard_map/pre/pallas_call | solution.py:359
  16.4 5.5 %conv.1 = (bf16[29,64,256]{2,1,0:T(8,128)(2,1)}, f32[29,64,256]{2,1,0:T(8,128)S(1)}, bf16[2816,128]{1,0:T(8,128)(2,1)S(1)}, bf16[2816,128]{1,0:T(8,128)(2,1)S(1)}) custom-call(s32[1]{0:T(128)} %bitcast.2.core.which, bf16[29,16,128]{2,1,0:T(8,128)(2,1)S(1)} %collective-permute-done.from_lower, bf16[29,16,128]{2,1,0:T(8,128)(2,1)S(1)} %collective-permute-done.1.from_upper, ...), custom_call_target="tpu_custom_call" | custom-call | flops 10000000000 | bytes 7575044 | tf_op jit(solution)/shard_map/conv/pallas_call | solution.py:359
  21.9 5.7 %collective-permute-start.2 = (bf16[2816,128]{1,0:T(8,128)(2,1)S(1)}, bf16[2816,128]{1,0:T(8,128)(2,1)S(1)}, u32[]{:S(2)}, u32[]{:S(2)}) collective-permute-start(bf16[2816,128]{1,0:T(8,128)(2,1)S(1)} %get-tuple-element.29), channel_id=1, source_target_pairs={{0,32},{32,0},{1,33},{33,1},{2,34},{34,2},{3,35},{35,3},{4,36},{36... | collective-permute-start | bytes 2162696 | tf_op jit(solution)/shard_map/ppermute | solution.py:386
  27.7 1.8 %collective-permute-done.2.other = bf16[2816,128]{1,0:T(8,128)(2,1)S(1)} collective-permute-done((bf16[2816,128]{1,0:T(8,128)(2,1)S(1)}, bf16[2816,128]{1,0:T(8,128)(2,1)S(1)}, u32[]{:S(2)}, u32[]{:S(2)}) %collective-permute-start.2) | collective-permute-done | bytes 720928 | tf_op jit(solution)/shard_map/ppermute | solution.py:386
  29.4 1.0 join.1
  30.5 9.7 %all-to-all-start = ((bf16[32,88,128]{2,1,0:T(8,128)(2,1)}), bf16[32,88,128]{2,1,0:T(8,128)(2,1)S(1)}, u32[]{:S(2)}, u32[]{:S(2)}) async-start(bf16[32,88,128]{2,1,0:T(8,128)(2,1)} %bitcast.9.after), calls=%async_computation | async-start | bytes 1441792 | tf_op jit(solution)/shard_map/all_to_all | solution.py:390
  40.2 0.0 copy-start.5
  40.2 1.0 copy-done.5
  41.2 1.2 %copy-done.19 = bf16[29,64,256]{2,1,0:T(8,128)(2,1)S(1)} copy-done((bf16[29,64,256]{2,1,0:T(8,128)(2,1)S(1)}, bf16[29,64,256]{2,1,0:T(8,128)(2,1)}, u32[]{:S(2)}) %copy-start.19) | copy-done | bytes 950296
  42.4 1.4 %inputs.1 = (bf16[29,16,128]{2,1,0:T(8,128)(2,1)S(1)}, bf16[29,16,128]{2,1,0:T(8,128)(2,1)S(1)}, bf16[29,64,128]{2,1,0:T(8,128)(2,1)S(1)}) custom-call(bf16[29,64,256]{2,1,0:T(8,128)(2,1)S(1)} %copy-done.19, bf16[448,448]{1,0:T(8,128)(2,1)S(1)} %copy-done.5, bf16[2,384,384]{2,1,0:T(8,128)(2,1)S(1)} %copy-done.2, bf16[2,320,320]{2,1,0:T(8,128)(2,1)S(1)} %copy-done.3, ...), custom_call_target="tpu_custom_call" | custom-call | flops 10000000000 | bytes 3784704 | tf_op jit(solution)/shard_map/inputs/pallas_call | solution.py:359
  43.8 0.0 collective-permute-start.3
  43.8 0.7 collective-permute-start.4
  44.5 3.3 %update.1 = (bf16[49,64,128]{2,1,0:T(8,128)(2,1)}, f32[8,128]{1,0:T(8,128)S(1)}) custom-call(bf16[49,64,128]{2,1,0:T(8,128)(2,1)S(1)} %bitcast.18, bf16[49,29,128]{2,1,0:T(8,128)(2,1)S(1)} %bitcast.24, f32[29,64,256]{2,1,0:T(8,128)S(1)} %copy-done.18, s32[1,128]{1,0:T(1,128)S(1)} %copy-done.15, s32[1,128]{1,0:T(1,128)S(1)} %copy-done.14, ...), custom_call_target="tpu_custom_call" | custom-call | flops 10000000000 | bytes 4350720 | tf_op jit(solution)/shard_map/update/pallas_call | solution.py:359
  47.8 0.6 collective-permute-done.4.back_one
  48.4 3.5 %back.1 = (f32[49,64,128]{2,1,0:T(8,128)}, f32[8,128]{1,0:T(8,128)S(1)}) custom-call(bf16[29,16,128]{2,1,0:T(8,128)(2,1)S(1)} %collective-permute-done.3.back_zero, bf16[29,16,128]{2,1,0:T(8,128)(2,1)S(1)} %collective-permute-done.4.back_one, bf16[29,64,128]{2,1,0:T(8,128)(2,1)S(1)} %get-tuple-element.30.after.inner, bf16[49,29,128]{2,1,0:T(8,128)(2,1)S(1)} %bitcast.25, ...), custom_call_target="tpu_custom_call" | custom-call | flops 10000000000 | bytes 3494656 | tf_op jit(solution)/shard_map/back/pallas_call | solution.py:359
  51.8 6.1 %all-to-all-done.pieces = bf16[32,88,128]{2,1,0:T(8,128)(2,1)S(1)} async-done(((bf16[32,88,128]{2,1,0:T(8,128)(2,1)}), bf16[32,88,128]{2,1,0:T(8,128)(2,1)S(1)}, u32[]{:S(2)}, u32[]{:S(2)}) %all-to-all-start) | async-done | bytes 720928 | tf_op jit(solution)/shard_map/all_to_all | solution.py:390
  58.0 0.1 add_plane.1
  58.1 19.1 %all_to_all.15.pieces = bf16[12,88,128]{2,1,0:T(8,128)(2,1)S(1)} all-to-all(bf16[12,88,128]{2,1,0:T(8,128)(2,1)S(1)} %add_plane.1), channel_id=1, replica_groups=mesh['z'=12,'core'=2,'x'=4,'y'=8] {'z'}, dimensions={0} | all-to-all | bytes 540672 | tf_op jit(solution)/shard_map/all_to_all | solution.py:390
  77.2 0.1 add_z.1
  77.2 27.5 %all_to_all.16 = bf16[32,88,128]{2,1,0:T(8,128)(2,1)S(1)} all-to-all(bf16[32,88,128]{2,1,0:T(8,128)(2,1)S(1)} %add_z.1), channel_id=1, replica_groups=mesh['z'=12,'core'=2,'x'=4,'y'=8] {'x','y'}, dimensions={0} | all-to-all | bytes 1441792 | tf_op jit(solution)/shard_map/all_to_all | solution.py:390
  104.7 7.8 %collective-permute-start.5 = (bf16[32,88,128]{2,1,0:T(8,128)(2,1)S(1)}, bf16[32,88,128]{2,1,0:T(8,128)(2,1)S(1)}, u32[]{:S(2)}, u32[]{:S(2)}) collective-permute-start(bf16[32,88,128]{2,1,0:T(8,128)(2,1)S(1)} %all_to_all.16), channel_id=1, source_target_pairs={{0,32},{32,0},{1,33},{33,1},{2,34},{34,2},{3,35},{35,3},{4,36},{36... | collective-permute-start | bytes 2162696 | tf_op jit(solution)/shard_map/ppermute | solution.py:386
  112.5 1.2 %unpack.2 = (f32[448,448]{1,0:T(8,128)}, f32[2,384,384]{2,1,0:T(8,128)}, f32[2,320,320]{2,1,0:T(8,128)}) custom-call(s32[1]{0:T(128)} %bitcast.2.core.which, bf16[2816,128]{1,0:T(8,128)(2,1)S(1)} %bitcast.14), custom_call_target="tpu_custom_call" | custom-call | flops 10000000 | bytes 3522564 | tf_op jit(solution)/shard_map/unpack/pallas_call | solution.py:359
  113.8 0.6 collective-permute-done.5
  114.3 1.3 %unpack.3 = (f32[448,448]{1,0:T(8,128)}, f32[2,384,384]{2,1,0:T(8,128)}, f32[2,320,320]{2,1,0:T(8,128)}) custom-call(s32[1]{0:T(128)} %bitcast.2.core.which, bf16[2816,128]{1,0:T(8,128)(2,1)S(1)} %bitcast.15, f32[448,448]{1,0:T(8,128)} %get-tuple-element.37.refs_0_, ...), custom_call_target="tpu_custom_call", output_to_operand_aliasing={{0}: (2, {}), {1}: (3, {}), {2}: (4, {})} | custom-call | flops 10000000 | bytes 6324228 | tf_op jit(solution)/shard_map/unpack/pallas_call | solution.py:359
  (35 shorter events, 0.1 us)
Async XLA Ops:
  0.6 13.7 %copy-start = (bf16[1,49,64,128]{3,2,1,0:T(8,128)(2,1)S(1)}, bf16[1,49,64,128]{3,2,1,0:T(8,128)(2,1)}, u32[]{:S(2)}) copy-start(bf16[1,49,64,128]{3,2,1,0:T(8,128)(2,1)} %param.15) | copy-start | bytes 2408452
  0.6 13.7 %copy-start.6 = (bf16[128,29,49]{0,1,2:T(8,128)(2,1)S(1)}, bf16[128,29,49]{0,1,2:T(8,128)(2,1)}, u32[]{:S(2)}) copy-start(bf16[128,29,49]{0,1,2:T(8,128)(2,1)} %param.17) | copy-start | bytes 1091332
  0.7 13.7 %copy-start.15 = (s32[1,128]{1,0:T(1,128)S(1)}, s32[1,128]{1,0:T(1,128)}, u32[]{:S(2)}) copy-start(s32[1,128]{1,0:T(1,128)} %bins.7) | copy-start | bytes 1540
  0.7 13.7 %copy-start.16 = (s32[1,128]{1,0:T(1,128)S(1)}, s32[1,128]{1,0:T(1,128)}, u32[]{:S(2)}) copy-start(s32[1,128]{1,0:T(1,128)} %sources.3) | copy-start | bytes 1540
  3.8 12.5 %collective-permute-start = (bf16[29,16,128]{2,1,0:T(8,128)(2,1)}, bf16[29,16,128]{2,1,0:T(8,128)(2,1)S(1)}, u32[]{:S(2)}, u32[]{:S(2)}) collective-permute-start(bf16[29,16,128]{2,1,0:T(8,128)(2,1)} %get-tuple-element.24), channel_id=1, source_target_pairs={{0,32},{32,64},{64,96},{96,128},{128,160},{160,192},{192,224},{224... | collective-permute-start | bytes 356360 | tf_op jit(solution)/shard_map/ppermute | solution.py:382
  7.3 9.0 %collective-permute-start.1 = (bf16[29,16,128]{2,1,0:T(8,128)(2,1)S(1)}, bf16[29,16,128]{2,1,0:T(8,128)(2,1)S(1)}, u32[]{:S(2)}, u32[]{:S(2)}) collective-permute-start(bf16[29,16,128]{2,1,0:T(8,128)(2,1)S(1)} %get-tuple-element.25), channel_id=1, source_target_pairs={{0,736},{32,0},{64,32},{96,64},{128,96},{160,128},{192,160},{224,1... | collective-permute-start | bytes 356360 | tf_op jit(solution)/shard_map/ppermute | solution.py:382
  14.4 2.0 %copy-start.1 = (bf16[1,49,64,128]{3,2,1,0:T(8,128)(2,1)S(1)}, bf16[1,49,64,128]{3,2,1,0:T(8,128)(2,1)}, u32[]{:S(2)}) copy-start(bf16[1,49,64,128]{3,2,1,0:T(8,128)(2,1)} %param.16) | copy-start | bytes 2408452
  14.4 2.0 %copy-start.2 = (bf16[2,384,384]{2,1,0:T(8,128)(2,1)S(1)}, bf16[2,384,384]{2,1,0:T(8,128)(2,1)}, u32[]{:S(2)}) copy-start(bf16[2,384,384]{2,1,0:T(8,128)(2,1)} %w_one.3) | copy-start | bytes 1769476
  14.4 2.0 %copy-start.3 = (bf16[2,320,320]{2,1,0:T(8,128)(2,1)S(1)}, bf16[2,320,320]{2,1,0:T(8,128)(2,1)}, u32[]{:S(2)}) copy-start(bf16[2,320,320]{2,1,0:T(8,128)(2,1)} %w_two.3) | copy-start | bytes 1228804
  14.4 2.0 %copy-start.4 = (bf16[448,448]{1,0:T(8,128)(2,1)S(1)}, bf16[448,448]{1,0:T(8,128)(2,1)}, u32[]{:S(2)}) copy-start(bf16[448,448]{1,0:T(8,128)(2,1)} %w_zero.3) | copy-start | bytes 1204228
  14.4 1.9 %copy-start.8 = (f32[1,2,32]{2,1,0:T(2,128)S(1)}, f32[1,2,32]{2,1,0:T(2,128)}, u32[]{:S(2)}) copy-start(f32[1,2,32]{2,1,0:T(2,128)} %param.29) | copy-start | bytes 772
  14.4 1.9 %copy-start.9 = (s32[1,2,32]{2,1,0:T(2,128)S(1)}, s32[1,2,32]{2,1,0:T(2,128)}, u32[]{:S(2)}) copy-start(s32[1,2,32]{2,1,0:T(2,128)} %param.27) | copy-start | bytes 772
  14.4 1.9 %copy-start.10 = (s32[1,2,32]{2,1,0:T(2,128)S(1)}, s32[1,2,32]{2,1,0:T(2,128)}, u32[]{:S(2)}) copy-start(s32[1,2,32]{2,1,0:T(2,128)} %param.28) | copy-start | bytes 772
  14.5 1.9 %copy-start.13 = (f32[1,128]{1,0:T(1,128)S(1)}, f32[1,128]{1,0:T(1,128)}, u32[]{:S(2)}) copy-start(f32[1,128]{1,0:T(1,128)} %scale.1) | copy-start | bytes 1540
  14.5 1.9 %copy-start.14 = (s32[1,128]{1,0:T(1,128)S(1)}, s32[1,128]{1,0:T(1,128)}, u32[]{:S(2)}) copy-start(s32[1,128]{1,0:T(1,128)} %targets.3) | copy-start | bytes 1540
  21.9 8.6 %copy-start.17 = (f32[29,64,256]{2,1,0:T(8,128)}, f32[29,64,256]{2,1,0:T(8,128)S(1)}, u32[]{:S(2)}) copy-start(f32[29,64,256]{2,1,0:T(8,128)S(1)} %get-tuple-element.26.message) | copy-start | bytes 5701636
  21.9 7.5 %collective-permute-start.2 = (bf16[2816,128]{1,0:T(8,128)(2,1)S(1)}, bf16[2816,128]{1,0:T(8,128)(2,1)S(1)}, u32[]{:S(2)}, u32[]{:S(2)}) collective-permute-start(bf16[2816,128]{1,0:T(8,128)(2,1)S(1)} %get-tuple-element.29), channel_id=1, source_target_pairs={{0,32},{32,0},{1,33},{33,1},{2,34},{34,2},{3,35},{35,3},{4,36},{36... | collective-permute-start | bytes 2162696 | tf_op jit(solution)/shard_map/ppermute | solution.py:386
  30.5 27.5 %all-to-all-start = ((bf16[32,88,128]{2,1,0:T(8,128)(2,1)}), bf16[32,88,128]{2,1,0:T(8,128)(2,1)S(1)}, u32[]{:S(2)}, u32[]{:S(2)}) async-start(bf16[32,88,128]{2,1,0:T(8,128)(2,1)} %bitcast.9.after), calls=%async_computation | async-start | bytes 1441792 | tf_op jit(solution)/shard_map/all_to_all | solution.py:390
  40.2 1.0 copy-start.5
  41.2 1.2 %copy-start.19 = (bf16[29,64,256]{2,1,0:T(8,128)(2,1)S(1)}, bf16[29,64,256]{2,1,0:T(8,128)(2,1)}, u32[]{:S(2)}) copy-start(bf16[29,64,256]{2,1,0:T(8,128)(2,1)} %get-tuple-element.27.conv_grad) | copy-start | bytes 2850820
  42.4 2.1 %copy-start.7 = (bf16[128,29,49]{0,1,2:T(8,128)(2,1)S(1)}, bf16[128,29,49]{0,1,2:T(8,128)(2,1)}, u32[]{:S(2)}) copy-start(bf16[128,29,49]{0,1,2:T(8,128)(2,1)} %param.17) | copy-start | bytes 1091332
  42.4 2.1 %copy-start.18 = (f32[29,64,256]{2,1,0:T(8,128)S(1)}, f32[29,64,256]{2,1,0:T(8,128)}, u32[]{:S(2)}) copy-start(f32[29,64,256]{2,1,0:T(8,128)} %copy-done.17) | copy-start | bytes 5701636
  43.8 4.0 %collective-permute-start.3 = (bf16[29,16,128]{2,1,0:T(8,128)(2,1)S(1)}, bf16[29,16,128]{2,1,0:T(8,128)(2,1)S(1)}, u32[]{:S(2)}, u32[]{:S(2)}) collective-permute-start(bf16[29,16,128]{2,1,0:T(8,128)(2,1)S(1)} %get-tuple-element.32), channel_id=1, source_target_pairs={{0,32},{32,64},{64,96},{96,128},{128,160},{160,192},{192,224},{224... | collective-permute-start | bytes 356360 | tf_op jit(solution)/shard_map/ppermute | solution.py:382
  43.8 4.6 %collective-permute-start.4 = (bf16[29,16,128]{2,1,0:T(8,128)(2,1)S(1)}, bf16[29,16,128]{2,1,0:T(8,128)(2,1)S(1)}, u32[]{:S(2)}, u32[]{:S(2)}) collective-permute-start(bf16[29,16,128]{2,1,0:T(8,128)(2,1)S(1)} %get-tuple-element.33), channel_id=1, source_target_pairs={{0,736},{32,0},{64,32},{96,64},{128,96},{160,128},{192,160},{224,1... | collective-permute-start | bytes 356360 | tf_op jit(solution)/shard_map/ppermute | solution.py:382
  44.5 3.9 %copy-start.11 = (s32[1,2,32]{2,1,0:T(2,128)S(1)}, s32[1,2,32]{2,1,0:T(2,128)}, u32[]{:S(2)}) copy-start(s32[1,2,32]{2,1,0:T(2,128)} %param.25) | copy-start | bytes 772
  44.5 3.9 %copy-start.12 = (s32[1,2,32]{2,1,0:T(2,128)S(1)}, s32[1,2,32]{2,1,0:T(2,128)}, u32[]{:S(2)}) copy-start(s32[1,2,32]{2,1,0:T(2,128)} %param.26) | copy-start | bytes 772
  104.7 9.6 %collective-permute-start.5 = (bf16[32,88,128]{2,1,0:T(8,128)(2,1)S(1)}, bf16[32,88,128]{2,1,0:T(8,128)(2,1)S(1)}, u32[]{:S(2)}, u32[]{:S(2)}) collective-permute-start(bf16[32,88,128]{2,1,0:T(8,128)(2,1)S(1)} %all_to_all.16), channel_id=1, source_target_pairs={{0,32},{32,0},{1,33},{33,1},{2,34},{34,2},{3,35},{35,3},{4,36},{36... | collective-permute-start | bytes 2162696 | tf_op jit(solution)/shard_map/ppermute | solution.py:386

commit v3 on v2

--- a/solution.py
+++ b/solution.py
@@ -107,8 +107,8 @@
 
 
 def rim_kernel(
-    node_far, wigner_far, atoms_far, bins_far, to_lower, to_upper,
-    frames, padded, gathered, rotated, node, wigner, atoms, bins, sems,
+    core, node_far, wigner_far, atoms_far, bins_far, to_lower, to_upper, node, wigner,
+    frames, padded, gathered, rotated, atoms, bins, sems,
 ):
     pairs = [(wigner_far, wigner), (bins_far, bins), (atoms_far, atoms), (node_far, node)]
     copies = [pltpu.make_async_copy(far, near, sems.at[index]) for index, (far, near) in enumerate(pairs)]
@@ -132,13 +132,18 @@
     to_upper[...] = rotated[:, :, LANES:wide]
 
 
-def pre_kernel(node, wigner, sources, bins, rotated_far, frames, padded, values, rotated, sem):
-    load_frames(frames, padded, wigner, bins[...])
-    values[...] = dot(flat(node[...]), one_hot(sources[...])).reshape(COEF, CH, LANES)
-    rotate_into(frames, values, rotated, 32)
-    copy = pltpu.make_async_copy(rotated, rotated_far, sem)
-    copy.start()
-    copy.wait()
+def pre_kernel(
+    node, cot, wigner, sources, targets, bins, halo_targets, halo_bins,
+    rotated, message_grad, frames, padded, values,
+):
+    joint_bins = jnp.concatenate([bins[...], halo_row(halo_bins[...], -1)], axis=1)
+    joint_targets = jnp.concatenate([targets[...], halo_row(halo_targets[...], -1)], axis=1)
+    load_frames(frames, padded, wigner, joint_bins)
+    inner = slice(0, LANES)
+    values[:, :, inner] = dot(flat(node[...]), one_hot(sources[...])).reshape(COEF, CH, LANES)
+    rotate_into(frames.at[:, :, inner], values.at[:, :, inner], rotated, 32)
+    values[...] = dot(flat(cot[...]), one_hot(joint_targets, 0.5)).reshape(COEF, CH, WIDE)
+    rotate_into(frames, values, message_grad, 16)
 
 
 def rows_of(values, first, last):
@@ -183,25 +188,17 @@
 
 
 def conv_kernel(
-    core, from_lower, from_upper, cot, wigner, targets, bins, halo_targets, halo_bins, w_zero, w_one, w_two,
-    scale, halo_scale, inner_rotated,
+    core, from_lower, from_upper, inner_rotated, message_grad, w_zero, w_one, w_two, scale, halo_scale,
     conv_grad_far, message, keep, send,
-    rotated, conv, packed, message_grad, conv_grad, frames, padded, values, sems,
-):
-    get_rotated = pltpu.make_async_copy(inner_rotated, rotated.at[:, :, 0:LANES], sems.at[0])
-    get_rotated.start()
-    joint_bins = jnp.concatenate([bins[...], halo_row(halo_bins[...], -1)], axis=1)
-    joint_targets = jnp.concatenate([targets[...], halo_row(halo_targets[...], -1)], axis=1)
-    load_frames(frames, padded, wigner, joint_bins)
-    values[...] = dot(flat(cot[...]), one_hot(joint_targets, 0.5)).reshape(COEF, CH, WIDE)
-    rotate_into(frames, values, message_grad, 16)
+    rotated, conv, packed, conv_grad, sem,
+):
+    rotated[:, :, 0:LANES] = inner_rotated[...]
     left = jnp.concatenate([flat(from_lower[...]), flat(from_upper[...])], axis=1)
     spread = dot(left, spread_table()).astype(bf16)
     for g in range(GROUPS):
         rotated[:, g * SUB : (g + 1) * SUB, LANES:WIDE] = spread[:, g * LANES : (g + 1) * LANES].reshape(
             TRUNC, SUB, LANES
         )
-    get_rotated.wait()
     conv_forward(rotated, conv, w_zero, w_one, w_two)
     weight = jnp.concatenate([scale[...], halo_row(halo_scale[...], 0.0)], axis=1)
     gating = jax.nn.sigmoid(conv[0])
@@ -215,7 +212,7 @@
         message[row] = value * factor
     conv_grad[0] = (message_grad[0] * factor + factor_grad * weight * gating * (1.0 - gating)).astype(bf16)
     message[0] = conv[0] * factor
-    put = pltpu.make_async_copy(conv_grad, conv_grad_far, sems.at[1])
+    put = pltpu.make_async_copy(conv_grad, conv_grad_far, sem)
     put.start()
 
     zero = dot_nt(rows_of(conv_grad, ZERO, ZERO), rows_of(rotated, ZERO, ZERO))
@@ -411,29 +408,28 @@
     padded = scr((COEF, PAD_ROWS, LANES), bf16)
     mark = arr((8, LANES), f32)
 
-    to_lower, to_upper = call(
-        rim_kernel, [packed_shape] * 2,
+    core = lax.axis_index("core").reshape(1)
+    to_lower, to_upper, near_node, near_table = call(
+        rim_kernel, [packed_shape] * 2 + [arr(node.shape, bf16), arr(table.shape, bf16)],
         [frames2, padded, scr((COEF, SUB, WIDE), f32), scr((TRUNC, SUB, WIDE), bf16),
-         scr(node.shape, bf16), scr(table.shape, bf16), scr(out_atoms.shape, jnp.int32),
+         scr(out_atoms.shape, jnp.int32),
          scr(out_bins.shape, jnp.int32), pltpu.SemaphoreType.DMA((4,))],
-        [node, table, out_atoms, out_bins], 10**9, "rim", hbm=4,
+        [core, node, table, out_atoms, out_bins], 10**9, "rim", scalars=1, hbm=4,
     )
     from_lower = from_behind(to_upper, graph, 1)
     from_upper = from_behind(to_lower, graph, -1)
-    (inner_rotated,) = call(
-        pre_kernel, [arr((TRUNC, CH, LANES), bf16)],
-        [frames1, padded, scr((COEF, CH, LANES), f32), scr((TRUNC, CH, LANES), bf16), pltpu.SemaphoreType.DMA],
-        [node, table, edge_source, edge_bin], 10**9, "pre", far_outs=1,
-    )
-    core = lax.axis_index("core").reshape(1)
+    inner_rotated, message_grad = call(
+        pre_kernel, [arr((TRUNC, CH, LANES), bf16), edges32],
+        [frames2, padded, scr((COEF, CH, WIDE), f32)],
+        [near_node, cot, near_table, edge_source, edge_target, edge_bin, in_targets, in_bins], 10**10, "pre",
+    )
     half = arr((PACKED // 2, LANES), bf16)
     conv_grad, message, keep, send = call(
         conv_kernel, [edges16, edges32, half, half],
         [scr((TRUNC, CH, WIDE), bf16), scr((TRUNC, CH, WIDE), f32), scr((2, PACKED // 2, LANES), bf16),
-         scr((TRUNC, CH, WIDE), f32), scr((TRUNC, CH, WIDE), bf16), frames2, padded, scr((COEF, CH, WIDE), f32),
-         pltpu.SemaphoreType.DMA((2,))],
-        [core, from_lower, from_upper, cot, table, edge_target, edge_bin, in_targets, in_bins] + weights
-        + [edge_scale, in_scale, inner_rotated], 10**10, "conv", scalars=1, hbm=1, far_outs=1,
+         scr((TRUNC, CH, WIDE), bf16), pltpu.SemaphoreType.DMA],
+        [core, from_lower, from_upper, inner_rotated, message_grad] + weights + [edge_scale, in_scale],
+        10**10, "conv", scalars=1, far_outs=1,
     )
 
     pieces = lax.axis_size(PLANE)

time: 117 us -> 113 us (0.966)
  Pallas kernels: 22.3 us -> 20.7 us
    pallas_call x11, Pallas kernels: 22.3 us -> 20.7 us  [call(): pl.pallas_call(kernel, out_shape=tuple(outs), in_specs=[scalar] * scalars...]
  transfers between devices with their start and end apart: 7 -> 7, of which waited for: 4 -> 4; matrix products, arithmetic and copies ran while one was open for 0% -> 0% of each run, Pallas kernels for 10% -> 12%
where the time goes in v3:
time: 113 us; the launch traced here: 112 us
  blocking collectives  45.5 us (40%)
  starting transfers between devices  33.7 us (30%)
  Pallas kernels  20.7 us (18%)
  waiting for transfers between devices  10 us (9%)
  local copies, waits for them, and re-layouts  1.27 us (1%)
    all_to_all x2, blocking collectives, to_all(): return lax.all_to_all(copies, axes, 0, 0)  45.5 us
    pallas_call x11, Pallas kernels, call(): pl.pallas_call(kernel, out_shape=tuple(outs), in_specs=[scalar] * scalars...  20.7 us
    ppermute x2, starting transfers between devices, swap_cores(): return lax.ppermute(value, 'core', [(0, 1), (1, 0)])  12.8 us
    ppermute x4, starting transfers between devices, from_behind(): lax.ppermute(value, axis, [(source, (source + steps) % count) for source...  11.3 us
    all_to_all x1, starting transfers between devices, to_all(): return lax.all_to_all(copies, axes, 0, 0)  9.67 us
    all_to_all x1, waiting for transfers between devices, to_all(): return lax.all_to_all(copies, axes, 0, 0)  7.13 us
    ppermute x2, waiting for transfers between devices, swap_cores(): return lax.ppermute(value, 'core', [(0, 1), (1, 0)])  2.36 us
  transfers between devices with their start and end apart: 7, of which 4 were waited for; matrix products, arithmetic and copies ran while one was open for 0% of the time, Pallas kernels for 12%

profile of v3, /device:TPU:1, one launch (start us, length us, event | category | flops | bytes accessed | tf_op | source)
XLA Modules:
  0.0 112.1 jit_solution(14798328500924642479)
XLA Ops:
  0.7 2.5 %rim.1 = (bf16[29,16,128]{2,1,0:T(8,128)(2,1)S(1)}, bf16[29,16,128]{2,1,0:T(8,128)(2,1)S(1)}, bf16[49,64,128]{2,1,0:T(8,128)(2,1)S(1)}, bf16[49,29,128]{2,1,0:T(8,128)(2,1)S(1)}) custom-call(s32[1]{0:T(128)} %bitcast.2.core.which, bf16[49,64,128]{2,1,0:T(8,128)(2,1)} %bitcast.16, bf16[49,29,128]{2,1,0:T(8,128)(2,1)} %bitcast.20, s32[2,32]{1,0:T(2,128)} %bitcast.28, ...), custom_call_target="tpu_custom_call" | custom-call | flops 1000000000 | bytes 2571268 | tf_op jit(solution)/shard_map/rim/pallas_call | solution.py:356
  3.2 3.5 %collective-permute-start = (bf16[29,16,128]{2,1,0:T(8,128)(2,1)S(1)}, bf16[29,16,128]{2,1,0:T(8,128)(2,1)S(1)}, u32[]{:S(2)}, u32[]{:S(2)}) collective-permute-start(bf16[29,16,128]{2,1,0:T(8,128)(2,1)S(1)} %get-tuple-element.28), channel_id=1, source_target_pairs={{0,32},{32,64},{64,96},{96,128},{128,160},{160,192},{192,224},{224... | collective-permute-start | bytes 356360 | tf_op jit(solution)/shard_map/ppermute | solution.py:379
  6.7 7.1 %collective-permute-start.1 = (bf16[29,16,128]{2,1,0:T(8,128)(2,1)S(1)}, bf16[29,16,128]{2,1,0:T(8,128)(2,1)S(1)}, u32[]{:S(2)}, u32[]{:S(2)}) collective-permute-start(bf16[29,16,128]{2,1,0:T(8,128)(2,1)S(1)} %get-tuple-element.29), channel_id=1, source_target_pairs={{0,736},{32,0},{64,32},{96,64},{128,96},{160,128},{192,160},{224,1... | collective-permute-start | bytes 356360 | tf_op jit(solution)/shard_map/ppermute | solution.py:379
  13.8 0.0 copy-start.2
  13.8 0.0 copy-start.3
  13.8 0.0 copy-start.4
  13.8 0.0 copy-start.6
  13.8 0.0 copy-start.11
  13.8 3.7 %pre.1 = (bf16[29,64,128]{2,1,0:T(8,128)(2,1)S(1)}, f32[29,64,256]{2,1,0:T(8,128)S(1)}) custom-call(bf16[49,64,128]{2,1,0:T(8,128)(2,1)S(1)} %get-tuple-element.30.node, bf16[49,64,128]{2,1,0:T(8,128)(2,1)S(1)} %bitcast.18, bf16[49,29,128]{2,1,0:T(8,128)(2,1)S(1)} %get-tuple-element.31.wigner, s32[1,128]{1,0:T(1,128)S(1)} %copy-done.13, ...), custom_call_target="tpu_custom_call" | custom-call | flops 10000000000 | bytes 4347136 | tf_op jit(solution)/shard_map/pre/pallas_call | solution.py:356
  17.6 2.7 %conv.1 = (bf16[29,64,256]{2,1,0:T(8,128)(2,1)}, f32[29,64,256]{2,1,0:T(8,128)S(1)}, bf16[2816,128]{1,0:T(8,128)(2,1)S(1)}, bf16[2816,128]{1,0:T(8,128)(2,1)S(1)}) custom-call(s32[1]{0:T(128)} %bitcast.2.core.which, bf16[29,16,128]{2,1,0:T(8,128)(2,1)S(1)} %collective-permute-done.from_lower, bf16[29,16,128]{2,1,0:T(8,128)(2,1)S(1)} %collective-permute-done.1.from_upper, ...), custom_call_target="tpu_custom_call" | custom-call | flops 10000000000 | bytes 8307460 | tf_op jit(solution)/shard_map/conv/pallas_call | solution.py:356
  20.3 5.0 %collective-permute-start.2 = (bf16[2816,128]{1,0:T(8,128)(2,1)S(1)}, bf16[2816,128]{1,0:T(8,128)(2,1)S(1)}, u32[]{:S(2)}, u32[]{:S(2)}) collective-permute-start(bf16[2816,128]{1,0:T(8,128)(2,1)S(1)} %get-tuple-element.37), channel_id=1, source_target_pairs={{0,32},{32,0},{1,33},{33,1},{2,34},{34,2},{3,35},{35,3},{4,36},{36... | collective-permute-start | bytes 2162696 | tf_op jit(solution)/shard_map/ppermute | solution.py:383
  25.3 1.8 %collective-permute-done.2.other = bf16[2816,128]{1,0:T(8,128)(2,1)S(1)} collective-permute-done((bf16[2816,128]{1,0:T(8,128)(2,1)S(1)}, bf16[2816,128]{1,0:T(8,128)(2,1)S(1)}, u32[]{:S(2)}, u32[]{:S(2)}) %collective-permute-start.2) | collective-permute-done | bytes 720928 | tf_op jit(solution)/shard_map/ppermute | solution.py:383
  27.1 1.0 join.1
  28.1 9.7 %all-to-all-start = ((bf16[32,88,128]{2,1,0:T(8,128)(2,1)}), bf16[32,88,128]{2,1,0:T(8,128)(2,1)S(1)}, u32[]{:S(2)}, u32[]{:S(2)}) async-start(bf16[32,88,128]{2,1,0:T(8,128)(2,1)} %bitcast.9.after), calls=%async_computation | async-start | bytes 1441792 | tf_op jit(solution)/shard_map/all_to_all | solution.py:387
  37.8 0.0 copy-start.17
  37.8 1.2 %copy-done.17 = bf16[29,64,256]{2,1,0:T(8,128)(2,1)S(1)} copy-done((bf16[29,64,256]{2,1,0:T(8,128)(2,1)S(1)}, bf16[29,64,256]{2,1,0:T(8,128)(2,1)}, u32[]{:S(2)}) %copy-start.17) | copy-done | bytes 950296
  39.0 1.4 %inputs.1 = (bf16[29,16,128]{2,1,0:T(8,128)(2,1)S(1)}, bf16[29,16,128]{2,1,0:T(8,128)(2,1)S(1)}, bf16[29,64,128]{2,1,0:T(8,128)(2,1)S(1)}) custom-call(bf16[29,64,256]{2,1,0:T(8,128)(2,1)S(1)} %copy-done.17, bf16[448,448]{1,0:T(8,128)(2,1)S(1)} %copy-done.4, bf16[2,384,384]{2,1,0:T(8,128)(2,1)S(1)} %copy-done.2, bf16[2,320,320]{2,1,0:T(8,128)(2,1)S(1)} %copy-done.3, ...), custom_call_target="tpu_custom_call" | custom-call | flops 10000000000 | bytes 3784704 | tf_op jit(solution)/shard_map/inputs/pallas_call | solution.py:356
  40.4 0.0 collective-permute-start.3
  40.4 0.7 collective-permute-start.4
  41.1 0.0 copy-start.10
  41.1 3.3 %update.1 = (bf16[49,64,128]{2,1,0:T(8,128)(2,1)}, f32[8,128]{1,0:T(8,128)S(1)}) custom-call(bf16[49,64,128]{2,1,0:T(8,128)(2,1)S(1)} %bitcast.17, bf16[49,29,128]{2,1,0:T(8,128)(2,1)S(1)} %bitcast.21, f32[29,64,256]{2,1,0:T(8,128)S(1)} %copy-done.16, s32[1,128]{1,0:T(1,128)S(1)} %copy-done.14, s32[1,128]{1,0:T(1,128)S(1)} %copy-done.12, ...), custom_call_target="tpu_custom_call" | custom-call | flops 10000000000 | bytes 4350720 | tf_op jit(solution)/shard_map/update/pallas_call | solution.py:356
  44.5 0.5 collective-permute-done.4.back_one
  45.0 3.5 %back.1 = (f32[49,64,128]{2,1,0:T(8,128)}, f32[8,128]{1,0:T(8,128)S(1)}) custom-call(bf16[29,16,128]{2,1,0:T(8,128)(2,1)S(1)} %collective-permute-done.3.back_zero, bf16[29,16,128]{2,1,0:T(8,128)(2,1)S(1)} %collective-permute-done.4.back_one, bf16[29,64,128]{2,1,0:T(8,128)(2,1)S(1)} %get-tuple-element.38.after.inner, bf16[49,29,128]{2,1,0:T(8,128)(2,1)S(1)} %bitcast.22, ...), custom_call_target="tpu_custom_call" | custom-call | flops 10000000000 | bytes 3494656 | tf_op jit(solution)/shard_map/back/pallas_call | solution.py:356
  48.5 7.1 %all-to-all-done.pieces = bf16[32,88,128]{2,1,0:T(8,128)(2,1)S(1)} async-done(((bf16[32,88,128]{2,1,0:T(8,128)(2,1)}), bf16[32,88,128]{2,1,0:T(8,128)(2,1)S(1)}, u32[]{:S(2)}, u32[]{:S(2)}) %all-to-all-start) | async-done | bytes 720928 | tf_op jit(solution)/shard_map/all_to_all | solution.py:387
  55.6 0.1 add_plane.1
  55.7 18.0 %all_to_all.15.pieces = bf16[12,88,128]{2,1,0:T(8,128)(2,1)S(1)} all-to-all(bf16[12,88,128]{2,1,0:T(8,128)(2,1)S(1)} %add_plane.1), channel_id=1, replica_groups=mesh['z'=12,'core'=2,'x'=4,'y'=8] {'z'}, dimensions={0} | all-to-all | bytes 540672 | tf_op jit(solution)/shard_map/all_to_all | solution.py:387
  73.7 0.1 add_z.1
  73.7 27.5 %all_to_all.16 = bf16[32,88,128]{2,1,0:T(8,128)(2,1)S(1)} all-to-all(bf16[32,88,128]{2,1,0:T(8,128)(2,1)S(1)} %add_z.1), channel_id=1, replica_groups=mesh['z'=12,'core'=2,'x'=4,'y'=8] {'x','y'}, dimensions={0} | all-to-all | bytes 1441792 | tf_op jit(solution)/shard_map/all_to_all | solution.py:387
  101.2 7.8 %collective-permute-start.5 = (bf16[32,88,128]{2,1,0:T(8,128)(2,1)S(1)}, bf16[32,88,128]{2,1,0:T(8,128)(2,1)S(1)}, u32[]{:S(2)}, u32[]{:S(2)}) collective-permute-start(bf16[32,88,128]{2,1,0:T(8,128)(2,1)S(1)} %all_to_all.16), channel_id=1, source_target_pairs={{0,32},{32,0},{1,33},{33,1},{2,34},{34,2},{3,35},{35,3},{4,36},{36... | collective-permute-start | bytes 2162696 | tf_op jit(solution)/shard_map/ppermute | solution.py:383
  109.0 1.2 %unpack.2 = (f32[448,448]{1,0:T(8,128)}, f32[2,384,384]{2,1,0:T(8,128)}, f32[2,320,320]{2,1,0:T(8,128)}) custom-call(s32[1]{0:T(128)} %bitcast.2.core.which, bf16[2816,128]{1,0:T(8,128)(2,1)S(1)} %bitcast.14), custom_call_target="tpu_custom_call" | custom-call | flops 10000000 | bytes 3522564 | tf_op jit(solution)/shard_map/unpack/pallas_call | solution.py:356
  110.3 0.6 collective-permute-done.5
  110.8 1.3 %unpack.3 = (f32[448,448]{1,0:T(8,128)}, f32[2,384,384]{2,1,0:T(8,128)}, f32[2,320,320]{2,1,0:T(8,128)}) custom-call(s32[1]{0:T(128)} %bitcast.2.core.which, bf16[2816,128]{1,0:T(8,128)(2,1)S(1)} %bitcast.15, f32[448,448]{1,0:T(8,128)} %get-tuple-element.45.refs_0_, ...), custom_call_target="tpu_custom_call", output_to_operand_aliasing={{0}: (2, {}), {1}: (3, {}), {2}: (4, {})} | custom-call | flops 10000000 | bytes 6324228 | tf_op jit(solution)/shard_map/unpack/pallas_call | solution.py:356
  (31 shorter events, 0.1 us)
Async XLA Ops:
  0.6 13.1 %copy-start.1 = (bf16[1,49,64,128]{3,2,1,0:T(8,128)(2,1)S(1)}, bf16[1,49,64,128]{3,2,1,0:T(8,128)(2,1)}, u32[]{:S(2)}) copy-start(bf16[1,49,64,128]{3,2,1,0:T(8,128)(2,1)} %param.16) | copy-start | bytes 2408452
  0.6 13.1 %copy-start.7 = (s32[1,2,32]{2,1,0:T(2,128)S(1)}, s32[1,2,32]{2,1,0:T(2,128)}, u32[]{:S(2)}) copy-start(s32[1,2,32]{2,1,0:T(2,128)} %param.27) | copy-start | bytes 772
  0.7 13.1 %copy-start.8 = (s32[1,2,32]{2,1,0:T(2,128)S(1)}, s32[1,2,32]{2,1,0:T(2,128)}, u32[]{:S(2)}) copy-start(s32[1,2,32]{2,1,0:T(2,128)} %param.28) | copy-start | bytes 772
  0.7 13.1 %copy-start.12 = (s32[1,128]{1,0:T(1,128)S(1)}, s32[1,128]{1,0:T(1,128)}, u32[]{:S(2)}) copy-start(s32[1,128]{1,0:T(1,128)} %targets.3) | copy-start | bytes 1540
  0.7 13.1 %copy-start.13 = (s32[1,128]{1,0:T(1,128)S(1)}, s32[1,128]{1,0:T(1,128)}, u32[]{:S(2)}) copy-start(s32[1,128]{1,0:T(1,128)} %sources.3) | copy-start | bytes 1540
  0.7 13.1 %copy-start.14 = (s32[1,128]{1,0:T(1,128)S(1)}, s32[1,128]{1,0:T(1,128)}, u32[]{:S(2)}) copy-start(s32[1,128]{1,0:T(1,128)} %bins.5) | copy-start | bytes 1540
  3.2 14.4 %collective-permute-start = (bf16[29,16,128]{2,1,0:T(8,128)(2,1)S(1)}, bf16[29,16,128]{2,1,0:T(8,128)(2,1)S(1)}, u32[]{:S(2)}, u32[]{:S(2)}) collective-permute-start(bf16[29,16,128]{2,1,0:T(8,128)(2,1)S(1)} %get-tuple-element.28), channel_id=1, source_target_pairs={{0,32},{32,64},{64,96},{96,128},{128,160},{160,192},{192,224},{224... | collective-permute-start | bytes 356360 | tf_op jit(solution)/shard_map/ppermute | solution.py:379
  6.7 10.9 %collective-permute-start.1 = (bf16[29,16,128]{2,1,0:T(8,128)(2,1)S(1)}, bf16[29,16,128]{2,1,0:T(8,128)(2,1)S(1)}, u32[]{:S(2)}, u32[]{:S(2)}) collective-permute-start(bf16[29,16,128]{2,1,0:T(8,128)(2,1)S(1)} %get-tuple-element.29), channel_id=1, source_target_pairs={{0,736},{32,0},{64,32},{96,64},{128,96},{160,128},{192,160},{224,1... | collective-permute-start | bytes 356360 | tf_op jit(solution)/shard_map/ppermute | solution.py:379
  13.8 3.8 %copy-start.2 = (bf16[2,384,384]{2,1,0:T(8,128)(2,1)S(1)}, bf16[2,384,384]{2,1,0:T(8,128)(2,1)}, u32[]{:S(2)}) copy-start(bf16[2,384,384]{2,1,0:T(8,128)(2,1)} %w_one.3) | copy-start | bytes 1769476
  13.8 3.8 %copy-start.3 = (bf16[2,320,320]{2,1,0:T(8,128)(2,1)S(1)}, bf16[2,320,320]{2,1,0:T(8,128)(2,1)}, u32[]{:S(2)}) copy-start(bf16[2,320,320]{2,1,0:T(8,128)(2,1)} %w_two.3) | copy-start | bytes 1228804
  13.8 3.8 %copy-start.4 = (bf16[448,448]{1,0:T(8,128)(2,1)S(1)}, bf16[448,448]{1,0:T(8,128)(2,1)}, u32[]{:S(2)}) copy-start(bf16[448,448]{1,0:T(8,128)(2,1)} %w_zero.3) | copy-start | bytes 1204228
  13.8 3.8 %copy-start.6 = (f32[1,2,32]{2,1,0:T(2,128)S(1)}, f32[1,2,32]{2,1,0:T(2,128)}, u32[]{:S(2)}) copy-start(f32[1,2,32]{2,1,0:T(2,128)} %param.29) | copy-start | bytes 772
  13.8 3.8 %copy-start.11 = (f32[1,128]{1,0:T(1,128)S(1)}, f32[1,128]{1,0:T(1,128)}, u32[]{:S(2)}) copy-start(f32[1,128]{1,0:T(1,128)} %scale.1) | copy-start | bytes 1540
  20.3 7.9 %copy-start.15 = (f32[29,64,256]{2,1,0:T(8,128)}, f32[29,64,256]{2,1,0:T(8,128)S(1)}, u32[]{:S(2)}) copy-start(f32[29,64,256]{2,1,0:T(8,128)S(1)} %get-tuple-element.34.message) | copy-start | bytes 5701636
  20.3 6.8 %collective-permute-start.2 = (bf16[2816,128]{1,0:T(8,128)(2,1)S(1)}, bf16[2816,128]{1,0:T(8,128)(2,1)S(1)}, u32[]{:S(2)}, u32[]{:S(2)}) collective-permute-start(bf16[2816,128]{1,0:T(8,128)(2,1)S(1)} %get-tuple-element.37), channel_id=1, source_target_pairs={{0,32},{32,0},{1,33},{33,1},{2,34},{34,2},{3,35},{35,3},{4,36},{36... | collective-permute-start | bytes 2162696 | tf_op jit(solution)/shard_map/ppermute | solution.py:383
  28.1 27.5 %all-to-all-start = ((bf16[32,88,128]{2,1,0:T(8,128)(2,1)}), bf16[32,88,128]{2,1,0:T(8,128)(2,1)S(1)}, u32[]{:S(2)}, u32[]{:S(2)}) async-start(bf16[32,88,128]{2,1,0:T(8,128)(2,1)} %bitcast.9.after), calls=%async_computation | async-start | bytes 1441792 | tf_op jit(solution)/shard_map/all_to_all | solution.py:387
  37.8 1.2 %copy-start.17 = (bf16[29,64,256]{2,1,0:T(8,128)(2,1)S(1)}, bf16[29,64,256]{2,1,0:T(8,128)(2,1)}, u32[]{:S(2)}) copy-start(bf16[29,64,256]{2,1,0:T(8,128)(2,1)} %get-tuple-element.35.conv_grad) | copy-start | bytes 2850820
  39.0 2.1 %copy-start = (bf16[1,49,64,128]{3,2,1,0:T(8,128)(2,1)S(1)}, bf16[1,49,64,128]{3,2,1,0:T(8,128)(2,1)}, u32[]{:S(2)}) copy-start(bf16[1,49,64,128]{3,2,1,0:T(8,128)(2,1)} %param.15) | copy-start | bytes 2408452
  39.0 2.1 %copy-start.5 = (bf16[128,29,49]{0,1,2:T(8,128)(2,1)S(1)}, bf16[128,29,49]{0,1,2:T(8,128)(2,1)}, u32[]{:S(2)}) copy-start(bf16[128,29,49]{0,1,2:T(8,128)(2,1)} %param.17) | copy-start | bytes 1091332
  39.0 2.1 %copy-start.16 = (f32[29,64,256]{2,1,0:T(8,128)S(1)}, f32[29,64,256]{2,1,0:T(8,128)}, u32[]{:S(2)}) copy-start(f32[29,64,256]{2,1,0:T(8,128)} %copy-done.15) | copy-start | bytes 5701636
  40.4 4.1 %collective-permute-start.3 = (bf16[29,16,128]{2,1,0:T(8,128)(2,1)S(1)}, bf16[29,16,128]{2,1,0:T(8,128)(2,1)S(1)}, u32[]{:S(2)}, u32[]{:S(2)}) collective-permute-start(bf16[29,16,128]{2,1,0:T(8,128)(2,1)S(1)} %get-tuple-element.40), channel_id=1, source_target_pairs={{0,32},{32,64},{64,96},{96,128},{128,160},{160,192},{192,224},{224... | collective-permute-start | bytes 356360 | tf_op jit(solution)/shard_map/ppermute | solution.py:379
  40.4 4.6 %collective-permute-start.4 = (bf16[29,16,128]{2,1,0:T(8,128)(2,1)S(1)}, bf16[29,16,128]{2,1,0:T(8,128)(2,1)S(1)}, u32[]{:S(2)}, u32[]{:S(2)}) collective-permute-start(bf16[29,16,128]{2,1,0:T(8,128)(2,1)S(1)} %get-tuple-element.41), channel_id=1, source_target_pairs={{0,736},{32,0},{64,32},{96,64},{128,96},{160,128},{192,160},{224,1... | collective-permute-start | bytes 356360 | tf_op jit(solution)/shard_map/ppermute | solution.py:379
  41.1 3.9 %copy-start.9 = (s32[1,2,32]{2,1,0:T(2,128)S(1)}, s32[1,2,32]{2,1,0:T(2,128)}, u32[]{:S(2)}) copy-start(s32[1,2,32]{2,1,0:T(2,128)} %param.25) | copy-start | bytes 772
  41.1 3.9 %copy-start.10 = (s32[1,2,32]{2,1,0:T(2,128)S(1)}, s32[1,2,32]{2,1,0:T(2,128)}, u32[]{:S(2)}) copy-start(s32[1,2,32]{2,1,0:T(2,128)} %param.26) | copy-start | bytes 772
  101.2 9.6 %collective-permute-start.5 = (bf16[32,88,128]{2,1,0:T(8,128)(2,1)S(1)}, bf16[32,88,128]{2,1,0:T(8,128)(2,1)S(1)}, u32[]{:S(2)}, u32[]{:S(2)}) collective-permute-start(bf16[32,88,128]{2,1,0:T(8,128)(2,1)S(1)} %all_to_all.16), channel_id=1, source_target_pairs={{0,32},{32,0},{1,33},{33,1},{2,34},{34,2},{3,35},{35,3},{4,36},{36... | collective-permute-start | bytes 2162696 | tf_op jit(solution)/shard_map/ppermute | solution.py:383

commit v4 on v3

--- a/solution.py
+++ b/solution.py
@@ -107,7 +107,7 @@
 
 
 def rim_kernel(
-    core, node_far, wigner_far, atoms_far, bins_far, to_lower, to_upper, node, wigner,
+    core, node_far, wigner_far, atoms_far, bins_far, outer, inner, node, wigner,
     frames, padded, gathered, rotated, atoms, bins, sems,
 ):
     pairs = [(wigner_far, wigner), (bins_far, bins), (atoms_far, atoms), (node_far, node)]
@@ -128,8 +128,8 @@
     )
     gathered[...] = dot(left, table).reshape(COEF, SUB, wide)
     rotate_into(frames, gathered, rotated, SUB)
-    to_lower[...] = rotated[:, :, 0:LANES]
-    to_upper[...] = rotated[:, :, LANES:wide]
+    outer[...] = rotated[:, :, pl.ds(pl.multiple_of(core[0] * LANES, LANES), LANES)]
+    inner[...] = rotated[:, :, pl.ds(pl.multiple_of((1 - core[0]) * LANES, LANES), LANES)]
 
 
 def pre_kernel(
@@ -139,11 +139,13 @@
     joint_bins = jnp.concatenate([bins[...], halo_row(halo_bins[...], -1)], axis=1)
     joint_targets = jnp.concatenate([targets[...], halo_row(halo_targets[...], -1)], axis=1)
     load_frames(frames, padded, wigner, joint_bins)
-    inner = slice(0, LANES)
+    inner, halo = slice(0, LANES), slice(LANES, WIDE)
     values[:, :, inner] = dot(flat(node[...]), one_hot(sources[...])).reshape(COEF, CH, LANES)
-    rotate_into(frames.at[:, :, inner], values.at[:, :, inner], rotated, 32)
-    values[...] = dot(flat(cot[...]), one_hot(joint_targets, 0.5)).reshape(COEF, CH, WIDE)
-    rotate_into(frames, values, message_grad, 16)
+    rotate_into(frames.at[:, :, inner], values.at[:, :, inner], rotated, CH)
+    table = one_hot(joint_targets, 0.5)
+    for part in (inner, halo):
+        values[:, :, part] = dot(flat(cot[...]), table[:, part]).reshape(COEF, CH, LANES)
+        rotate_into(frames.at[:, :, part], values.at[:, :, part], message_grad.at[:, :, part], CH)
 
 
 def rows_of(values, first, last):
@@ -188,12 +190,14 @@
 
 
 def conv_kernel(
-    core, from_lower, from_upper, inner_rotated, message_grad, w_zero, w_one, w_two, scale, halo_scale,
-    conv_grad_far, message, keep, send,
-    rotated, conv, packed, conv_grad, sem,
+    core, outer, inner, inner_rotated, message_grad, w_zero, w_one, w_two, scale, halo_scale,
+    conv_grad, message, keep, send,
+    rotated, conv, packed, halo,
 ):
     rotated[:, :, 0:LANES] = inner_rotated[...]
-    left = jnp.concatenate([flat(from_lower[...]), flat(from_upper[...])], axis=1)
+    halo[core[0]] = flat(outer[...])
+    halo[1 - core[0]] = flat(inner[...])
+    left = jnp.concatenate([halo[0], halo[1]], axis=1)
     spread = dot(left, spread_table()).astype(bf16)
     for g in range(GROUPS):
         rotated[:, g * SUB : (g + 1) * SUB, LANES:WIDE] = spread[:, g * LANES : (g + 1) * LANES].reshape(
@@ -212,8 +216,6 @@
         message[row] = value * factor
     conv_grad[0] = (message_grad[0] * factor + factor_grad * weight * gating * (1.0 - gating)).astype(bf16)
     message[0] = conv[0] * factor
-    put = pltpu.make_async_copy(conv_grad, conv_grad_far, sem)
-    put.start()
 
     zero = dot_nt(rows_of(conv_grad, ZERO, ZERO), rows_of(rotated, ZERO, ZERO))
     pairs = []
@@ -229,7 +231,6 @@
     pack_grads(packed.at[1], [one[1]] + two)
     keep[...] = packed[core[0]]
     send[...] = packed[1 - core[0]]
-    put.wait()
 
 
 def input_kernel(conv_grad, w_zero, w_one, w_two, after, to_lower, to_upper, inner, joint):
@@ -304,8 +305,29 @@
             total[index] = found
 
 
-def join_kernel(keep, other, joint):
-    joint[...] = (keep[...].astype(f32) + other[...].astype(f32)).astype(bf16)
+def leave_kernel(conv_grad, message, conv_grad_far, message_far, token, sems):
+    puts = [
+        pltpu.make_async_copy(conv_grad, conv_grad_far, sems.at[0]),
+        pltpu.make_async_copy(message, message_far, sems.at[1]),
+    ]
+    for put in puts:
+        put.start()
+    token[...] = jnp.zeros(token.shape, token.dtype)
+    for put in puts:
+        put.wait()
+
+
+def join_kernel(keep, other, after, joint_far, joint, sems):
+    count = sems.shape[0]
+    rows = joint.shape[0] // count
+    copies = []
+    for index in range(count):
+        part = slice(index * rows, (index + 1) * rows)
+        joint[part, :] = (keep[part, :].astype(f32) + other[part, :].astype(f32)).astype(bf16)
+        copies.append(pltpu.make_async_copy(joint.at[part, :], joint_far.at[part, :], sems.at[index]))
+        copies[-1].start()
+    for copy in copies:
+        copy.wait()
 
 
 def unpack_kernel(replicas, swapped, which, packed, *refs):
@@ -379,6 +401,14 @@
     return lax.ppermute(value, axis, [(source, (source + steps) % count) for source in range(count)])
 
 
+def across_chips(value):
+    chips = lax.axis_size("z")
+    pairs = []
+    for chip in range(chips):
+        pairs += [(2 * chip, (2 * chip - 1) % (2 * chips)), (2 * chip + 1, (2 * chip + 2) % (2 * chips))]
+    return lax.ppermute(value, ("z", "core"), pairs)
+
+
 def swap_cores(value):
     return lax.ppermute(value, "core", [(0, 1), (1, 0)])
 
@@ -409,15 +439,14 @@
     mark = arr((8, LANES), f32)
 
     core = lax.axis_index("core").reshape(1)
-    to_lower, to_upper, near_node, near_table = call(
+    outer, inner, near_node, near_table = call(
         rim_kernel, [packed_shape] * 2 + [arr(node.shape, bf16), arr(table.shape, bf16)],
         [frames2, padded, scr((COEF, SUB, WIDE), f32), scr((TRUNC, SUB, WIDE), bf16),
          scr(out_atoms.shape, jnp.int32),
          scr(out_bins.shape, jnp.int32), pltpu.SemaphoreType.DMA((4,))],
         [core, node, table, out_atoms, out_bins], 10**9, "rim", scalars=1, hbm=4,
     )
-    from_lower = from_behind(to_upper, graph, 1)
-    from_upper = from_behind(to_lower, graph, -1)
+    outer, inner = across_chips(outer), swap_cores(inner)
     inner_rotated, message_grad = call(
         pre_kernel, [arr((TRUNC, CH, LANES), bf16), edges32],
         [frames2, padded, scr((COEF, CH, WIDE), f32)],
@@ -427,13 +456,21 @@
     conv_grad, message, keep, send = call(
         conv_kernel, [edges16, edges32, half, half],
         [scr((TRUNC, CH, WIDE), bf16), scr((TRUNC, CH, WIDE), f32), scr((2, PACKED // 2, LANES), bf16),
-         scr((TRUNC, CH, WIDE), bf16), pltpu.SemaphoreType.DMA],
-        [core, from_lower, from_upper, inner_rotated, message_grad] + weights + [edge_scale, in_scale],
-        10**10, "conv", scalars=1, far_outs=1,
+         scr((2, TRUNC * SUB, LANES), bf16)],
+        [core, outer, inner, inner_rotated, message_grad] + weights + [edge_scale, in_scale],
+        10**10, "conv", scalars=1,
     )
 
     pieces = lax.axis_size(PLANE)
-    (joint,) = call(join_kernel, [half], [], [keep, swap_cores(send)], 10**6, "join")
+    other = swap_cores(send)
+    conv_grad, message, token = call(
+        leave_kernel, [edges16, edges32, mark], [pltpu.SemaphoreType.DMA((2,))], [conv_grad, message], 10**6, "leave",
+        far_outs=2,
+    )
+    (joint,) = call(
+        join_kernel, [half], [scr(half.shape, bf16), pltpu.SemaphoreType.DMA((4,))], [keep, other, token],
+        10**6, "join", far=1, far_outs=1,
+    )
     joint = joint.reshape(pieces, -1, LANES)
     piece = joint.shape[1:]
     parts = to_all(joint, PLANE)

time: 113 us -> 114 us (level)
  starting transfers between devices: 33.7 us -> 37.3 us
  blocking collectives: 45.5 us -> 43.3 us
  waiting for transfers between devices: 10 us -> 8.15 us
    ppermute x4 -> x2, starting transfers between devices: 11.3 us -> 0.52 us  [from_behind(): lax.ppermute(value, axis, [(source, (source + steps) % count) for source...]
    ppermute x2 -> x3, starting transfers between devices: 12.8 us -> 21.7 us  [swap_cores(): return lax.ppermute(value, 'core', [(0, 1), (1, 0)])]
    ppermute x0 -> x1, starting transfers between devices: none -> 5.39 us  [across_chips(): return lax.ppermute(value, ('z', 'core'), pairs)]
    all_to_all x2, blocking collectives: 45.5 us -> 43.3 us  [to_all(): return lax.all_to_all(copies, axes, 0, 0)]
    ppermute x2 -> x3, waiting for transfers between devices: 2.36 us -> 1.08 us  [swap_cores(): return lax.ppermute(value, 'core', [(0, 1), (1, 0)])]
    unnamed x36 -> x48, local copies, waits for them, and re-layouts: 1.27 us -> 2.29 us
    pallas_call x11 -> x12, Pallas kernels: 20.7 us -> 20.5 us  [call(): pl.pallas_call(kernel, out_shape=tuple(outs), in_specs=[scalar] * scalars...]
where the time goes in v4:
time: 114 us; the launch traced here: 113 us
  blocking collectives  43.3 us (38%)
  starting transfers between devices  37.3 us (33%)
  Pallas kernels  20.5 us (18%)
  waiting for transfers between devices  8.15 us (7%)
  local copies, waits for them, and re-layouts  2.29 us (2%)
    all_to_all x2, blocking collectives, to_all(): return lax.all_to_all(copies, axes, 0, 0)  43.3 us
    ppermute x3, starting transfers between devices, swap_cores(): return lax.ppermute(value, 'core', [(0, 1), (1, 0)])  21.7 us
    pallas_call x12, Pallas kernels, call(): pl.pallas_call(kernel, out_shape=tuple(outs), in_specs=[scalar] * scalars...  20.5 us
    all_to_all x1, starting transfers between devices, to_all(): return lax.all_to_all(copies, axes, 0, 0)  9.68 us
    all_to_all x1, waiting for transfers between devices, to_all(): return lax.all_to_all(copies, axes, 0, 0)  6.39 us
    ppermute x1, starting transfers between devices, across_chips(): return lax.ppermute(value, ('z', 'core'), pairs)  5.39 us
    unnamed x48, local copies, waits for them, and re-layouts  2.29 us
  transfers between devices with their start and end apart: 7, of which 4 were waited for; matrix products, arithmetic and copies ran while one was open for 0% of the time, Pallas kernels for 12%

profile of v4, /device:TPU:1, one launch (start us, length us, event | category | flops | bytes accessed | tf_op | source)
XLA Modules:
  0.0 112.6 jit_solution(12464664157834073947)
XLA Ops:
  0.6 0.0 copy-start.22
  0.7 0.0 copy-start.13
  0.7 0.0 copy-start.11
  0.7 2.5 %rim.1 = (bf16[29,16,128]{2,1,0:T(8,128)(2,1)S(1)}, bf16[29,16,128]{2,1,0:T(8,128)(2,1)S(1)}, bf16[49,64,128]{2,1,0:T(8,128)(2,1)S(1)}, bf16[49,29,128]{2,1,0:T(8,128)(2,1)S(1)}) custom-call(s32[1]{0:T(128)} %bitcast.2.core.which, bf16[49,64,128]{2,1,0:T(8,128)(2,1)} %bitcast.18, bf16[49,29,128]{2,1,0:T(8,128)(2,1)} %bitcast.22, s32[2,32]{1,0:T(2,128)} %bitcast.30, ...), custom_call_target="tpu_custom_call" | custom-call | flops 1000000000 | bytes 2571268 | tf_op jit(solution)/shard_map/rim/pallas_call | solution.py:378
  3.2 5.4 %collective-permute-start = (bf16[29,16,128]{2,1,0:T(8,128)(2,1)S(1)}, bf16[29,16,128]{2,1,0:T(8,128)(2,1)S(1)}, u32[]{:S(2)}, u32[]{:S(2)}) collective-permute-start(bf16[29,16,128]{2,1,0:T(8,128)(2,1)S(1)} %get-tuple-element.31), channel_id=1, source_target_pairs={{0,736},{32,64},{64,32},{96,128},{128,96},{160,192},{192,160},{224... | collective-permute-start | bytes 356360 | tf_op jit(solution)/shard_map/ppermute | solution.py:409
  8.6 12.0 %collective-permute-start.1 = (bf16[29,16,128]{2,1,0:T(8,128)(2,1)S(1)}, bf16[29,16,128]{2,1,0:T(8,128)(2,1)S(1)}, u32[]{:S(2)}, u32[]{:S(2)}) collective-permute-start(bf16[29,16,128]{2,1,0:T(8,128)(2,1)S(1)} %get-tuple-element.32), channel_id=1, source_target_pairs={{0,32},{32,0},{1,33},{33,1},{2,34},{34,2},{3,35},{35,3},{4,36},{36... | collective-permute-start | bytes 356360 | tf_op jit(solution)/shard_map/ppermute | solution.py:413
  20.7 0.0 copy-start.6
  20.7 0.0 copy-start.7
  20.8 2.1 %pre.1 = (bf16[29,64,128]{2,1,0:T(8,128)(2,1)S(1)}, f32[29,64,256]{2,1,0:T(8,128)S(1)}) custom-call(bf16[49,64,128]{2,1,0:T(8,128)(2,1)S(1)} %get-tuple-element.33.node, bf16[49,64,128]{2,1,0:T(8,128)(2,1)S(1)} %bitcast.20, bf16[49,29,128]{2,1,0:T(8,128)(2,1)S(1)} %get-tuple-element.34.wigner, s32[1,128]{1,0:T(1,128)S(1)} %copy-done.20, ...), custom_call_target="tpu_custom_call" | custom-call | flops 10000000000 | bytes 4347136 | tf_op jit(solution)/shard_map/pre/pallas_call | solution.py:378
  22.9 2.6 %conv.1 = (bf16[29,64,256]{2,1,0:T(8,128)(2,1)S(1)}, f32[29,64,256]{2,1,0:T(8,128)S(1)}, bf16[2816,128]{1,0:T(8,128)(2,1)S(1)}, bf16[2816,128]{1,0:T(8,128)(2,1)S(1)}) custom-call(s32[1]{0:T(128)} %bitcast.2.core.which, bf16[29,16,128]{2,1,0:T(8,128)(2,1)S(1)} %collective-permute-done.outer, bf16[29,16,128]{2,1,0:T(8,128)(2,1)S(1)} %collective-permute-done.1.inner, ...), custom_call_target="tpu_custom_call" | custom-call | flops 10000000000 | bytes 8307460 | tf_op jit(solution)/shard_map/conv/pallas_call | solution.py:378
  25.5 1.9 %collective-permute-start.2 = (bf16[2816,128]{1,0:T(8,128)(2,1)S(1)}, bf16[2816,128]{1,0:T(8,128)(2,1)S(1)}, u32[]{:S(2)}, u32[]{:S(2)}) collective-permute-start(bf16[2816,128]{1,0:T(8,128)(2,1)S(1)} %get-tuple-element.42), channel_id=1, source_target_pairs={{0,32},{32,0},{1,33},{33,1},{2,34},{34,2},{3,35},{35,3},{4,36},{36... | collective-permute-start | bytes 2162696 | tf_op jit(solution)/shard_map/ppermute | solution.py:413
  27.4 1.6 %leave.1 = (bf16[29,64,256]{2,1,0:T(8,128)(2,1)}, f32[29,64,256]{2,1,0:T(8,128)}, f32[8,128]{1,0:T(8,128)S(1)}) custom-call(bf16[29,64,256]{2,1,0:T(8,128)(2,1)S(1)} %get-tuple-element.37.conv_grad, f32[29,64,256]{2,1,0:T(8,128)S(1)} %get-tuple-element.38.message), custom_call_target="tpu_custom_call" | custom-call | flops 1000000 | bytes 5705728 | tf_op jit(solution)/shard_map/leave/pallas_call | solution.py:378
  29.1 0.5 collective-permute-done.2.other
  29.6 0.9 join.1
  30.5 9.7 %all-to-all-start = ((bf16[32,88,128]{2,1,0:T(8,128)(2,1)}), bf16[32,88,128]{2,1,0:T(8,128)(2,1)S(1)}, u32[]{:S(2)}, u32[]{:S(2)}) async-start(bf16[32,88,128]{2,1,0:T(8,128)(2,1)} %bitcast.14), calls=%async_computation | async-start | bytes 1441792 | tf_op jit(solution)/shard_map/all_to_all | solution.py:417
  40.2 1.1 %copy-done = bf16[2816,128]{1,0:T(8,128)(2,1)S(1)} copy-done((bf16[2816,128]{1,0:T(8,128)(2,1)S(1)}, bf16[2816,128]{1,0:T(8,128)(2,1)}, u32[]{:S(2)}) %copy-start) | copy-done | bytes 720920
  41.4 1.0 copy-done.8
  42.5 1.4 %inputs.1 = (bf16[29,16,128]{2,1,0:T(8,128)(2,1)S(1)}, bf16[29,16,128]{2,1,0:T(8,128)(2,1)S(1)}, bf16[29,64,128]{2,1,0:T(8,128)(2,1)S(1)}) custom-call(bf16[29,64,256]{2,1,0:T(8,128)(2,1)S(1)} %copy-done.2, bf16[448,448]{1,0:T(8,128)(2,1)S(1)} %copy-done.8, bf16[2,384,384]{2,1,0:T(8,128)(2,1)S(1)} %copy-done.5, bf16[2,320,320]{2,1,0:T(8,128)(2,1)S(1)} %copy-done.6, ...), custom_call_target="tpu_custom_call" | custom-call | flops 10000000000 | bytes 3784704 | tf_op jit(solution)/shard_map/inputs/pallas_call | solution.py:378
  43.8 0.0 collective-permute-start.3
  43.9 0.5 collective-permute-start.4
  44.4 3.3 %update.1 = (bf16[49,64,128]{2,1,0:T(8,128)(2,1)}, f32[8,128]{1,0:T(8,128)S(1)}) custom-call(bf16[49,64,128]{2,1,0:T(8,128)(2,1)S(1)} %bitcast.19, bf16[49,29,128]{2,1,0:T(8,128)(2,1)S(1)} %bitcast.23, f32[29,64,256]{2,1,0:T(8,128)S(1)} %copy-done.1, s32[1,128]{1,0:T(1,128)S(1)} %copy-done.23, s32[1,128]{1,0:T(1,128)S(1)} %copy-done.19, ...), custom_call_target="tpu_custom_call" | custom-call | flops 10000000000 | bytes 4350720 | tf_op jit(solution)/shard_map/update/pallas_call | solution.py:378
  47.8 0.7 collective-permute-done.4.back_one
  48.4 3.5 %back.1 = (f32[49,64,128]{2,1,0:T(8,128)}, f32[8,128]{1,0:T(8,128)S(1)}) custom-call(bf16[29,16,128]{2,1,0:T(8,128)(2,1)S(1)} %collective-permute-done.3.back_zero, bf16[29,16,128]{2,1,0:T(8,128)(2,1)S(1)} %collective-permute-done.4.back_one, bf16[29,64,128]{2,1,0:T(8,128)(2,1)S(1)} %get-tuple-element.44.after.inner, bf16[49,29,128]{2,1,0:T(8,128)(2,1)S(1)} %bitcast.24, ...), custom_call_target="tpu_custom_call" | custom-call | flops 10000000000 | bytes 3494656 | tf_op jit(solution)/shard_map/back/pallas_call | solution.py:378
  51.9 6.4 %all-to-all-done.pieces = bf16[32,88,128]{2,1,0:T(8,128)(2,1)S(1)} async-done(((bf16[32,88,128]{2,1,0:T(8,128)(2,1)}), bf16[32,88,128]{2,1,0:T(8,128)(2,1)S(1)}, u32[]{:S(2)}, u32[]{:S(2)}) %all-to-all-start) | async-done | bytes 720928 | tf_op jit(solution)/shard_map/all_to_all | solution.py:417
  58.3 0.1 add_plane.1
  58.4 15.5 %all_to_all.15.pieces = bf16[12,88,128]{2,1,0:T(8,128)(2,1)S(1)} all-to-all(bf16[12,88,128]{2,1,0:T(8,128)(2,1)S(1)} %add_plane.1), channel_id=1, replica_groups=mesh['z'=12,'core'=2,'x'=4,'y'=8] {'z'}, dimensions={0} | all-to-all | bytes 540672 | tf_op jit(solution)/shard_map/all_to_all | solution.py:417
  74.0 0.1 add_z.1
  74.0 27.8 %all_to_all.16 = bf16[32,88,128]{2,1,0:T(8,128)(2,1)S(1)} all-to-all(bf16[32,88,128]{2,1,0:T(8,128)(2,1)S(1)} %add_z.1), channel_id=1, replica_groups=mesh['z'=12,'core'=2,'x'=4,'y'=8] {'x','y'}, dimensions={0} | all-to-all | bytes 1441792 | tf_op jit(solution)/shard_map/all_to_all | solution.py:417
  101.8 7.7 %collective-permute-start.5 = (bf16[32,88,128]{2,1,0:T(8,128)(2,1)S(1)}, bf16[32,88,128]{2,1,0:T(8,128)(2,1)S(1)}, u32[]{:S(2)}, u32[]{:S(2)}) collective-permute-start(bf16[32,88,128]{2,1,0:T(8,128)(2,1)S(1)} %all_to_all.16), channel_id=1, source_target_pairs={{0,32},{32,0},{1,33},{33,1},{2,34},{34,2},{3,35},{35,3},{4,36},{36... | collective-permute-start | bytes 2162696 | tf_op jit(solution)/shard_map/ppermute | solution.py:413
  109.5 1.2 %unpack.2 = (f32[448,448]{1,0:T(8,128)}, f32[2,384,384]{2,1,0:T(8,128)}, f32[2,320,320]{2,1,0:T(8,128)}) custom-call(s32[1]{0:T(128)} %bitcast.2.core.which, bf16[2816,128]{1,0:T(8,128)(2,1)S(1)} %bitcast.16), custom_call_target="tpu_custom_call" | custom-call | flops 10000000 | bytes 3522564 | tf_op jit(solution)/shard_map/unpack/pallas_call | solution.py:378
  110.8 0.6 collective-permute-done.5
  111.3 1.3 %unpack.3 = (f32[448,448]{1,0:T(8,128)}, f32[2,384,384]{2,1,0:T(8,128)}, f32[2,320,320]{2,1,0:T(8,128)}) custom-call(s32[1]{0:T(128)} %bitcast.2.core.which, bf16[2816,128]{1,0:T(8,128)(2,1)S(1)} %bitcast.17, f32[448,448]{1,0:T(8,128)} %get-tuple-element.51.refs_0_, ...), custom_call_target="tpu_custom_call", output_to_operand_aliasing={{0}: (2, {}), {1}: (3, {}), {2}: (4, {})} | custom-call | flops 10000000 | bytes 6324228 | tf_op jit(solution)/shard_map/unpack/pallas_call | solution.py:378
  (44 shorter events, 0.1 us)
Async XLA Ops:
  0.6 20.0 %copy-start.22 = (s32[1,128]{1,0:T(1,128)S(1)}, s32[1,128]{1,0:T(1,128)}, u32[]{:S(2)}) copy-start(s32[1,128]{1,0:T(1,128)} %bins.5) | copy-start | bytes 1540
  0.6 20.0 %copy-start.18 = (s32[1,128]{1,0:T(1,128)S(1)}, s32[1,128]{1,0:T(1,128)}, u32[]{:S(2)}) copy-start(s32[1,128]{1,0:T(1,128)} %targets.3) | copy-start | bytes 1540
  0.7 20.0 %copy-start.20 = (s32[1,128]{1,0:T(1,128)S(1)}, s32[1,128]{1,0:T(1,128)}, u32[]{:S(2)}) copy-start(s32[1,128]{1,0:T(1,128)} %sources.3) | copy-start | bytes 1540
  0.7 20.0 %copy-start.13 = (s32[1,2,32]{2,1,0:T(2,128)S(1)}, s32[1,2,32]{2,1,0:T(2,128)}, u32[]{:S(2)}) copy-start(s32[1,2,32]{2,1,0:T(2,128)} %param.28) | copy-start | bytes 772
  0.7 20.0 %copy-start.11 = (s32[1,2,32]{2,1,0:T(2,128)S(1)}, s32[1,2,32]{2,1,0:T(2,128)}, u32[]{:S(2)}) copy-start(s32[1,2,32]{2,1,0:T(2,128)} %param.27) | copy-start | bytes 772
  0.7 20.0 %copy-start.4 = (bf16[1,49,64,128]{3,2,1,0:T(8,128)(2,1)S(1)}, bf16[1,49,64,128]{3,2,1,0:T(8,128)(2,1)}, u32[]{:S(2)}) copy-start(bf16[1,49,64,128]{3,2,1,0:T(8,128)(2,1)} %param.16) | copy-start | bytes 2408452
  3.2 19.6 %collective-permute-start = (bf16[29,16,128]{2,1,0:T(8,128)(2,1)S(1)}, bf16[29,16,128]{2,1,0:T(8,128)(2,1)S(1)}, u32[]{:S(2)}, u32[]{:S(2)}) collective-permute-start(bf16[29,16,128]{2,1,0:T(8,128)(2,1)S(1)} %get-tuple-element.31), channel_id=1, source_target_pairs={{0,736},{32,64},{64,32},{96,128},{128,96},{160,192},{192,160},{224... | collective-permute-start | bytes 356360 | tf_op jit(solution)/shard_map/ppermute | solution.py:409
  8.6 14.3 %collective-permute-start.1 = (bf16[29,16,128]{2,1,0:T(8,128)(2,1)S(1)}, bf16[29,16,128]{2,1,0:T(8,128)(2,1)S(1)}, u32[]{:S(2)}, u32[]{:S(2)}) collective-permute-start(bf16[29,16,128]{2,1,0:T(8,128)(2,1)S(1)} %get-tuple-element.32), channel_id=1, source_target_pairs={{0,32},{32,0},{1,33},{33,1},{2,34},{34,2},{3,35},{35,3},{4,36},{36... | collective-permute-start | bytes 356360 | tf_op jit(solution)/shard_map/ppermute | solution.py:413
  20.7 2.2 %copy-start.5 = (bf16[2,384,384]{2,1,0:T(8,128)(2,1)S(1)}, bf16[2,384,384]{2,1,0:T(8,128)(2,1)}, u32[]{:S(2)}) copy-start(bf16[2,384,384]{2,1,0:T(8,128)(2,1)} %w_one.3) | copy-start | bytes 1769476
  20.7 2.2 %copy-start.6 = (bf16[2,320,320]{2,1,0:T(8,128)(2,1)S(1)}, bf16[2,320,320]{2,1,0:T(8,128)(2,1)}, u32[]{:S(2)}) copy-start(bf16[2,320,320]{2,1,0:T(8,128)(2,1)} %w_two.3) | copy-start | bytes 1228804
  20.7 2.1 %copy-start.7 = (bf16[448,448]{1,0:T(8,128)(2,1)S(1)}, bf16[448,448]{1,0:T(8,128)(2,1)}, u32[]{:S(2)}) copy-start(bf16[448,448]{1,0:T(8,128)(2,1)} %w_zero.3) | copy-start | bytes 1204228
  20.7 2.1 %copy-start.10 = (f32[1,2,32]{2,1,0:T(2,128)S(1)}, f32[1,2,32]{2,1,0:T(2,128)}, u32[]{:S(2)}) copy-start(f32[1,2,32]{2,1,0:T(2,128)} %param.29) | copy-start | bytes 772
  20.7 2.1 %copy-start.17 = (f32[1,128]{1,0:T(1,128)S(1)}, f32[1,128]{1,0:T(1,128)}, u32[]{:S(2)}) copy-start(f32[1,128]{1,0:T(1,128)} %scale.1) | copy-start | bytes 1540
  25.5 4.1 %collective-permute-start.2 = (bf16[2816,128]{1,0:T(8,128)(2,1)S(1)}, bf16[2816,128]{1,0:T(8,128)(2,1)S(1)}, u32[]{:S(2)}, u32[]{:S(2)}) collective-permute-start(bf16[2816,128]{1,0:T(8,128)(2,1)S(1)} %get-tuple-element.42), channel_id=1, source_target_pairs={{0,32},{32,0},{1,33},{33,1},{2,34},{34,2},{3,35},{35,3},{4,36},{36... | collective-permute-start | bytes 2162696 | tf_op jit(solution)/shard_map/ppermute | solution.py:413
  29.1 11.2 %copy-start.2 = (bf16[29,64,256]{2,1,0:T(8,128)(2,1)S(1)}, bf16[29,64,256]{2,1,0:T(8,128)(2,1)}, u32[]{:S(2)}) copy-start(bf16[29,64,256]{2,1,0:T(8,128)(2,1)} %get-tuple-element.40.conv_grad) | copy-start | bytes 2850820
  30.5 27.8 %all-to-all-start = ((bf16[32,88,128]{2,1,0:T(8,128)(2,1)}), bf16[32,88,128]{2,1,0:T(8,128)(2,1)S(1)}, u32[]{:S(2)}, u32[]{:S(2)}) async-start(bf16[32,88,128]{2,1,0:T(8,128)(2,1)} %bitcast.14), calls=%async_computation | async-start | bytes 1441792 | tf_op jit(solution)/shard_map/all_to_all | solution.py:417
  40.2 1.1 %copy-start = (bf16[2816,128]{1,0:T(8,128)(2,1)S(1)}, bf16[2816,128]{1,0:T(8,128)(2,1)}, u32[]{:S(2)}) copy-start(bf16[2816,128]{1,0:T(8,128)(2,1)} %join.1) | copy-start | bytes 2162692
  41.4 1.0 copy-start.8
  42.4 2.0 %copy-start.1 = (f32[29,64,256]{2,1,0:T(8,128)S(1)}, f32[29,64,256]{2,1,0:T(8,128)}, u32[]{:S(2)}) copy-start(f32[29,64,256]{2,1,0:T(8,128)} %get-tuple-element.39.message) | copy-start | bytes 5701636
  42.4 2.0 %copy-start.3 = (bf16[1,49,64,128]{3,2,1,0:T(8,128)(2,1)S(1)}, bf16[1,49,64,128]{3,2,1,0:T(8,128)(2,1)}, u32[]{:S(2)}) copy-start(bf16[1,49,64,128]{3,2,1,0:T(8,128)(2,1)} %param.15) | copy-start | bytes 2408452
  42.4 2.0 %copy-start.9 = (bf16[128,29,49]{0,1,2:T(8,128)(2,1)S(1)}, bf16[128,29,49]{0,1,2:T(8,128)(2,1)}, u32[]{:S(2)}) copy-start(bf16[128,29,49]{0,1,2:T(8,128)(2,1)} %param.17) | copy-start | bytes 1091332
  42.4 2.0 %copy-start.12 = (s32[1,2,32]{2,1,0:T(2,128)S(1)}, s32[1,2,32]{2,1,0:T(2,128)}, u32[]{:S(2)}) copy-start(s32[1,2,32]{2,1,0:T(2,128)} %param.27) | copy-start | bytes 772
  42.4 2.0 %copy-start.14 = (s32[1,2,32]{2,1,0:T(2,128)S(1)}, s32[1,2,32]{2,1,0:T(2,128)}, u32[]{:S(2)}) copy-start(s32[1,2,32]{2,1,0:T(2,128)} %param.28) | copy-start | bytes 772
  42.4 2.0 %copy-start.19 = (s32[1,128]{1,0:T(1,128)S(1)}, s32[1,128]{1,0:T(1,128)}, u32[]{:S(2)}) copy-start(s32[1,128]{1,0:T(1,128)} %targets.3) | copy-start | bytes 1540
  42.4 2.0 %copy-start.23 = (s32[1,128]{1,0:T(1,128)S(1)}, s32[1,128]{1,0:T(1,128)}, u32[]{:S(2)}) copy-start(s32[1,128]{1,0:T(1,128)} %bins.5) | copy-start | bytes 1540
  43.8 3.9 %collective-permute-start.3 = (bf16[29,16,128]{2,1,0:T(8,128)(2,1)S(1)}, bf16[29,16,128]{2,1,0:T(8,128)(2,1)S(1)}, u32[]{:S(2)}, u32[]{:S(2)}) collective-permute-start(bf16[29,16,128]{2,1,0:T(8,128)(2,1)S(1)} %get-tuple-element.46), channel_id=1, source_target_pairs={{0,32},{32,64},{64,96},{96,128},{128,160},{160,192},{192,224},{224... | collective-permute-start | bytes 356360 | tf_op jit(solution)/shard_map/ppermute | solution.py:401
  43.9 4.6 %collective-permute-start.4 = (bf16[29,16,128]{2,1,0:T(8,128)(2,1)S(1)}, bf16[29,16,128]{2,1,0:T(8,128)(2,1)S(1)}, u32[]{:S(2)}, u32[]{:S(2)}) collective-permute-start(bf16[29,16,128]{2,1,0:T(8,128)(2,1)S(1)} %get-tuple-element.47), channel_id=1, source_target_pairs={{0,736},{32,0},{64,32},{96,64},{128,96},{160,128},{192,160},{224,1... | collective-permute-start | bytes 356360 | tf_op jit(solution)/shard_map/ppermute | solution.py:401
  44.4 4.0 %copy-start.15 = (s32[1,2,32]{2,1,0:T(2,128)S(1)}, s32[1,2,32]{2,1,0:T(2,128)}, u32[]{:S(2)}) copy-start(s32[1,2,32]{2,1,0:T(2,128)} %param.25) | copy-start | bytes 772
  44.4 4.0 %copy-start.16 = (s32[1,2,32]{2,1,0:T(2,128)S(1)}, s32[1,2,32]{2,1,0:T(2,128)}, u32[]{:S(2)}) copy-start(s32[1,2,32]{2,1,0:T(2,128)} %param.26) | copy-start | bytes 772
  44.4 4.0 %copy-start.21 = (s32[1,128]{1,0:T(1,128)S(1)}, s32[1,128]{1,0:T(1,128)}, u32[]{:S(2)}) copy-start(s32[1,128]{1,0:T(1,128)} %sources.3) | copy-start | bytes 1540
  101.8 9.5 %collective-permute-start.5 = (bf16[32,88,128]{2,1,0:T(8,128)(2,1)S(1)}, bf16[32,88,128]{2,1,0:T(8,128)(2,1)S(1)}, u32[]{:S(2)}, u32[]{:S(2)}) collective-permute-start(bf16[32,88,128]{2,1,0:T(8,128)(2,1)S(1)} %all_to_all.16), channel_id=1, source_target_pairs={{0,32},{32,0},{1,33},{33,1},{2,34},{34,2},{3,35},{35,3},{4,36},{36... | collective-permute-start | bytes 2162696 | tf_op jit(solution)/shard_map/ppermute | solution.py:413

commit v5 on v4

--- a/solution.py
+++ b/solution.py
@@ -132,18 +132,19 @@
     inner[...] = rotated[:, :, pl.ds(pl.multiple_of((1 - core[0]) * LANES, LANES), LANES)]
 
 
-def pre_kernel(
-    node, cot, wigner, sources, targets, bins, halo_targets, halo_bins,
-    rotated, message_grad, frames, padded, values,
-):
+def pre_kernel(node, wigner, sources, bins, inner_in, rotated, inner, frames, padded, values):
+    load_frames(frames, padded, wigner, bins[...])
+    values[...] = dot(flat(node[...]), one_hot(sources[...])).reshape(COEF, CH, LANES)
+    rotate_into(frames, values, rotated, CH)
+    inner[...] = inner_in[...]
+
+
+def cot_kernel(cot, wigner, targets, bins, halo_targets, halo_bins, after, message_grad, frames, padded, values):
     joint_bins = jnp.concatenate([bins[...], halo_row(halo_bins[...], -1)], axis=1)
     joint_targets = jnp.concatenate([targets[...], halo_row(halo_targets[...], -1)], axis=1)
     load_frames(frames, padded, wigner, joint_bins)
-    inner, halo = slice(0, LANES), slice(LANES, WIDE)
-    values[:, :, inner] = dot(flat(node[...]), one_hot(sources[...])).reshape(COEF, CH, LANES)
-    rotate_into(frames.at[:, :, inner], values.at[:, :, inner], rotated, CH)
     table = one_hot(joint_targets, 0.5)
-    for part in (inner, halo):
+    for part in (slice(0, LANES), slice(LANES, WIDE)):
         values[:, :, part] = dot(flat(cot[...]), table[:, part]).reshape(COEF, CH, LANES)
         rotate_into(frames.at[:, :, part], values.at[:, :, part], message_grad.at[:, :, part], CH)
 
@@ -446,12 +447,17 @@
          scr(out_bins.shape, jnp.int32), pltpu.SemaphoreType.DMA((4,))],
         [core, node, table, out_atoms, out_bins], 10**9, "rim", scalars=1, hbm=4,
     )
-    outer, inner = across_chips(outer), swap_cores(inner)
-    inner_rotated, message_grad = call(
-        pre_kernel, [arr((TRUNC, CH, LANES), bf16), edges32],
-        [frames2, padded, scr((COEF, CH, WIDE), f32)],
-        [near_node, cot, near_table, edge_source, edge_target, edge_bin, in_targets, in_bins], 10**10, "pre",
-    )
+    outer = across_chips(outer)
+    inner_rotated, inner = call(
+        pre_kernel, [arr((TRUNC, CH, LANES), bf16), packed_shape],
+        [frames1, padded, scr((COEF, CH, LANES), f32)],
+        [near_node, near_table, edge_source, edge_bin, inner], 10**10, "pre",
+    )
+    (message_grad,) = call(
+        cot_kernel, [edges32], [frames2, padded, scr((COEF, CH, WIDE), f32)],
+        [cot, near_table, edge_target, edge_bin, in_targets, in_bins, inner], 10**10, "cotangent", far=1,
+    )
+    inner = swap_cores(inner)
     half = arr((PACKED // 2, LANES), bf16)
     conv_grad, message, keep, send = call(
         conv_kernel, [edges16, edges32, half, half],

time: 114 us -> 114 us (level)
    pallas_call x12 -> x13, Pallas kernels: 20.5 us -> 20.9 us  [call(): pl.pallas_call(kernel, out_shape=tuple(outs), in_specs=[scalar] * scalars...]
where the time goes in v5:
time: 114 us; the launch traced here: 113 us
  blocking collectives  43.3 us (38%)
  starting transfers between devices  37.3 us (33%)
  Pallas kernels  20.9 us (18%)
  waiting for transfers between devices  8.15 us (7%)
  local copies, waits for them, and re-layouts  2.29 us (2%)
    all_to_all x2, blocking collectives, to_all(): return lax.all_to_all(copies, axes, 0, 0)  43.3 us
    ppermute x3, starting transfers between devices, swap_cores(): return lax.ppermute(value, 'core', [(0, 1), (1, 0)])  21.7 us
    pallas_call x13, Pallas kernels, call(): pl.pallas_call(kernel, out_shape=tuple(outs), in_specs=[scalar] * scalars...  20.9 us
    all_to_all x1, starting transfers between devices, to_all(): return lax.all_to_all(copies, axes, 0, 0)  9.67 us
    all_to_all x1, waiting for transfers between devices, to_all(): return lax.all_to_all(copies, axes, 0, 0)  6.39 us
    ppermute x1, starting transfers between devices, across_chips(): return lax.ppermute(value, ('z', 'core'), pairs)  5.39 us
    unnamed x48, local copies, waits for them, and re-layouts  2.29 us
  transfers between devices with their start and end apart: 7, of which 4 were waited for; matrix products, arithmetic and copies ran while one was open for 0% of the time, Pallas kernels for 12%

profile of v5, /device:TPU:1, one launch (start us, length us, event | category | flops | bytes accessed | tf_op | source)
XLA Modules:
  0.0 113.0 jit_solution(5864151248273795505)
XLA Ops:
  0.6 0.0 copy-start.22
  0.6 0.0 copy-start.20
  0.7 2.4 %rim.1 = (bf16[29,16,128]{2,1,0:T(8,128)(2,1)S(1)}, bf16[29,16,128]{2,1,0:T(8,128)(2,1)S(1)}, bf16[49,64,128]{2,1,0:T(8,128)(2,1)S(1)}, bf16[49,29,128]{2,1,0:T(8,128)(2,1)S(1)}) custom-call(s32[1]{0:T(128)} %bitcast.2.core.which, bf16[49,64,128]{2,1,0:T(8,128)(2,1)} %bitcast.18, bf16[49,29,128]{2,1,0:T(8,128)(2,1)} %bitcast.22, s32[2,32]{1,0:T(2,128)} %bitcast.30, ...), custom_call_target="tpu_custom_call" | custom-call | flops 1000000000 | bytes 2571268 | tf_op jit(solution)/shard_map/rim/pallas_call | solution.py:379
  3.1 5.4 %collective-permute-start = (bf16[29,16,128]{2,1,0:T(8,128)(2,1)S(1)}, bf16[29,16,128]{2,1,0:T(8,128)(2,1)S(1)}, u32[]{:S(2)}, u32[]{:S(2)}) collective-permute-start(bf16[29,16,128]{2,1,0:T(8,128)(2,1)S(1)} %get-tuple-element.31), channel_id=1, source_target_pairs={{0,736},{32,64},{64,32},{96,128},{128,96},{160,192},{192,160},{224... | collective-permute-start | bytes 356360 | tf_op jit(solution)/shard_map/ppermute | solution.py:410
  8.5 0.0 copy-start.11
  8.5 0.0 copy-start.13
  8.5 0.8 pre.1
  9.3 12.0 %collective-permute-start.1 = (bf16[29,16,128]{2,1,0:T(8,128)(2,1)S(1)}, bf16[29,16,128]{2,1,0:T(8,128)(2,1)S(1)}, u32[]{:S(2)}, u32[]{:S(2)}) collective-permute-start(bf16[29,16,128]{2,1,0:T(8,128)(2,1)S(1)} %get-tuple-element.35.after), channel_id=1, source_target_pairs={{0,32},{32,0},{1,33},{33,1},{2,34},{34,2},{3,35},{35,3},{4,36},{36... | collective-permute-start | bytes 356360 | tf_op jit(solution)/shard_map/ppermute | solution.py:414
  21.5 1.7 %cotangent.1.message_grad = f32[29,64,256]{2,1,0:T(8,128)S(1)} custom-call(bf16[49,64,128]{2,1,0:T(8,128)(2,1)S(1)} %bitcast.20, bf16[49,29,128]{2,1,0:T(8,128)(2,1)S(1)} %get-tuple-element.33.wigner, s32[1,128]{1,0:T(1,128)S(1)} %copy-done.18, s32[1,128]{1,0:T(1,128)S(1)} %copy-done.22, s32[2,32]{1,0:T(2,128)S(1)} %bitcast.26, s32[2,32]{1,0:T(2,128)S(1)} %bitcast.28, ...), custom_call_target="tpu_custom_call" | custom-call | flops 10000000000 | bytes 3187456 | tf_op jit(solution)/shard_map/cotangent/pallas_call | solution.py:379
  23.3 2.6 %conv.1 = (bf16[29,64,256]{2,1,0:T(8,128)(2,1)S(1)}, f32[29,64,256]{2,1,0:T(8,128)S(1)}, bf16[2816,128]{1,0:T(8,128)(2,1)S(1)}, bf16[2816,128]{1,0:T(8,128)(2,1)S(1)}) custom-call(s32[1]{0:T(128)} %bitcast.2.core.which, bf16[29,16,128]{2,1,0:T(8,128)(2,1)S(1)} %collective-permute-done.outer, bf16[29,16,128]{2,1,0:T(8,128)(2,1)S(1)} %collective-permute-done.1.inner, ...), custom_call_target="tpu_custom_call" | custom-call | flops 10000000000 | bytes 8307460 | tf_op jit(solution)/shard_map/conv/pallas_call | solution.py:379
  25.9 1.9 %collective-permute-start.2 = (bf16[2816,128]{1,0:T(8,128)(2,1)S(1)}, bf16[2816,128]{1,0:T(8,128)(2,1)S(1)}, u32[]{:S(2)}, u32[]{:S(2)}) collective-permute-start(bf16[2816,128]{1,0:T(8,128)(2,1)S(1)} %get-tuple-element.42), channel_id=1, source_target_pairs={{0,32},{32,0},{1,33},{33,1},{2,34},{34,2},{3,35},{35,3},{4,36},{36... | collective-permute-start | bytes 2162696 | tf_op jit(solution)/shard_map/ppermute | solution.py:414
  27.8 1.6 %leave.1 = (bf16[29,64,256]{2,1,0:T(8,128)(2,1)}, f32[29,64,256]{2,1,0:T(8,128)}, f32[8,128]{1,0:T(8,128)S(1)}) custom-call(bf16[29,64,256]{2,1,0:T(8,128)(2,1)S(1)} %get-tuple-element.37.conv_grad, f32[29,64,256]{2,1,0:T(8,128)S(1)} %get-tuple-element.38.message), custom_call_target="tpu_custom_call" | custom-call | flops 1000000 | bytes 5705728 | tf_op jit(solution)/shard_map/leave/pallas_call | solution.py:379
  29.5 0.5 collective-permute-done.2.other
  30.0 0.9 join.1
  30.9 9.7 %all-to-all-start = ((bf16[32,88,128]{2,1,0:T(8,128)(2,1)}), bf16[32,88,128]{2,1,0:T(8,128)(2,1)S(1)}, u32[]{:S(2)}, u32[]{:S(2)}) async-start(bf16[32,88,128]{2,1,0:T(8,128)(2,1)} %bitcast.14), calls=%async_computation | async-start | bytes 1441792 | tf_op jit(solution)/shard_map/all_to_all | solution.py:418
  40.6 1.1 %copy-done = bf16[2816,128]{1,0:T(8,128)(2,1)S(1)} copy-done((bf16[2816,128]{1,0:T(8,128)(2,1)S(1)}, bf16[2816,128]{1,0:T(8,128)(2,1)}, u32[]{:S(2)}) %copy-start) | copy-done | bytes 720920
  41.8 1.0 copy-done.8
  42.8 1.4 %inputs.1 = (bf16[29,16,128]{2,1,0:T(8,128)(2,1)S(1)}, bf16[29,16,128]{2,1,0:T(8,128)(2,1)S(1)}, bf16[29,64,128]{2,1,0:T(8,128)(2,1)S(1)}) custom-call(bf16[29,64,256]{2,1,0:T(8,128)(2,1)S(1)} %copy-done.2, bf16[448,448]{1,0:T(8,128)(2,1)S(1)} %copy-done.8, bf16[2,384,384]{2,1,0:T(8,128)(2,1)S(1)} %copy-done.5, bf16[2,320,320]{2,1,0:T(8,128)(2,1)S(1)} %copy-done.6, ...), custom_call_target="tpu_custom_call" | custom-call | flops 10000000000 | bytes 3784704 | tf_op jit(solution)/shard_map/inputs/pallas_call | solution.py:379
  44.2 0.0 collective-permute-start.3
  44.2 0.5 collective-permute-start.4
  44.8 3.3 %update.1 = (bf16[49,64,128]{2,1,0:T(8,128)(2,1)}, f32[8,128]{1,0:T(8,128)S(1)}) custom-call(bf16[49,64,128]{2,1,0:T(8,128)(2,1)S(1)} %bitcast.19, bf16[49,29,128]{2,1,0:T(8,128)(2,1)S(1)} %bitcast.23, f32[29,64,256]{2,1,0:T(8,128)S(1)} %copy-done.1, s32[1,128]{1,0:T(1,128)S(1)} %copy-done.23, s32[1,128]{1,0:T(1,128)S(1)} %copy-done.19, ...), custom_call_target="tpu_custom_call" | custom-call | flops 10000000000 | bytes 4350720 | tf_op jit(solution)/shard_map/update/pallas_call | solution.py:379
  48.1 0.7 collective-permute-done.4.back_one
  48.8 3.5 %back.1 = (f32[49,64,128]{2,1,0:T(8,128)}, f32[8,128]{1,0:T(8,128)S(1)}) custom-call(bf16[29,16,128]{2,1,0:T(8,128)(2,1)S(1)} %collective-permute-done.3.back_zero, bf16[29,16,128]{2,1,0:T(8,128)(2,1)S(1)} %collective-permute-done.4.back_one, bf16[29,64,128]{2,1,0:T(8,128)(2,1)S(1)} %get-tuple-element.44.after.inner, bf16[49,29,128]{2,1,0:T(8,128)(2,1)S(1)} %bitcast.24, ...), custom_call_target="tpu_custom_call" | custom-call | flops 10000000000 | bytes 3494656 | tf_op jit(solution)/shard_map/back/pallas_call | solution.py:379
  52.3 6.4 %all-to-all-done.pieces = bf16[32,88,128]{2,1,0:T(8,128)(2,1)S(1)} async-done(((bf16[32,88,128]{2,1,0:T(8,128)(2,1)}), bf16[32,88,128]{2,1,0:T(8,128)(2,1)S(1)}, u32[]{:S(2)}, u32[]{:S(2)}) %all-to-all-start) | async-done | bytes 720928 | tf_op jit(solution)/shard_map/all_to_all | solution.py:418
  58.7 0.1 add_plane.1
  58.8 15.5 %all_to_all.15.pieces = bf16[12,88,128]{2,1,0:T(8,128)(2,1)S(1)} all-to-all(bf16[12,88,128]{2,1,0:T(8,128)(2,1)S(1)} %add_plane.1), channel_id=1, replica_groups=mesh['z'=12,'core'=2,'x'=4,'y'=8] {'z'}, dimensions={0} | all-to-all | bytes 540672 | tf_op jit(solution)/shard_map/all_to_all | solution.py:418
  74.3 0.1 add_z.1
  74.4 27.8 %all_to_all.16 = bf16[32,88,128]{2,1,0:T(8,128)(2,1)S(1)} all-to-all(bf16[32,88,128]{2,1,0:T(8,128)(2,1)S(1)} %add_z.1), channel_id=1, replica_groups=mesh['z'=12,'core'=2,'x'=4,'y'=8] {'x','y'}, dimensions={0} | all-to-all | bytes 1441792 | tf_op jit(solution)/shard_map/all_to_all | solution.py:418
  102.2 7.7 %collective-permute-start.5 = (bf16[32,88,128]{2,1,0:T(8,128)(2,1)S(1)}, bf16[32,88,128]{2,1,0:T(8,128)(2,1)S(1)}, u32[]{:S(2)}, u32[]{:S(2)}) collective-permute-start(bf16[32,88,128]{2,1,0:T(8,128)(2,1)S(1)} %all_to_all.16), channel_id=1, source_target_pairs={{0,32},{32,0},{1,33},{33,1},{2,34},{34,2},{3,35},{35,3},{4,36},{36... | collective-permute-start | bytes 2162696 | tf_op jit(solution)/shard_map/ppermute | solution.py:414
  109.9 1.2 %unpack.2 = (f32[448,448]{1,0:T(8,128)}, f32[2,384,384]{2,1,0:T(8,128)}, f32[2,320,320]{2,1,0:T(8,128)}) custom-call(s32[1]{0:T(128)} %bitcast.2.core.which, bf16[2816,128]{1,0:T(8,128)(2,1)S(1)} %bitcast.16), custom_call_target="tpu_custom_call" | custom-call | flops 10000000 | bytes 3522564 | tf_op jit(solution)/shard_map/unpack/pallas_call | solution.py:379
  111.2 0.6 collective-permute-done.5
  111.7 1.3 %unpack.3 = (f32[448,448]{1,0:T(8,128)}, f32[2,384,384]{2,1,0:T(8,128)}, f32[2,320,320]{2,1,0:T(8,128)}) custom-call(s32[1]{0:T(128)} %bitcast.2.core.which, bf16[2816,128]{1,0:T(8,128)(2,1)S(1)} %bitcast.17, f32[448,448]{1,0:T(8,128)} %get-tuple-element.51.refs_0_, ...), custom_call_target="tpu_custom_call", output_to_operand_aliasing={{0}: (2, {}), {1}: (3, {}), {2}: (4, {})} | custom-call | flops 10000000 | bytes 6324228 | tf_op jit(solution)/shard_map/unpack/pallas_call | solution.py:379
  (45 shorter events, 0.1 us)
Async XLA Ops:
  0.6 7.8 %copy-start.22 = (s32[1,128]{1,0:T(1,128)S(1)}, s32[1,128]{1,0:T(1,128)}, u32[]{:S(2)}) copy-start(s32[1,128]{1,0:T(1,128)} %bins.7) | copy-start | bytes 1540
  0.6 7.8 %copy-start.20 = (s32[1,128]{1,0:T(1,128)S(1)}, s32[1,128]{1,0:T(1,128)}, u32[]{:S(2)}) copy-start(s32[1,128]{1,0:T(1,128)} %sources.3) | copy-start | bytes 1540
  3.1 20.2 %collective-permute-start = (bf16[29,16,128]{2,1,0:T(8,128)(2,1)S(1)}, bf16[29,16,128]{2,1,0:T(8,128)(2,1)S(1)}, u32[]{:S(2)}, u32[]{:S(2)}) collective-permute-start(bf16[29,16,128]{2,1,0:T(8,128)(2,1)S(1)} %get-tuple-element.31), channel_id=1, source_target_pairs={{0,736},{32,64},{64,32},{96,128},{128,96},{160,192},{192,160},{224... | collective-permute-start | bytes 356360 | tf_op jit(solution)/shard_map/ppermute | solution.py:410
  8.5 12.9 %copy-start.4 = (bf16[1,49,64,128]{3,2,1,0:T(8,128)(2,1)S(1)}, bf16[1,49,64,128]{3,2,1,0:T(8,128)(2,1)}, u32[]{:S(2)}) copy-start(bf16[1,49,64,128]{3,2,1,0:T(8,128)(2,1)} %param.16) | copy-start | bytes 2408452
  8.5 12.9 %copy-start.11 = (s32[1,2,32]{2,1,0:T(2,128)S(1)}, s32[1,2,32]{2,1,0:T(2,128)}, u32[]{:S(2)}) copy-start(s32[1,2,32]{2,1,0:T(2,128)} %param.27) | copy-start | bytes 772
  8.5 12.9 %copy-start.13 = (s32[1,2,32]{2,1,0:T(2,128)S(1)}, s32[1,2,32]{2,1,0:T(2,128)}, u32[]{:S(2)}) copy-start(s32[1,2,32]{2,1,0:T(2,128)} %param.28) | copy-start | bytes 772
  8.5 12.9 %copy-start.18 = (s32[1,128]{1,0:T(1,128)S(1)}, s32[1,128]{1,0:T(1,128)}, u32[]{:S(2)}) copy-start(s32[1,128]{1,0:T(1,128)} %targets.3) | copy-start | bytes 1540
  9.3 13.9 %collective-permute-start.1 = (bf16[29,16,128]{2,1,0:T(8,128)(2,1)S(1)}, bf16[29,16,128]{2,1,0:T(8,128)(2,1)S(1)}, u32[]{:S(2)}, u32[]{:S(2)}) collective-permute-start(bf16[29,16,128]{2,1,0:T(8,128)(2,1)S(1)} %get-tuple-element.35.after), channel_id=1, source_target_pairs={{0,32},{32,0},{1,33},{33,1},{2,34},{34,2},{3,35},{35,3},{4,36},{36... | collective-permute-start | bytes 356360 | tf_op jit(solution)/shard_map/ppermute | solution.py:414
  21.4 1.8 %copy-start.5 = (bf16[2,384,384]{2,1,0:T(8,128)(2,1)S(1)}, bf16[2,384,384]{2,1,0:T(8,128)(2,1)}, u32[]{:S(2)}) copy-start(bf16[2,384,384]{2,1,0:T(8,128)(2,1)} %w_one.3) | copy-start | bytes 1769476
  21.4 1.8 %copy-start.6 = (bf16[2,320,320]{2,1,0:T(8,128)(2,1)S(1)}, bf16[2,320,320]{2,1,0:T(8,128)(2,1)}, u32[]{:S(2)}) copy-start(bf16[2,320,320]{2,1,0:T(8,128)(2,1)} %w_two.3) | copy-start | bytes 1228804
  21.5 1.8 %copy-start.7 = (bf16[448,448]{1,0:T(8,128)(2,1)S(1)}, bf16[448,448]{1,0:T(8,128)(2,1)}, u32[]{:S(2)}) copy-start(bf16[448,448]{1,0:T(8,128)(2,1)} %w_zero.3) | copy-start | bytes 1204228
  21.5 1.8 %copy-start.10 = (f32[1,2,32]{2,1,0:T(2,128)S(1)}, f32[1,2,32]{2,1,0:T(2,128)}, u32[]{:S(2)}) copy-start(f32[1,2,32]{2,1,0:T(2,128)} %param.29) | copy-start | bytes 772
  21.5 1.8 %copy-start.17 = (f32[1,128]{1,0:T(1,128)S(1)}, f32[1,128]{1,0:T(1,128)}, u32[]{:S(2)}) copy-start(f32[1,128]{1,0:T(1,128)} %scale.1) | copy-start | bytes 1540
  25.9 4.1 %collective-permute-start.2 = (bf16[2816,128]{1,0:T(8,128)(2,1)S(1)}, bf16[2816,128]{1,0:T(8,128)(2,1)S(1)}, u32[]{:S(2)}, u32[]{:S(2)}) collective-permute-start(bf16[2816,128]{1,0:T(8,128)(2,1)S(1)} %get-tuple-element.42), channel_id=1, source_target_pairs={{0,32},{32,0},{1,33},{33,1},{2,34},{34,2},{3,35},{35,3},{4,36},{36... | collective-permute-start | bytes 2162696 | tf_op jit(solution)/shard_map/ppermute | solution.py:414
  29.5 11.2 %copy-start.2 = (bf16[29,64,256]{2,1,0:T(8,128)(2,1)S(1)}, bf16[29,64,256]{2,1,0:T(8,128)(2,1)}, u32[]{:S(2)}) copy-start(bf16[29,64,256]{2,1,0:T(8,128)(2,1)} %get-tuple-element.40.conv_grad) | copy-start | bytes 2850820
  30.9 27.8 %all-to-all-start = ((bf16[32,88,128]{2,1,0:T(8,128)(2,1)}), bf16[32,88,128]{2,1,0:T(8,128)(2,1)S(1)}, u32[]{:S(2)}, u32[]{:S(2)}) async-start(bf16[32,88,128]{2,1,0:T(8,128)(2,1)} %bitcast.14), calls=%async_computation | async-start | bytes 1441792 | tf_op jit(solution)/shard_map/all_to_all | solution.py:418
  40.6 1.1 %copy-start = (bf16[2816,128]{1,0:T(8,128)(2,1)S(1)}, bf16[2816,128]{1,0:T(8,128)(2,1)}, u32[]{:S(2)}) copy-start(bf16[2816,128]{1,0:T(8,128)(2,1)} %join.1) | copy-start | bytes 2162692
  41.8 1.0 copy-start.8
  42.8 2.0 %copy-start.1 = (f32[29,64,256]{2,1,0:T(8,128)S(1)}, f32[29,64,256]{2,1,0:T(8,128)}, u32[]{:S(2)}) copy-start(f32[29,64,256]{2,1,0:T(8,128)} %get-tuple-element.39.message) | copy-start | bytes 5701636
  42.8 2.0 %copy-start.3 = (bf16[1,49,64,128]{3,2,1,0:T(8,128)(2,1)S(1)}, bf16[1,49,64,128]{3,2,1,0:T(8,128)(2,1)}, u32[]{:S(2)}) copy-start(bf16[1,49,64,128]{3,2,1,0:T(8,128)(2,1)} %param.15) | copy-start | bytes 2408452
  42.8 2.0 %copy-start.9 = (bf16[128,29,49]{0,1,2:T(8,128)(2,1)S(1)}, bf16[128,29,49]{0,1,2:T(8,128)(2,1)}, u32[]{:S(2)}) copy-start(bf16[128,29,49]{0,1,2:T(8,128)(2,1)} %param.17) | copy-start | bytes 1091332
  42.8 2.0 %copy-start.12 = (s32[1,2,32]{2,1,0:T(2,128)S(1)}, s32[1,2,32]{2,1,0:T(2,128)}, u32[]{:S(2)}) copy-start(s32[1,2,32]{2,1,0:T(2,128)} %param.27) | copy-start | bytes 772
  42.8 2.0 %copy-start.14 = (s32[1,2,32]{2,1,0:T(2,128)S(1)}, s32[1,2,32]{2,1,0:T(2,128)}, u32[]{:S(2)}) copy-start(s32[1,2,32]{2,1,0:T(2,128)} %param.28) | copy-start | bytes 772
  42.8 2.0 %copy-start.19 = (s32[1,128]{1,0:T(1,128)S(1)}, s32[1,128]{1,0:T(1,128)}, u32[]{:S(2)}) copy-start(s32[1,128]{1,0:T(1,128)} %targets.3) | copy-start | bytes 1540
  42.8 2.0 %copy-start.23 = (s32[1,128]{1,0:T(1,128)S(1)}, s32[1,128]{1,0:T(1,128)}, u32[]{:S(2)}) copy-start(s32[1,128]{1,0:T(1,128)} %bins.7) | copy-start | bytes 1540
  44.2 3.9 %collective-permute-start.3 = (bf16[29,16,128]{2,1,0:T(8,128)(2,1)S(1)}, bf16[29,16,128]{2,1,0:T(8,128)(2,1)S(1)}, u32[]{:S(2)}, u32[]{:S(2)}) collective-permute-start(bf16[29,16,128]{2,1,0:T(8,128)(2,1)S(1)} %get-tuple-element.46), channel_id=1, source_target_pairs={{0,32},{32,64},{64,96},{96,128},{128,160},{160,192},{192,224},{224... | collective-permute-start | bytes 356360 | tf_op jit(solution)/shard_map/ppermute | solution.py:402
  44.2 4.6 %collective-permute-start.4 = (bf16[29,16,128]{2,1,0:T(8,128)(2,1)S(1)}, bf16[29,16,128]{2,1,0:T(8,128)(2,1)S(1)}, u32[]{:S(2)}, u32[]{:S(2)}) collective-permute-start(bf16[29,16,128]{2,1,0:T(8,128)(2,1)S(1)} %get-tuple-element.47), channel_id=1, source_target_pairs={{0,736},{32,0},{64,32},{96,64},{128,96},{160,128},{192,160},{224,1... | collective-permute-start | bytes 356360 | tf_op jit(solution)/shard_map/ppermute | solution.py:402
  44.8 4.0 %copy-start.15 = (s32[1,2,32]{2,1,0:T(2,128)S(1)}, s32[1,2,32]{2,1,0:T(2,128)}, u32[]{:S(2)}) copy-start(s32[1,2,32]{2,1,0:T(2,128)} %param.25) | copy-start | bytes 772
  44.8 4.0 %copy-start.16 = (s32[1,2,32]{2,1,0:T(2,128)S(1)}, s32[1,2,32]{2,1,0:T(2,128)}, u32[]{:S(2)}) copy-start(s32[1,2,32]{2,1,0:T(2,128)} %param.26) | copy-start | bytes 772
  44.8 4.0 %copy-start.21 = (s32[1,128]{1,0:T(1,128)S(1)}, s32[1,128]{1,0:T(1,128)}, u32[]{:S(2)}) copy-start(s32[1,128]{1,0:T(1,128)} %sources.3) | copy-start | bytes 1540
  102.2 9.5 %collective-permute-start.5 = (bf16[32,88,128]{2,1,0:T(8,128)(2,1)S(1)}, bf16[32,88,128]{2,1,0:T(8,128)(2,1)S(1)}, u32[]{:S(2)}, u32[]{:S(2)}) collective-permute-start(bf16[32,88,128]{2,1,0:T(8,128)(2,1)S(1)} %all_to_all.16), channel_id=1, source_target_pairs={{0,32},{32,0},{1,33},{33,1},{2,34},{34,2},{3,35},{35,3},{4,36},{36... | collective-permute-start | bytes 2162696 | tf_op jit(solution)/shard_map/ppermute | solution.py:414

commit v6 on v4

--- a/solution.py
+++ b/solution.py
@@ -107,7 +107,7 @@
 
 
 def rim_kernel(
-    core, node_far, wigner_far, atoms_far, bins_far, outer, inner, node, wigner,
+    core, node_far, wigner_far, atoms_far, bins_far, to_lower, to_upper, node, wigner,
     frames, padded, gathered, rotated, atoms, bins, sems,
 ):
     pairs = [(wigner_far, wigner), (bins_far, bins), (atoms_far, atoms), (node_far, node)]
@@ -128,8 +128,8 @@
     )
     gathered[...] = dot(left, table).reshape(COEF, SUB, wide)
     rotate_into(frames, gathered, rotated, SUB)
-    outer[...] = rotated[:, :, pl.ds(pl.multiple_of(core[0] * LANES, LANES), LANES)]
-    inner[...] = rotated[:, :, pl.ds(pl.multiple_of((1 - core[0]) * LANES, LANES), LANES)]
+    to_lower[...] = rotated[:, :, 0:LANES]
+    to_upper[...] = rotated[:, :, LANES:wide]
 
 
 def pre_kernel(
@@ -190,14 +190,12 @@
 
 
 def conv_kernel(
-    core, outer, inner, inner_rotated, message_grad, w_zero, w_one, w_two, scale, halo_scale,
+    core, from_lower, from_upper, inner_rotated, message_grad, w_zero, w_one, w_two, scale, halo_scale,
     conv_grad, message, keep, send,
-    rotated, conv, packed, halo,
+    rotated, conv, packed,
 ):
     rotated[:, :, 0:LANES] = inner_rotated[...]
-    halo[core[0]] = flat(outer[...])
-    halo[1 - core[0]] = flat(inner[...])
-    left = jnp.concatenate([halo[0], halo[1]], axis=1)
+    left = jnp.concatenate([flat(from_lower[...]), flat(from_upper[...])], axis=1)
     spread = dot(left, spread_table()).astype(bf16)
     for g in range(GROUPS):
         rotated[:, g * SUB : (g + 1) * SUB, LANES:WIDE] = spread[:, g * LANES : (g + 1) * LANES].reshape(
@@ -401,14 +399,6 @@
     return lax.ppermute(value, axis, [(source, (source + steps) % count) for source in range(count)])
 
 
-def across_chips(value):
-    chips = lax.axis_size("z")
-    pairs = []
-    for chip in range(chips):
-        pairs += [(2 * chip, (2 * chip - 1) % (2 * chips)), (2 * chip + 1, (2 * chip + 2) % (2 * chips))]
-    return lax.ppermute(value, ("z", "core"), pairs)
-
-
 def swap_cores(value):
     return lax.ppermute(value, "core", [(0, 1), (1, 0)])
 
@@ -439,14 +429,15 @@
     mark = arr((8, LANES), f32)
 
     core = lax.axis_index("core").reshape(1)
-    outer, inner, near_node, near_table = call(
+    to_lower, to_upper, near_node, near_table = call(
         rim_kernel, [packed_shape] * 2 + [arr(node.shape, bf16), arr(table.shape, bf16)],
         [frames2, padded, scr((COEF, SUB, WIDE), f32), scr((TRUNC, SUB, WIDE), bf16),
          scr(out_atoms.shape, jnp.int32),
          scr(out_bins.shape, jnp.int32), pltpu.SemaphoreType.DMA((4,))],
         [core, node, table, out_atoms, out_bins], 10**9, "rim", scalars=1, hbm=4,
     )
-    outer, inner = across_chips(outer), swap_cores(inner)
+    from_lower = from_behind(to_upper, graph, 1)
+    from_upper = from_behind(to_lower, graph, -1)
     inner_rotated, message_grad = call(
         pre_kernel, [arr((TRUNC, CH, LANES), bf16), edges32],
         [frames2, padded, scr((COEF, CH, WIDE), f32)],
@@ -455,9 +446,8 @@
     half = arr((PACKED // 2, LANES), bf16)
     conv_grad, message, keep, send = call(
         conv_kernel, [edges16, edges32, half, half],
-        [scr((TRUNC, CH, WIDE), bf16), scr((TRUNC, CH, WIDE), f32), scr((2, PACKED // 2, LANES), bf16),
-         scr((2, TRUNC * SUB, LANES), bf16)],
-        [core, outer, inner, inner_rotated, message_grad] + weights + [edge_scale, in_scale],
+        [scr((TRUNC, CH, WIDE), bf16), scr((TRUNC, CH, WIDE), f32), scr((2, PACKED // 2, LANES), bf16)],
+        [core, from_lower, from_upper, inner_rotated, message_grad] + weights + [edge_scale, in_scale],
         10**10, "conv", scalars=1,
     )
 

time: 114 us -> 113 us (level)
  blocking collectives: 43.3 us -> 46.8 us
  starting transfers between devices: 37.3 us -> 34 us
    ppermute x2 -> x4, starting transfers between devices: 0.52 us -> 11.3 us  [from_behind(): lax.ppermute(value, axis, [(source, (source + steps) % count) for source...]
    ppermute x3 -> x2, starting transfers between devices: 21.7 us -> 13.1 us  [swap_cores(): return lax.ppermute(value, 'core', [(0, 1), (1, 0)])]
    ppermute x1 -> x0, starting transfers between devices: 5.39 us -> none  [across_chips(): return lax.ppermute(value, ('z', 'core'), pairs)]
    all_to_all x2, blocking collectives: 43.3 us -> 46.8 us  [to_all(): return lax.all_to_all(copies, axes, 0, 0)]
where the time goes in v6:
time: 113 us; the launch traced here: 112 us
  blocking collectives  46.8 us (41%)
  starting transfers between devices  34 us (30%)
  Pallas kernels  20.5 us (18%)
  waiting for transfers between devices  7.32 us (6%)
  local copies, waits for them, and re-layouts  2.29 us (2%)
    all_to_all x2, blocking collectives, to_all(): return lax.all_to_all(copies, axes, 0, 0)  46.8 us
    pallas_call x12, Pallas kernels, call(): pl.pallas_call(kernel, out_shape=tuple(outs), in_specs=[scalar] * scalars...  20.5 us
    ppermute x2, starting transfers between devices, swap_cores(): return lax.ppermute(value, 'core', [(0, 1), (1, 0)])  13.1 us
    ppermute x4, starting transfers between devices, from_behind(): lax.ppermute(value, axis, [(source, (source + steps) % count) for source...  11.3 us
    all_to_all x1, starting transfers between devices, to_all(): return lax.all_to_all(copies, axes, 0, 0)  9.69 us
    all_to_all x1, waiting for transfers between devices, to_all(): return lax.all_to_all(copies, axes, 0, 0)  6.1 us
    unnamed x48, local copies, waits for them, and re-layouts  2.29 us
  transfers between devices with their start and end apart: 7, of which 4 were waited for; matrix products, arithmetic and copies ran while one was open for 0% of the time, Pallas kernels for 12%

profile of v6, /device:TPU:1, one launch (start us, length us, event | category | flops | bytes accessed | tf_op | source)
XLA Modules:
  0.0 112.0 jit_solution(16209954590525528779)
XLA Ops:
  0.6 0.0 copy-start.22
  0.7 0.0 copy-start.13
  0.7 0.0 copy-start.11
  0.7 2.5 %rim.1 = (bf16[29,16,128]{2,1,0:T(8,128)(2,1)S(1)}, bf16[29,16,128]{2,1,0:T(8,128)(2,1)S(1)}, bf16[49,64,128]{2,1,0:T(8,128)(2,1)S(1)}, bf16[49,29,128]{2,1,0:T(8,128)(2,1)S(1)}) custom-call(s32[1]{0:T(128)} %bitcast.2.core.which, bf16[49,64,128]{2,1,0:T(8,128)(2,1)} %bitcast.18, bf16[49,29,128]{2,1,0:T(8,128)(2,1)} %bitcast.22, s32[2,32]{1,0:T(2,128)} %bitcast.30, ...), custom_call_target="tpu_custom_call" | custom-call | flops 1000000000 | bytes 2571268 | tf_op jit(solution)/shard_map/rim/pallas_call | solution.py:376
  3.2 3.5 %collective-permute-start = (bf16[29,16,128]{2,1,0:T(8,128)(2,1)S(1)}, bf16[29,16,128]{2,1,0:T(8,128)(2,1)S(1)}, u32[]{:S(2)}, u32[]{:S(2)}) collective-permute-start(bf16[29,16,128]{2,1,0:T(8,128)(2,1)S(1)} %get-tuple-element.31), channel_id=1, source_target_pairs={{0,32},{32,64},{64,96},{96,128},{128,160},{160,192},{192,224},{224... | collective-permute-start | bytes 356360 | tf_op jit(solution)/shard_map/ppermute | solution.py:399
  6.7 7.1 %collective-permute-start.1 = (bf16[29,16,128]{2,1,0:T(8,128)(2,1)S(1)}, bf16[29,16,128]{2,1,0:T(8,128)(2,1)S(1)}, u32[]{:S(2)}, u32[]{:S(2)}) collective-permute-start(bf16[29,16,128]{2,1,0:T(8,128)(2,1)S(1)} %get-tuple-element.32), channel_id=1, source_target_pairs={{0,736},{32,0},{64,32},{96,64},{128,96},{160,128},{192,160},{224,1... | collective-permute-start | bytes 356360 | tf_op jit(solution)/shard_map/ppermute | solution.py:399
  13.8 0.0 copy-start.5
  13.8 0.0 copy-start.10
  13.8 2.1 %pre.1 = (bf16[29,64,128]{2,1,0:T(8,128)(2,1)S(1)}, f32[29,64,256]{2,1,0:T(8,128)S(1)}) custom-call(bf16[49,64,128]{2,1,0:T(8,128)(2,1)S(1)} %get-tuple-element.33.node, bf16[49,64,128]{2,1,0:T(8,128)(2,1)S(1)} %bitcast.20, bf16[49,29,128]{2,1,0:T(8,128)(2,1)S(1)} %get-tuple-element.34.wigner, s32[1,128]{1,0:T(1,128)S(1)} %copy-done.20, ...), custom_call_target="tpu_custom_call" | custom-call | flops 10000000000 | bytes 4347136 | tf_op jit(solution)/shard_map/pre/pallas_call | solution.py:376
  16.0 2.6 %conv.1 = (bf16[29,64,256]{2,1,0:T(8,128)(2,1)S(1)}, f32[29,64,256]{2,1,0:T(8,128)S(1)}, bf16[2816,128]{1,0:T(8,128)(2,1)S(1)}, bf16[2816,128]{1,0:T(8,128)(2,1)S(1)}) custom-call(s32[1]{0:T(128)} %bitcast.2.core.which, bf16[29,16,128]{2,1,0:T(8,128)(2,1)S(1)} %collective-permute-done.from_lower, bf16[29,16,128]{2,1,0:T(8,128)(2,1)S(1)} %collective-permute-done.1.from_upper, ...), custom_call_target="tpu_custom_call" | custom-call | flops 10000000000 | bytes 8307460 | tf_op jit(solution)/shard_map/conv/pallas_call | solution.py:376
  18.6 5.3 %collective-permute-start.2 = (bf16[2816,128]{1,0:T(8,128)(2,1)S(1)}, bf16[2816,128]{1,0:T(8,128)(2,1)S(1)}, u32[]{:S(2)}, u32[]{:S(2)}) collective-permute-start(bf16[2816,128]{1,0:T(8,128)(2,1)S(1)} %get-tuple-element.42), channel_id=1, source_target_pairs={{0,32},{32,0},{1,33},{33,1},{2,34},{34,2},{3,35},{35,3},{4,36},{36... | collective-permute-start | bytes 2162696 | tf_op jit(solution)/shard_map/ppermute | solution.py:403
  23.9 1.6 %leave.1 = (bf16[29,64,256]{2,1,0:T(8,128)(2,1)}, f32[29,64,256]{2,1,0:T(8,128)}, f32[8,128]{1,0:T(8,128)S(1)}) custom-call(bf16[29,64,256]{2,1,0:T(8,128)(2,1)S(1)} %get-tuple-element.37.conv_grad, f32[29,64,256]{2,1,0:T(8,128)S(1)} %get-tuple-element.38.message), custom_call_target="tpu_custom_call" | custom-call | flops 1000000 | bytes 5705728 | tf_op jit(solution)/shard_map/leave/pallas_call | solution.py:376
  25.5 0.2 collective-permute-done.2.other
  25.7 0.9 join.1
  26.6 9.7 %all-to-all-start = ((bf16[32,88,128]{2,1,0:T(8,128)(2,1)}), bf16[32,88,128]{2,1,0:T(8,128)(2,1)S(1)}, u32[]{:S(2)}, u32[]{:S(2)}) async-start(bf16[32,88,128]{2,1,0:T(8,128)(2,1)} %bitcast.14), calls=%async_computation | async-start | bytes 1441792 | tf_op jit(solution)/shard_map/all_to_all | solution.py:407
  36.3 1.1 %copy-done = bf16[2816,128]{1,0:T(8,128)(2,1)S(1)} copy-done((bf16[2816,128]{1,0:T(8,128)(2,1)S(1)}, bf16[2816,128]{1,0:T(8,128)(2,1)}, u32[]{:S(2)}) %copy-start) | copy-done | bytes 720920
  37.5 1.0 copy-done.8
  38.6 1.4 %inputs.1 = (bf16[29,16,128]{2,1,0:T(8,128)(2,1)S(1)}, bf16[29,16,128]{2,1,0:T(8,128)(2,1)S(1)}, bf16[29,64,128]{2,1,0:T(8,128)(2,1)S(1)}) custom-call(bf16[29,64,256]{2,1,0:T(8,128)(2,1)S(1)} %copy-done.2, bf16[448,448]{1,0:T(8,128)(2,1)S(1)} %copy-done.8, bf16[2,384,384]{2,1,0:T(8,128)(2,1)S(1)} %copy-done.5, bf16[2,320,320]{2,1,0:T(8,128)(2,1)S(1)} %copy-done.6, ...), custom_call_target="tpu_custom_call" | custom-call | flops 10000000000 | bytes 3784704 | tf_op jit(solution)/shard_map/inputs/pallas_call | solution.py:376
  39.9 0.0 collective-permute-start.3
  40.0 0.7 collective-permute-start.4
  40.7 3.3 %update.1 = (bf16[49,64,128]{2,1,0:T(8,128)(2,1)}, f32[8,128]{1,0:T(8,128)S(1)}) custom-call(bf16[49,64,128]{2,1,0:T(8,128)(2,1)S(1)} %bitcast.19, bf16[49,29,128]{2,1,0:T(8,128)(2,1)S(1)} %bitcast.23, f32[29,64,256]{2,1,0:T(8,128)S(1)} %copy-done.1, s32[1,128]{1,0:T(1,128)S(1)} %copy-done.23, s32[1,128]{1,0:T(1,128)S(1)} %copy-done.19, ...), custom_call_target="tpu_custom_call" | custom-call | flops 10000000000 | bytes 4350720 | tf_op jit(solution)/shard_map/update/pallas_call | solution.py:376
  44.0 0.5 collective-permute-done.4.back_one
  44.5 3.5 %back.1 = (f32[49,64,128]{2,1,0:T(8,128)}, f32[8,128]{1,0:T(8,128)S(1)}) custom-call(bf16[29,16,128]{2,1,0:T(8,128)(2,1)S(1)} %collective-permute-done.3.back_zero, bf16[29,16,128]{2,1,0:T(8,128)(2,1)S(1)} %collective-permute-done.4.back_one, bf16[29,64,128]{2,1,0:T(8,128)(2,1)S(1)} %get-tuple-element.44.after.inner, bf16[49,29,128]{2,1,0:T(8,128)(2,1)S(1)} %bitcast.24, ...), custom_call_target="tpu_custom_call" | custom-call | flops 10000000000 | bytes 3494656 | tf_op jit(solution)/shard_map/back/pallas_call | solution.py:376
  48.0 6.1 %all-to-all-done.pieces = bf16[32,88,128]{2,1,0:T(8,128)(2,1)S(1)} async-done(((bf16[32,88,128]{2,1,0:T(8,128)(2,1)}), bf16[32,88,128]{2,1,0:T(8,128)(2,1)S(1)}, u32[]{:S(2)}, u32[]{:S(2)}) %all-to-all-start) | async-done | bytes 720928 | tf_op jit(solution)/shard_map/all_to_all | solution.py:407
  54.1 0.1 add_plane.1
  54.2 19.3 %all_to_all.15.pieces = bf16[12,88,128]{2,1,0:T(8,128)(2,1)S(1)} all-to-all(bf16[12,88,128]{2,1,0:T(8,128)(2,1)S(1)} %add_plane.1), channel_id=1, replica_groups=mesh['z'=12,'core'=2,'x'=4,'y'=8] {'z'}, dimensions={0} | all-to-all | bytes 540672 | tf_op jit(solution)/shard_map/all_to_all | solution.py:407
  73.5 0.1 add_z.1
  73.6 27.5 %all_to_all.16 = bf16[32,88,128]{2,1,0:T(8,128)(2,1)S(1)} all-to-all(bf16[32,88,128]{2,1,0:T(8,128)(2,1)S(1)} %add_z.1), channel_id=1, replica_groups=mesh['z'=12,'core'=2,'x'=4,'y'=8] {'x','y'}, dimensions={0} | all-to-all | bytes 1441792 | tf_op jit(solution)/shard_map/all_to_all | solution.py:407
  101.1 7.8 %collective-permute-start.5 = (bf16[32,88,128]{2,1,0:T(8,128)(2,1)S(1)}, bf16[32,88,128]{2,1,0:T(8,128)(2,1)S(1)}, u32[]{:S(2)}, u32[]{:S(2)}) collective-permute-start(bf16[32,88,128]{2,1,0:T(8,128)(2,1)S(1)} %all_to_all.16), channel_id=1, source_target_pairs={{0,32},{32,0},{1,33},{33,1},{2,34},{34,2},{3,35},{35,3},{4,36},{36... | collective-permute-start | bytes 2162696 | tf_op jit(solution)/shard_map/ppermute | solution.py:403
  108.9 1.2 %unpack.2 = (f32[448,448]{1,0:T(8,128)}, f32[2,384,384]{2,1,0:T(8,128)}, f32[2,320,320]{2,1,0:T(8,128)}) custom-call(s32[1]{0:T(128)} %bitcast.2.core.which, bf16[2816,128]{1,0:T(8,128)(2,1)S(1)} %bitcast.16), custom_call_target="tpu_custom_call" | custom-call | flops 10000000 | bytes 3522564 | tf_op jit(solution)/shard_map/unpack/pallas_call | solution.py:376
  110.1 0.6 collective-permute-done.5
  110.7 1.3 %unpack.3 = (f32[448,448]{1,0:T(8,128)}, f32[2,384,384]{2,1,0:T(8,128)}, f32[2,320,320]{2,1,0:T(8,128)}) custom-call(s32[1]{0:T(128)} %bitcast.2.core.which, bf16[2816,128]{1,0:T(8,128)(2,1)S(1)} %bitcast.17, f32[448,448]{1,0:T(8,128)} %get-tuple-element.51.refs_0_, ...), custom_call_target="tpu_custom_call", output_to_operand_aliasing={{0}: (2, {}), {1}: (3, {}), {2}: (4, {})} | custom-call | flops 10000000 | bytes 6324228 | tf_op jit(solution)/shard_map/unpack/pallas_call | solution.py:376
  (44 shorter events, 0.1 us)
Async XLA Ops:
  0.6 13.1 %copy-start.22 = (s32[1,128]{1,0:T(1,128)S(1)}, s32[1,128]{1,0:T(1,128)}, u32[]{:S(2)}) copy-start(s32[1,128]{1,0:T(1,128)} %bins.5) | copy-start | bytes 1540
  0.6 13.1 %copy-start.18 = (s32[1,128]{1,0:T(1,128)S(1)}, s32[1,128]{1,0:T(1,128)}, u32[]{:S(2)}) copy-start(s32[1,128]{1,0:T(1,128)} %targets.3) | copy-start | bytes 1540
  0.7 13.1 %copy-start.20 = (s32[1,128]{1,0:T(1,128)S(1)}, s32[1,128]{1,0:T(1,128)}, u32[]{:S(2)}) copy-start(s32[1,128]{1,0:T(1,128)} %sources.3) | copy-start | bytes 1540
  0.7 13.1 %copy-start.13 = (s32[1,2,32]{2,1,0:T(2,128)S(1)}, s32[1,2,32]{2,1,0:T(2,128)}, u32[]{:S(2)}) copy-start(s32[1,2,32]{2,1,0:T(2,128)} %param.28) | copy-start | bytes 772
  0.7 13.1 %copy-start.11 = (s32[1,2,32]{2,1,0:T(2,128)S(1)}, s32[1,2,32]{2,1,0:T(2,128)}, u32[]{:S(2)}) copy-start(s32[1,2,32]{2,1,0:T(2,128)} %param.27) | copy-start | bytes 772
  0.7 13.1 %copy-start.4 = (bf16[1,49,64,128]{3,2,1,0:T(8,128)(2,1)S(1)}, bf16[1,49,64,128]{3,2,1,0:T(8,128)(2,1)}, u32[]{:S(2)}) copy-start(bf16[1,49,64,128]{3,2,1,0:T(8,128)(2,1)} %param.16) | copy-start | bytes 2408452
  3.2 12.7 %collective-permute-start = (bf16[29,16,128]{2,1,0:T(8,128)(2,1)S(1)}, bf16[29,16,128]{2,1,0:T(8,128)(2,1)S(1)}, u32[]{:S(2)}, u32[]{:S(2)}) collective-permute-start(bf16[29,16,128]{2,1,0:T(8,128)(2,1)S(1)} %get-tuple-element.31), channel_id=1, source_target_pairs={{0,32},{32,64},{64,96},{96,128},{128,160},{160,192},{192,224},{224... | collective-permute-start | bytes 356360 | tf_op jit(solution)/shard_map/ppermute | solution.py:399
  6.7 9.2 %collective-permute-start.1 = (bf16[29,16,128]{2,1,0:T(8,128)(2,1)S(1)}, bf16[29,16,128]{2,1,0:T(8,128)(2,1)S(1)}, u32[]{:S(2)}, u32[]{:S(2)}) collective-permute-start(bf16[29,16,128]{2,1,0:T(8,128)(2,1)S(1)} %get-tuple-element.32), channel_id=1, source_target_pairs={{0,736},{32,0},{64,32},{96,64},{128,96},{160,128},{192,160},{224,1... | collective-permute-start | bytes 356360 | tf_op jit(solution)/shard_map/ppermute | solution.py:399
  13.8 2.2 %copy-start.5 = (bf16[2,384,384]{2,1,0:T(8,128)(2,1)S(1)}, bf16[2,384,384]{2,1,0:T(8,128)(2,1)}, u32[]{:S(2)}) copy-start(bf16[2,384,384]{2,1,0:T(8,128)(2,1)} %w_one.3) | copy-start | bytes 1769476
  13.8 2.2 %copy-start.6 = (bf16[2,320,320]{2,1,0:T(8,128)(2,1)S(1)}, bf16[2,320,320]{2,1,0:T(8,128)(2,1)}, u32[]{:S(2)}) copy-start(bf16[2,320,320]{2,1,0:T(8,128)(2,1)} %w_two.3) | copy-start | bytes 1228804
  13.8 2.2 %copy-start.7 = (bf16[448,448]{1,0:T(8,128)(2,1)S(1)}, bf16[448,448]{1,0:T(8,128)(2,1)}, u32[]{:S(2)}) copy-start(bf16[448,448]{1,0:T(8,128)(2,1)} %w_zero.3) | copy-start | bytes 1204228
  13.8 2.1 %copy-start.10 = (f32[1,2,32]{2,1,0:T(2,128)S(1)}, f32[1,2,32]{2,1,0:T(2,128)}, u32[]{:S(2)}) copy-start(f32[1,2,32]{2,1,0:T(2,128)} %param.29) | copy-start | bytes 772
  13.8 2.1 %copy-start.17 = (f32[1,128]{1,0:T(1,128)S(1)}, f32[1,128]{1,0:T(1,128)}, u32[]{:S(2)}) copy-start(f32[1,128]{1,0:T(1,128)} %scale.1) | copy-start | bytes 1540
  18.6 7.1 %collective-permute-start.2 = (bf16[2816,128]{1,0:T(8,128)(2,1)S(1)}, bf16[2816,128]{1,0:T(8,128)(2,1)S(1)}, u32[]{:S(2)}, u32[]{:S(2)}) collective-permute-start(bf16[2816,128]{1,0:T(8,128)(2,1)S(1)} %get-tuple-element.42), channel_id=1, source_target_pairs={{0,32},{32,0},{1,33},{33,1},{2,34},{34,2},{3,35},{35,3},{4,36},{36... | collective-permute-start | bytes 2162696 | tf_op jit(solution)/shard_map/ppermute | solution.py:403
  25.5 10.8 %copy-start.2 = (bf16[29,64,256]{2,1,0:T(8,128)(2,1)S(1)}, bf16[29,64,256]{2,1,0:T(8,128)(2,1)}, u32[]{:S(2)}) copy-start(bf16[29,64,256]{2,1,0:T(8,128)(2,1)} %get-tuple-element.40.conv_grad) | copy-start | bytes 2850820
  26.6 27.5 %all-to-all-start = ((bf16[32,88,128]{2,1,0:T(8,128)(2,1)}), bf16[32,88,128]{2,1,0:T(8,128)(2,1)S(1)}, u32[]{:S(2)}, u32[]{:S(2)}) async-start(bf16[32,88,128]{2,1,0:T(8,128)(2,1)} %bitcast.14), calls=%async_computation | async-start | bytes 1441792 | tf_op jit(solution)/shard_map/all_to_all | solution.py:407
  36.3 1.1 %copy-start = (bf16[2816,128]{1,0:T(8,128)(2,1)S(1)}, bf16[2816,128]{1,0:T(8,128)(2,1)}, u32[]{:S(2)}) copy-start(bf16[2816,128]{1,0:T(8,128)(2,1)} %join.1) | copy-start | bytes 2162692
  37.5 1.0 copy-start.8
  38.5 2.1 %copy-start.1 = (f32[29,64,256]{2,1,0:T(8,128)S(1)}, f32[29,64,256]{2,1,0:T(8,128)}, u32[]{:S(2)}) copy-start(f32[29,64,256]{2,1,0:T(8,128)} %get-tuple-element.39.message) | copy-start | bytes 5701636
  38.5 2.1 %copy-start.3 = (bf16[1,49,64,128]{3,2,1,0:T(8,128)(2,1)S(1)}, bf16[1,49,64,128]{3,2,1,0:T(8,128)(2,1)}, u32[]{:S(2)}) copy-start(bf16[1,49,64,128]{3,2,1,0:T(8,128)(2,1)} %param.15) | copy-start | bytes 2408452
  38.5 2.1 %copy-start.9 = (bf16[128,29,49]{0,1,2:T(8,128)(2,1)S(1)}, bf16[128,29,49]{0,1,2:T(8,128)(2,1)}, u32[]{:S(2)}) copy-start(bf16[128,29,49]{0,1,2:T(8,128)(2,1)} %param.17) | copy-start | bytes 1091332
  38.5 2.1 %copy-start.12 = (s32[1,2,32]{2,1,0:T(2,128)S(1)}, s32[1,2,32]{2,1,0:T(2,128)}, u32[]{:S(2)}) copy-start(s32[1,2,32]{2,1,0:T(2,128)} %param.27) | copy-start | bytes 772
  38.5 2.1 %copy-start.14 = (s32[1,2,32]{2,1,0:T(2,128)S(1)}, s32[1,2,32]{2,1,0:T(2,128)}, u32[]{:S(2)}) copy-start(s32[1,2,32]{2,1,0:T(2,128)} %param.28) | copy-start | bytes 772
  38.5 2.1 %copy-start.19 = (s32[1,128]{1,0:T(1,128)S(1)}, s32[1,128]{1,0:T(1,128)}, u32[]{:S(2)}) copy-start(s32[1,128]{1,0:T(1,128)} %targets.3) | copy-start | bytes 1540
  38.5 2.1 %copy-start.23 = (s32[1,128]{1,0:T(1,128)S(1)}, s32[1,128]{1,0:T(1,128)}, u32[]{:S(2)}) copy-start(s32[1,128]{1,0:T(1,128)} %bins.5) | copy-start | bytes 1540
  39.9 4.1 %collective-permute-start.3 = (bf16[29,16,128]{2,1,0:T(8,128)(2,1)S(1)}, bf16[29,16,128]{2,1,0:T(8,128)(2,1)S(1)}, u32[]{:S(2)}, u32[]{:S(2)}) collective-permute-start(bf16[29,16,128]{2,1,0:T(8,128)(2,1)S(1)} %get-tuple-element.46), channel_id=1, source_target_pairs={{0,32},{32,64},{64,96},{96,128},{128,160},{160,192},{192,224},{224... | collective-permute-start | bytes 356360 | tf_op jit(solution)/shard_map/ppermute | solution.py:399
  40.0 4.6 %collective-permute-start.4 = (bf16[29,16,128]{2,1,0:T(8,128)(2,1)S(1)}, bf16[29,16,128]{2,1,0:T(8,128)(2,1)S(1)}, u32[]{:S(2)}, u32[]{:S(2)}) collective-permute-start(bf16[29,16,128]{2,1,0:T(8,128)(2,1)S(1)} %get-tuple-element.47), channel_id=1, source_target_pairs={{0,736},{32,0},{64,32},{96,64},{128,96},{160,128},{192,160},{224,1... | collective-permute-start | bytes 356360 | tf_op jit(solution)/shard_map/ppermute | solution.py:399
  40.7 3.9 %copy-start.15 = (s32[1,2,32]{2,1,0:T(2,128)S(1)}, s32[1,2,32]{2,1,0:T(2,128)}, u32[]{:S(2)}) copy-start(s32[1,2,32]{2,1,0:T(2,128)} %param.25) | copy-start | bytes 772
  40.7 3.9 %copy-start.16 = (s32[1,2,32]{2,1,0:T(2,128)S(1)}, s32[1,2,32]{2,1,0:T(2,128)}, u32[]{:S(2)}) copy-start(s32[1,2,32]{2,1,0:T(2,128)} %param.26) | copy-start | bytes 772
  40.7 3.8 %copy-start.21 = (s32[1,128]{1,0:T(1,128)S(1)}, s32[1,128]{1,0:T(1,128)}, u32[]{:S(2)}) copy-start(s32[1,128]{1,0:T(1,128)} %sources.3) | copy-start | bytes 1540
  101.1 9.6 %collective-permute-start.5 = (bf16[32,88,128]{2,1,0:T(8,128)(2,1)S(1)}, bf16[32,88,128]{2,1,0:T(8,128)(2,1)S(1)}, u32[]{:S(2)}, u32[]{:S(2)}) collective-permute-start(bf16[32,88,128]{2,1,0:T(8,128)(2,1)S(1)} %all_to_all.16), channel_id=1, source_target_pairs={{0,32},{32,0},{1,33},{33,1},{2,34},{34,2},{3,35},{35,3},{4,36},{36... | collective-permute-start | bytes 2162696 | tf_op jit(solution)/shard_map/ppermute | solution.py:403
